TPU v7x, 32 devices: a whole 2x2x4 slice. The times are simulated.
32 devices in a mesh: ens: 2 (over y), dom: 4 (over z), feat: 2 (over x), sub: 2 (over core).
Axes of the slice: x: 2, y: 2, z: 4, core: 2. Of those that a mesh axis runs over, the one named last changes fastest.
Arguments:
- grid_state: bfloat16 [512, 49152], P(None, ('ens', 'dom', 'sub', 'feat')), parts along dimension 1, may hold values from -6 to 6
- mesh_state: bfloat16 [512, 8192], P('feat', ('ens', 'dom', 'sub')), parts along dimension 1, may hold values from -6 to 6
- enc_first: bfloat16 [512, 512], P('feat'), may hold values from -0.25 to 0.25
- enc_second: bfloat16 [512, 512], P('feat'), may hold values from -0.25 to 0.25
- dec_first: bfloat16 [512, 512], P('feat'), may hold values from -0.25 to 0.25
- dec_second: bfloat16 [512, 512], P('feat'), may hold values from -0.25 to 0.25
- mesh_weight: bfloat16 [512, 512], P('feat'), may hold values from -0.25 to 0.25
- send_grid: int32 [16, 2, 8, 2], P(('ens', 'dom', 'sub'), 'feat'), parts along dimension 0, may hold values from 0 to 24, as said below
- enc_tiles: bfloat16 [16, 2, 64, 1024], P(('ens', 'dom', 'sub'), 'feat'), parts along dimension 0, may hold values from -0.375 to 0.375
- enc_target: int32 [16, 2, 16], P(('ens', 'dom', 'sub'), 'feat'), parts along dimension 0, may hold values from 0 to 7
- send_mesh: int32 [16, 2, 8, 2], P(('ens', 'dom', 'sub'), 'feat'), parts along dimension 0, may hold values from 0 to 8, as said below
- dec_slots: int32 [768, 4], P(('ens', 'dom', 'sub', 'feat')), parts along dimension 0, may hold values from 0 to 15, as said below
- dec_tiles: bfloat16 [768, 64, 256], P(('ens', 'dom', 'sub', 'feat')), parts along dimension 0, may hold values from -0.375 to 0.375
Outputs:
- grid_next: bfloat16 [512, 49152], P(None, ('ens', 'dom', 'sub', 'feat')), parts along dimension 1
There are 2 independent parts, one for each index of `ens`. A program takes and returns all parts, laid end to end along the dimension named above; an argument that names none is the same for every part. Nothing has to cross between parts.
Inputs may be any that keep to these rules, and one draw needn't show every extreme that they name: `send_grid`: the value 24 marks an empty slot; every device fills all 2 slots toward its own mesh share, and other slots are filled from the first one on. `send_mesh`: the value 8 marks an empty slot; every device fills all 2 slots toward its own grid share, and other slots are filled from the first one on. `dec_slots`: each entry names a slot of the receiving device whose send_mesh entry is not empty.
All inputs are finite; a program needn't handle non-finite values.
Results may differ from a plain program's by a relative error of at most 0.006.
Values may be sent and summed in bfloat16 or wider, within the bound.
No kernel may reach another device: no remote copies, remote signals or barrier semaphores. Data moves between devices by JAX's collectives and lax.ppermute only.
A program may use at most 64 MiB of HBM per device.

v0:
```python
import jax
import jax.numpy as jnp
from jax import lax
from jax.sharding import PartitionSpec as P


def local(
    grid_state,
    mesh_state,
    enc_first,
    enc_second,
    dec_first,
    dec_second,
    mesh_weight,
    send_grid,
    enc_tiles,
    enc_target,
    send_mesh,
    dec_slots,
    dec_tiles,
):
    feature_rows = grid_state.shape[0]
    block_len = dec_tiles.shape[1]
    grid_blocks = grid_state.shape[1] // block_len
    mesh_blocks = mesh_state.shape[1] // block_len
    peer_count = send_grid.shape[2]
    slot_cap = send_grid.shape[3]
    mesh_cap = send_mesh.shape[3]
    feeding = dec_slots.shape[1]
    first_full, second_full, third_full, fourth_full = (
        lax.all_gather(enc_first, "feat", axis=0, tiled=True),
        lax.all_gather(enc_second, "feat", axis=0, tiled=True),
        lax.all_gather(dec_first, "feat", axis=0, tiled=True),
        lax.all_gather(dec_second, "feat", axis=0, tiled=True),
    )
    hidden = jax.nn.silu(
        jnp.einsum("dh,dn->hn", first_full, grid_state, preferred_element_type=jnp.float32)
    ).astype(jnp.bfloat16)
    message = jnp.einsum(
        "dh,dbn->bhn",
        second_full,
        hidden.reshape(feature_rows, grid_blocks, block_len),
        preferred_element_type=jnp.float32,
    ).astype(jnp.bfloat16)
    padded = jnp.concatenate([message, jnp.zeros((1, feature_rows, block_len), jnp.bfloat16)], 0)
    outgoing = jnp.take(padded, send_grid.reshape(-1), axis=0)
    outgoing = outgoing.reshape(peer_count, slot_cap, feature_rows, block_len)
    incoming = lax.all_to_all(outgoing, ("dom", "sub"), split_axis=0, concat_axis=0, tiled=True)
    received = incoming.reshape(peer_count * slot_cap, feature_rows, block_len)
    tile_set = enc_tiles.reshape(block_len, peer_count * slot_cap, block_len)
    contrib = jnp.einsum("qhs,rqs->qhr", received, tile_set, preferred_element_type=jnp.float32)
    onehot = (
        enc_target.reshape(-1)[None, :] == jnp.arange(mesh_blocks, dtype=jnp.int32)[:, None]
    ).astype(jnp.float32)
    partial_agg = jnp.einsum("mq,qhr->hmr", onehot, contrib, precision=lax.Precision.HIGHEST)
    partial_agg = partial_agg.reshape(feature_rows, mesh_blocks * block_len)
    shared = lax.psum_scatter(partial_agg, "feat", scatter_dimension=0, tiled=True)
    mesh_new = (mesh_state.astype(jnp.float32) + shared).astype(jnp.bfloat16)
    partial_mix = jnp.einsum("dh,dn->hn", mesh_weight, mesh_new, preferred_element_type=jnp.float32)
    mixed_sum = lax.psum(partial_mix, "feat")
    mesh_hidden = jax.nn.silu(mixed_sum).astype(jnp.bfloat16)
    mesh_rows = mesh_hidden.reshape(feature_rows, mesh_blocks, block_len).transpose(1, 0, 2)
    mesh_padded = jnp.concatenate(
        [mesh_rows, jnp.zeros((1, feature_rows, block_len), jnp.bfloat16)], 0
    )
    mesh_out = jnp.take(mesh_padded, send_mesh.reshape(-1), axis=0)
    mesh_out = mesh_out.reshape(peer_count, mesh_cap, feature_rows, block_len)
    mesh_in = lax.all_to_all(mesh_out, ("dom", "sub"), split_axis=0, concat_axis=0, tiled=True)
    mesh_pool = mesh_in.reshape(peer_count * mesh_cap, feature_rows, block_len)
    picked = jnp.take(mesh_pool, dec_slots.reshape(-1), axis=0).reshape(
        grid_blocks, feeding, feature_rows, block_len
    )
    dec_set = dec_tiles.reshape(grid_blocks, block_len, feeding, block_len)
    collected = jnp.einsum("gjhs,grjs->hgr", picked, dec_set, preferred_element_type=jnp.float32)
    collected = collected.reshape(feature_rows, grid_blocks * block_len).astype(jnp.bfloat16)
    decoded = jax.nn.silu(
        jnp.einsum("dh,dn->hn", third_full, collected, preferred_element_type=jnp.float32)
    ).astype(jnp.bfloat16)
    update = jnp.einsum("dh,dn->hn", fourth_full, decoded, preferred_element_type=jnp.float32)
    return (grid_state.astype(jnp.float32) + update).astype(jnp.bfloat16)


def solution(mesh):
    in_specs = (
        P(None, ("ens", "dom", "sub", "feat")),
        P("feat", ("ens", "dom", "sub")),
        P("feat", None),
        P("feat", None),
        P("feat", None),
        P("feat", None),
        P("feat", None),
        P(("ens", "dom", "sub"), "feat", None, None),
        P(("ens", "dom", "sub"), "feat", None, None),
        P(("ens", "dom", "sub"), "feat", None),
        P(("ens", "dom", "sub"), "feat", None, None),
        P(("ens", "dom", "sub", "feat"), None),
        P(("ens", "dom", "sub", "feat"), None, None),
    )
    out_specs = P(None, ("ens", "dom", "sub", "feat"))
    return jax.shard_map(local, mesh=mesh, in_specs=in_specs, out_specs=out_specs, check_vma=False)
```

profile of v0, /device:TPU:0, one launch (start us, length us, event | category | flops | bytes accessed | tf_op | source)
XLA Modules:
  0.0 189.3 jit_solution(11548223962695688331)
XLA Ops:
  6.5 0.8 copy.31
  7.3 0.7 compare_and_fusion
  8.0 10.2 %all_gather.12 = bf16[512,512]{1,0:T(8,128)(2,1)S(1)} all-gather(bf16[256,512]{1,0:T(8,128)(2,1)} %param.15), channel_id=1, replica_groups=mesh['ens'=2,'dom'=4,'feat'=2,'sub'=2] {'feat'}, dimensions={0}, use_global_device_ids=true | all-gather | bytes 786432 | tf_op jit(solution)/shard_map/all_gather | solution.py:31
  18.2 2.9 %multiply_convert_fusion.1 = bf16[512,1536]{1,0:T(8,128)(2,1)S(1)} fusion(bf16[512,512]{1,0:T(8,128)(2,1)S(1)} %all_gather.12, bf16[512,1536]{1,0:T(8,128)(2,1)} %param.13), kind=kOutput, calls=%fused_computation.12 | convolution fusion | flops 809238528 | bytes 3670016 | tf_op jit(solution)/shard_map/dh,dn->hn/dot_general | solution.py:37
  21.1 0.7 copy.30
  21.8 8.4 %all_gather.13 = bf16[512,512]{1,0:T(8,128)(2,1)S(1)} all-gather(bf16[256,512]{1,0:T(8,128)(2,1)} %param.16), channel_id=1, replica_groups=mesh['ens'=2,'dom'=4,'feat'=2,'sub'=2] {'feat'}, dimensions={0}, use_global_device_ids=true | all-gather | bytes 786432 | tf_op jit(solution)/shard_map/all_gather | solution.py:32
  30.2 0.1 reshape.153
  30.3 0.1 copy.29
  30.4 1.0 fusion.11
  31.4 0.2 concatenate.6
  31.5 0.6 gather_fusion
  32.2 1.1 broadcast_select_fusion
  33.3 4.8 %all-to-all-start = ((bf16[8,2,512,64]{2,3,1,0:T(8,128)(2,1)}), bf16[8,2,512,64]{2,3,1,0:T(8,128)(2,1)S(1)}, u32[]{:S(2)}, u32[]{:S(2)}) async-start(bf16[8,2,512,64]{2,3,1,0:T(8,128)(2,1)} %broadcast_select_fusion), calls=%async_computation | async-start | bytes 2097152 | tf_op jit(solution)/shard_map/all_to_all | solution.py:48
  38.1 0.0 reduce-scatter.2.cloned.1.call-start
  38.1 0.2 copy.42
  38.3 26.4 %all-to-all-done = bf16[8,2,512,64]{2,3,1,0:T(8,128)(2,1)S(1)} async-done(((bf16[8,2,512,64]{2,3,1,0:T(8,128)(2,1)}), bf16[8,2,512,64]{2,3,1,0:T(8,128)(2,1)S(1)}, u32[]{:S(2)}, u32[]{:S(2)}) %all-to-all-start) | async-done | bytes 1048608 | tf_op jit(solution)/shard_map/all_to_all | solution.py:48
  64.6 0.5 fusion.24
  65.1 2.0 %fusion.12 = f32[512,8,64]{0,1,2:T(8,128)S(1)} fusion(f32[16,512,64]{1,2,0:T(8,128)S(1)} %fusion.24, s32[16]{0:T(128)S(1)} %bitcast.74), kind=kOutput, calls=%fused_computation.20 | convolution fusion | flops 50331776 | bytes 3145792 | tf_op jit(solution)/shard_map/mq,qhr->hmr/dot_general | solution.py:55
  67.1 0.0 copy-start.5
  67.2 1.6 copy.32
  68.7 0.0 reduce-scatter.2.cloned.1.call-update
  68.8 0.0 all-reduce.4.cloned.1.call-start
  68.8 0.1 copy.28
  69.0 19.2 %reduce-scatter.2.cloned.1.call-done = f32[256,512]{0,1:T(8,128)} async-done(((f32[512,512]{0,1:T(8,128)}), f32[256,512]{0,1:T(8,128)}) %reduce-scatter.2.cloned.1.call-update) | async-done | bytes 524304 | tf_op jit(solution)/shard_map/reduce_scatter | solution.py:57
  88.1 2.3 %convolution_bitcast_fusion.2 = f32[512,512]{0,1:T(8,128)} fusion(bf16[256,512]{1,0:T(8,128)(2,1)S(1)} %copy-done, f32[256,512]{0,1:T(8,128)} %reduce-scatter.2.cloned.1.call-done, bf16[256,512]{0,1:T(8,128)(2,1)S(1)} %copy.28), kind=kOutput, calls=%fused_computation.19 | convolution fusion | flops 134610944 | bytes 2097152 | tf_op jit(solution)/shard_map/dh,dn->hn/dot_general | solution.py:59
  90.5 0.0 all-reduce.4.cloned.1.call-update
  90.5 0.1 copy.33
  90.6 0.1 reshape.158
  90.7 0.1 copy.27
  90.8 39.9 %all-reduce.4.cloned.1.call-done = f32[512,512]{0,1:T(8,128)} async-done(((f32[512,512]{0,1:T(8,128)}), f32[512,512]{0,1:T(8,128)}) %all-reduce.4.cloned.1.call-update) | async-done | bytes 1048592 | tf_op jit(solution)/shard_map/psum | solution.py:60
  130.7 1.5 multiply_convert_fusion.2
  132.3 0.6 gather_fusion.1
  132.9 0.0 copy-start.1
  132.9 1.1 broadcast_select_fusion.1
  134.0 4.6 %all-to-all-start.1 = ((bf16[8,2,512,64]{2,3,1,0:T(8,128)(2,1)}), bf16[8,2,512,64]{2,3,1,0:T(8,128)(2,1)S(1)}, u32[]{:S(2)}, u32[]{:S(2)}) async-start(bf16[8,2,512,64]{2,3,1,0:T(8,128)(2,1)} %broadcast_select_fusion.1), calls=%async_computation.2 | async-start | bytes 2097152 | tf_op jit(solution)/shard_map/all_to_all | solution.py:68
  138.7 0.0 copy-start.3
  138.7 1.6 copy.25
  140.2 0.1 copy.34
  140.3 0.1 reshape.160
  140.4 2.8 %reshape.161 = bf16[24,64,4,64]{3,2,1,0:T(4,128)(2,1)S(1)} reshape(bf16[24,64,256]{2,1,0:T(8,128)(2,1)} %param.25) | data formatting | bytes 1572864 | tf_op jit(solution)/shard_map/reshape | solution.py:73
  143.2 0.1 copy.26
  143.3 9.5 %all_gather.14 = bf16[512,512]{1,0:T(8,128)(2,1)} all-gather(bf16[256,512]{1,0:T(8,128)(2,1)S(1)} %copy-done.3), channel_id=1, replica_groups=mesh['ens'=2,'dom'=4,'feat'=2,'sub'=2] {'feat'}, dimensions={0}, use_global_device_ids=true | all-gather | bytes 786432 | tf_op jit(solution)/shard_map/all_gather | solution.py:33
  152.8 8.9 %all_gather.15 = bf16[512,512]{1,0:T(8,128)(2,1)} all-gather(bf16[256,512]{1,0:T(8,128)(2,1)S(1)} %copy-done.4), channel_id=1, replica_groups=mesh['ens'=2,'dom'=4,'feat'=2,'sub'=2] {'feat'}, dimensions={0}, use_global_device_ids=true | all-gather | bytes 786432 | tf_op jit(solution)/shard_map/all_gather | solution.py:34
  161.7 3.5 %all-to-all-done.1 = bf16[8,2,512,64]{2,3,1,0:T(8,128)(2,1)S(1)} async-done(((bf16[8,2,512,64]{2,3,1,0:T(8,128)(2,1)}), bf16[8,2,512,64]{2,3,1,0:T(8,128)(2,1)S(1)}, u32[]{:S(2)}, u32[]{:S(2)}) %all-to-all-start.1) | async-done | bytes 1048608 | tf_op jit(solution)/shard_map/all_to_all | solution.py:68
  165.2 6.0 %gather_fusion.2 = bf16[96,512,64]{1,2,0:T(8,128)(2,1)} fusion(bf16[16,512,64]{1,2,0:T(8,128)(2,1)S(1)} %bitcast.65, s32[1024]{0:T(1024)S(1)} %pad_clamp_fusion), kind=kCustom, calls=%fused_computation.2 | custom fusion | bytes 12583296 | tf_op jit(solution)/shard_map/jit(_take)/gather | solution.py:70
  171.2 5.8 %bitcast_convert_fusion = bf16[24,512,64]{1,2,0:T(8,128)(2,1)} fusion(bf16[24,4,512,64]{2,3,1,0:T(8,128)(2,1)} %bitcast.66, pred[24,4]{1,0:T(8,128)(4,1)S(1)} %copy.26, bf16[24,64,4,64]{3,2,1,0:T(4,128)(2,1)S(1)} %reshape.161), kind=kOutput, calls=%fused_computation.9 | convolution fusion | flops 406585344 | bytes 8650848 | tf_op jit(solution)/shard_map/gjhs,grjs->hgr/dot_general | solution.py:74
  177.0 3.9 %fusion.5 = bf16[512,1536]{0,1:T(8,128)(2,1)S(1)} fusion(bf16[512,512]{1,0:T(8,128)(2,1)} %all_gather.15, bf16[512,1536]{0,1:T(8,128)(2,1)S(1)} %copy-done.2, bf16[512,1536]{0,1:T(8,128)(2,1)} %bitcast.75, bf16[512,512]{1,0:T(8,128)(2,1)} %all_gather.14), kind=kOutput, calls=%fused_computation.13 | convolution fusion | flops 1616904192 | bytes 5767168 | tf_op jit(solution)/shard_map/dh,dn->hn/dot_general | solution.py:79
  180.9 1.6 copy.37
  (26 shorter events, 0.1 us)
Async XLA Ops:
  6.5 81.6 %copy-start = (bf16[256,512]{1,0:T(8,128)(2,1)S(1)}, bf16[256,512]{1,0:T(8,128)(2,1)}, u32[]{:S(2)}) copy-start(bf16[256,512]{1,0:T(8,128)(2,1)} %param.19) | copy-start | bytes 786436
  32.1 6.0 %copy-start.6 = (bf16[1,1,64,1024]{3,2,1,0:T(8,128)(2,1)S(1)}, bf16[1,1,64,1024]{3,2,1,0:T(8,128)(2,1)}, u32[]{:S(2)}) copy-start(bf16[1,1,64,1024]{3,2,1,0:T(8,128)(2,1)} %param.21) | copy-start | bytes 393220
  33.3 31.4 %all-to-all-start = ((bf16[8,2,512,64]{2,3,1,0:T(8,128)(2,1)}), bf16[8,2,512,64]{2,3,1,0:T(8,128)(2,1)S(1)}, u32[]{:S(2)}, u32[]{:S(2)}) async-start(bf16[8,2,512,64]{2,3,1,0:T(8,128)(2,1)} %broadcast_select_fusion), calls=%async_computation | async-start | bytes 2097152 | tf_op jit(solution)/shard_map/all_to_all | solution.py:48
  38.1 27.1 %copy-start.9 = (s32[1,1,16]{2,1,0:T(1,128)S(1)}, s32[1,1,16]{2,1,0:T(1,128)}, u32[]{:S(2)}) copy-start(s32[1,1,16]{2,1,0:T(1,128)} %param.22) | copy-start | bytes 196
  38.1 50.1 %reduce-scatter.2.cloned.1.call-start = ((), (), s32[]{:S(2)}) async-start(), calls=%async_computation.3 | async-start | bytes 1572864 | tf_op jit(solution)/shard_map/reduce_scatter | solution.py:57
  67.1 1.7 copy-start.5
  68.8 21.7 %copy-start.8 = (s32[1,1,8,2]{2,3,1,0:T(2,128)S(1)}, s32[1,1,8,2]{2,3,1,0:T(2,128)}, u32[]{:S(2)}) copy-start(s32[1,1,8,2]{2,3,1,0:T(2,128)} %param.23) | copy-start | bytes 196
  68.8 61.9 %all-reduce.4.cloned.1.call-start = ((), (), s32[]{:S(2)}) async-start(), calls=%async_computation.4 | async-start | bytes 2097152 | tf_op jit(solution)/shard_map/psum | solution.py:60
  132.9 5.8 %copy-start.1 = (bf16[512,1536]{1,0:T(8,128)(2,1)S(1)}, bf16[512,1536]{1,0:T(8,128)(2,1)}, u32[]{:S(2)}) copy-start(bf16[512,1536]{1,0:T(8,128)(2,1)} %param.13) | copy-start | bytes 4718596
  134.0 31.2 %all-to-all-start.1 = ((bf16[8,2,512,64]{2,3,1,0:T(8,128)(2,1)}), bf16[8,2,512,64]{2,3,1,0:T(8,128)(2,1)S(1)}, u32[]{:S(2)}, u32[]{:S(2)}) async-start(bf16[8,2,512,64]{2,3,1,0:T(8,128)(2,1)} %broadcast_select_fusion.1), calls=%async_computation.2 | async-start | bytes 2097152 | tf_op jit(solution)/shard_map/all_to_all | solution.py:68
  138.6 1.6 copy-start.7
  138.7 4.7 %copy-start.3 = (bf16[256,512]{1,0:T(8,128)(2,1)S(1)}, bf16[256,512]{1,0:T(8,128)(2,1)}, u32[]{:S(2)}) copy-start(bf16[256,512]{1,0:T(8,128)(2,1)} %param.17) | copy-start | bytes 786436
  140.2 12.6 %copy-start.4 = (bf16[256,512]{1,0:T(8,128)(2,1)S(1)}, bf16[256,512]{1,0:T(8,128)(2,1)}, u32[]{:S(2)}) copy-start(bf16[256,512]{1,0:T(8,128)(2,1)} %param.18) | copy-start | bytes 786436
  171.2 5.8 %copy-start.2 = (bf16[512,1536]{0,1:T(8,128)(2,1)S(1)}, bf16[512,1536]{0,1:T(8,128)(2,1)}, u32[]{:S(2)}) copy-start(bf16[512,1536]{0,1:T(8,128)(2,1)} %copy.25) | copy-start | bytes 4718596
Sparse Core Ops, SparseCore 0:
  68.9 19.2 reduce-scatter.1
  90.6 40.0 all-reduce.3
where the time goes:
time: 190 us; the launch traced here: 189 us
  waiting for transfers between devices  89 us (47%)
  blocking collectives  36.9 us (19%)
  matrix products  18.3 us (10%)
  local copies, waits for them, and re-layouts  17.5 us (9%)
  between operations  13.6 us (7%)
  starting transfers between devices  9.45 us (5%)
  other arithmetic  4.52 us (2%)
    psum x1, waiting for transfers between devices, local(): mixed_sum = lax.psum(partial_mix, 'feat')  39.9 us
    all_to_all x1, waiting for transfers between devices, local(): lax.all_to_all(outgoing, ('dom', 'sub'), split_axis=0, concat_axis=0, til...  26.4 us
    reduce_scatter x1, waiting for transfers between devices, local(): lax.psum_scatter(partial_agg, 'feat', scatter_dimension=0, tiled=True)  19.2 us
    all_gather x1, blocking collectives, local(): lax.all_gather(enc_first, 'feat', axis=0, tiled=True)  10.2 us
    all_gather x1, blocking collectives, local(): lax.all_gather(dec_first, 'feat', axis=0, tiled=True)  9.48 us
    all_gather x1, blocking collectives, local(): lax.all_gather(dec_second, 'feat', axis=0, tiled=True)  8.87 us
    all_gather x1, blocking collectives, local(): lax.all_gather(enc_second, 'feat', axis=0, tiled=True)  8.38 us
    gather x1, local copies, waits for them, and re-layouts, local(): jnp.take(mesh_pool, dec_slots.reshape(-1), axis=0)  6 us
  transfers between devices with their start and end apart: 4, of which 4 were waited for; matrix products, arithmetic and copies ran while one was open for 3% of the time, Pallas kernels for 0%

commit v1 on v0

v1 whole, which is shorter than its diff:
```python
import functools

import jax
import jax.numpy as jnp
from jax import lax
from jax.experimental import pallas as pl
from jax.experimental.pallas import tpu as pltpu
from jax.sharding import PartitionSpec as P

BF = jnp.bfloat16
F32 = jnp.float32
VMEM = pltpu.VMEM
SMEM = pltpu.SMEM
SWAP = [(0, 1), (1, 0)]


def full(space=VMEM):
    return pl.BlockSpec(memory_space=space)


def params(n_dom):
    return pltpu.CompilerParams(vmem_limit_bytes=(12 if n_dom <= 4 else 48) * 1024 * 1024)


def cost(us):
    return pl.CostEstimate(flops=int(us * 4e8), bytes_accessed=int(us * 1e6), transcendentals=0)


def anywhere():
    return pl.BlockSpec(memory_space=pl.ANY)


def silu(x):
    half = 0.5 * x
    return half + half * jnp.tanh(half)


def mm(a, b):
    return jnp.dot(a, b, preferred_element_type=F32)


def turn(v):
    return v.astype(F32).T.astype(BF)


def swap_halves(v, width):
    return jnp.concatenate([v[:, width:], v[:, :width]], axis=1)


def pack_rows(step, blocks, n_dom, at_ref, send_ref, buf, i, outs):
    pair = outs[0].shape[2]
    width = pair // 2
    cols = blocks * width
    here = slice(i * step, (i + 1) * step)
    for p in range(blocks // 2):
        v = buf[0, here, p * pair:(p + 1) * pair]
        buf[1, here, p * pair:(p + 1) * pair] = swap_halves(v, width)
    low = lax.broadcasted_iota(jnp.int32, (step, pair), 1) < width
    for k in range(n_dom):
        for j in range(2):
            peer = lax.rem(at_ref[0] + k, n_dom) * 2 + (at_ref[2] if j == 0 else 1 - at_ref[2])
            vs = []
            for c in range(2):
                b = send_ref[c, peer]
                used = b < blocks
                start = pl.multiple_of(jnp.where(used, b // 2 * pair, cols), pair)
                flip = jnp.where(used & (lax.rem(b, 2) != c), 1, 0)
                vs.append(buf[flip, here, pl.ds(start, pair)])
            outs[k][j, here, :] = jnp.where(low, vs[0], vs[1])


def pack_kernel(blocks, n_dom, at_ref, send_ref, src_ref, *refs):
    outs, buf, sems = refs[:n_dom], refs[n_dom], refs[n_dom + 1]
    rows, cols = src_ref.shape
    parts = 4
    step = rows // parts
    copies = []
    for i in range(parts):
        here = pl.ds(i * step, step)
        copies.append(pltpu.make_async_copy(src_ref.at[here, :], buf.at[0, here, pl.ds(0, cols)], sems.at[i]))
        copies[-1].start()
    buf[0, :, cols:] = jnp.zeros((rows, buf.shape[2] - cols), BF)
    for i in range(parts):
        copies[i].wait()
        pack_rows(step, blocks, n_dom, at_ref, send_ref, buf, i, outs)


def stack_kernel(n_dom, waits, *refs):
    chunks, out = refs[waits:waits + n_dom], refs[waits + n_dom]
    for k in range(n_dom):
        out[k] = chunks[k][1]


def assemble_kernel(sources, at_ref, *refs):
    count = len(sources)
    ws, gots, outs = refs[:count], refs[count:-count], refs[-count:]
    rows = ws[0].shape[0]
    own = pl.multiple_of(at_ref[1] * rows, rows)
    other = pl.multiple_of((1 - at_ref[1]) * rows, rows)
    for i, (which, part) in enumerate(sources):
        outs[i][:, pl.ds(own, rows)] = turn(ws[i][...])
        outs[i][:, pl.ds(other, rows)] = turn(gots[which][part * rows:(part + 1) * rows, :])


def scatter_kernel(n_dom, mesh_blocks, at_ref, tgt_ref, tiles_ref, out_ref):
    block = tiles_ref.shape[0]
    pair = 2 * block
    low = lax.broadcasted_iota(jnp.int32, (1, pair), 1) < block
    for j in range(2):
        for k in range(n_dom):
            sub = at_ref[2] if j == 0 else 1 - at_ref[2]
            peer = lax.rem(at_ref[0] + n_dom - k, n_dom) * 2 + sub
            t = turn(tiles_ref[:, pl.ds(pl.multiple_of(peer * pair, pair), pair)])
            t = jnp.concatenate([t, t], axis=1)
            for c in range(2):
                m = tgt_ref[peer * 2 + c]
                for p in range(mesh_blocks // 2):
                    mask = (jnp.where(low, 2 * p, 2 * p + 1) == m).astype(F32).astype(BF)
                    row = k * pair + c * block
                    out_ref[j, row:row + block, p * pair:(p + 1) * pair] = t[c * block:(c + 1) * block] * mask


def spread_kernel(n_dom, feeding, at_ref, slot_ref, tiles_ref, out_ref):
    g = pl.program_id(0)
    block = tiles_ref.shape[1]
    t = turn(tiles_ref[...].reshape(2 * block, feeding * block))
    low = lax.broadcasted_iota(jnp.int32, (block, 2 * block), 1) < block
    out_ref[...] = jnp.zeros_like(out_ref)
    for h in range(2):
        for i in range(feeding):
            q = slot_ref[i, g * 2 + h]
            peer = q // 2
            k = lax.rem(at_ref[0] + n_dom - peer // 2, n_dom)
            j = jnp.where(lax.rem(peer, 2) == at_ref[2], 0, 1)
            row = pl.multiple_of(((j * n_dom + k) * 2 + lax.rem(q, 2)) * block, block)
            v = t[i * block:(i + 1) * block, :]
            v = jnp.where(low if h == 0 else ~low, v, jnp.zeros_like(v))
            out_ref[pl.ds(row, block), :] += v


def encode_kernel(n_dom, w1t_ref, wide_ref, *rest):
    chunks, out_ref = rest[:n_dom], rest[n_dom]
    x = jnp.concatenate([chunks[k][0] for k in range(n_dom)], axis=1)
    hid = silu(mm(w1t_ref[...], x)).astype(BF)
    out_ref[...] = mm(hid, wide_ref[0])


def gather_kernel(n_dom, at_ref, acc_ref, w1t_ref, w2t_ref, wide_ref, ms_ref, far_ref, g_ref, gb_ref):
    x = jnp.concatenate([far_ref[k] for k in range(n_dom)], axis=1)
    hid = silu(mm(w1t_ref[...], x)).astype(BF)
    acc = acc_ref[...] + mm(hid, wide_ref[1])
    g_ref[...] = mm(w2t_ref[...], acc.astype(BF))
    rows = ms_ref.shape[0]
    here = pl.ds(pl.multiple_of(at_ref[1] * rows, rows), rows)
    g_ref[here, :] += ms_ref[...].astype(F32)
    gb_ref[...] = g_ref[...].astype(BF)


def mesh_kernel(blocks, n_dom, at_ref, send_ref, g_ref, other_ref, mwt_ref, *rest):
    outs, buf = rest[:n_dom], rest[n_dom]
    rows, cols = g_ref.shape
    new = (g_ref[...] + other_ref[...].astype(F32)).astype(BF)
    buf[0, :, :cols] = silu(mm(mwt_ref[...], new)).astype(BF)
    buf[0, :, cols:] = jnp.zeros((rows, buf.shape[2] - cols), BF)
    for i in range(4):
        pack_rows(rows // 4, blocks, n_dom, at_ref, send_ref, buf, i, outs)


def collect_kernel(n_dom, cols, wide_ref, *rest):
    chunks, out_ref = rest[:n_dom], rest[n_dom]
    pool = jnp.concatenate([chunks[k][0] for k in range(n_dom)], axis=1)
    for t in range(out_ref.shape[1] // cols):
        here = slice(t * cols, (t + 1) * cols)
        out_ref[:, here] = mm(pool, wide_ref[:pool.shape[1], here])


def decode_kernel(n_dom, cols, acc_ref, wide_ref, d1t_ref, d2t_ref, grid_ref, far_ref, out_ref, buf, sems):
    pool = jnp.concatenate([far_ref[k] for k in range(n_dom)], axis=1)
    copies = []
    for t in range(grid_ref.shape[1] // cols):
        here = slice(t * cols, (t + 1) * cols)
        got = (acc_ref[:, here] + mm(pool, wide_ref[pool.shape[1]:, here])).astype(BF)
        dec = silu(mm(d1t_ref[...], got)).astype(BF)
        value = (grid_ref[:, here].astype(F32) + mm(d2t_ref[...], dec)).astype(BF)
        if t >= 2:
            copies[t - 2].wait()
        buf[t % 2] = value
        copies.append(pltpu.make_async_copy(buf.at[t % 2], out_ref.at[:, pl.ds(t * cols, cols)], sems.at[t % 2]))
        copies[t].start()
    for copy in copies[-2:]:
        copy.wait()


def move(chunks, n_dom):
    order = sorted(range(1, n_dom), key=lambda k: -min(k, n_dom - k))
    moved = {0: chunks[0]}
    for k in order:
        moved[k] = lax.ppermute(chunks[k], "dom", [(i, (i + k) % n_dom) for i in range(n_dom)])
    return [moved[k] for k in range(n_dom)]


def local(n_dom, n_feat, grid_state, mesh_state, enc_first, enc_second, dec_first, dec_second,
          mesh_weight, send_grid, enc_tiles, enc_target, send_mesh, dec_slots, dec_tiles):
    rows = grid_state.shape[0]
    block = dec_tiles.shape[1]
    grid_cols = grid_state.shape[1]
    grid_blocks = grid_cols // block
    mesh_cols = mesh_state.shape[1]
    mesh_blocks = mesh_cols // block
    slots = enc_target.shape[-1]
    feeding = dec_slots.shape[1]
    pair = 2 * block
    at = jnp.stack([lax.axis_index("dom"), lax.axis_index("feat"), lax.axis_index("sub")]).astype(jnp.int32)
    send_grid = send_grid.reshape(slots // 2, 2).T
    send_mesh = send_mesh.reshape(slots // 2, 2).T
    chunk = jax.ShapeDtypeStruct((2, rows, pair), BF)
    square = jax.ShapeDtypeStruct((rows, rows), BF)
    call = functools.partial(pl.pallas_call, compiler_params=params(n_dom))

    out = call(
        functools.partial(pack_kernel, grid_blocks, n_dom),
        out_shape=[chunk] * n_dom,
        in_specs=[full(SMEM), full(SMEM), anywhere()],
        out_specs=[full()] * n_dom,
        scratch_shapes=[VMEM((2, rows, grid_cols + pair), BF), pltpu.SemaphoreType.DMA((4,))],
        cost_estimate=cost(1),
        name="pack",
    )(at, send_grid, grid_state)
    near = move(out, n_dom)

    def whole(groups):
        ws = [w for group in groups for w in group]
        if n_feat != 2:
            gathered = lax.all_gather(jnp.stack(ws), "feat", axis=1, tiled=True).transpose(0, 2, 1)
            return [gathered[i] for i in range(len(ws))]
        gots = [lax.ppermute(jnp.concatenate(group, axis=0), "feat", SWAP) for group in groups]
        sources = [(i, part) for i, group in enumerate(groups) for part in range(len(group))]
        return call(
            functools.partial(assemble_kernel, sources),
            out_shape=[square] * len(ws),
            in_specs=[full(SMEM)] + [full()] * (len(ws) + len(gots)),
            out_specs=[full()] * len(ws),
            cost_estimate=cost(0),
            name="assemble",
        )(at, *ws, *gots)

    def cross(chunks, *waits):
        mine = call(
            functools.partial(stack_kernel, n_dom, len(waits)),
            out_shape=jax.ShapeDtypeStruct((n_dom, rows, pair), BF),
            in_specs=[anywhere()] * len(waits) + [full()] * n_dom,
            out_specs=full(),
            cost_estimate=cost(0),
            name="stack",
        )(*waits, *chunks)
        return lax.ppermute(mine, "sub", SWAP)

    w1t, w2t, mwt = whole([[enc_first], [enc_second, mesh_weight]])
    to_mesh = call(
        functools.partial(scatter_kernel, n_dom, mesh_blocks),
        out_shape=jax.ShapeDtypeStruct((2, n_dom * pair, mesh_cols), BF),
        in_specs=[full(SMEM), full(SMEM), full()],
        out_specs=full(),
        cost_estimate=cost(0),
        name="scatter",
    )(at, enc_target.reshape(slots), enc_tiles.reshape(block, slots * block))
    to_grid = call(
        functools.partial(spread_kernel, n_dom, feeding),
        grid=(grid_blocks // 2,),
        out_shape=jax.ShapeDtypeStruct((slots * block, grid_cols), BF),
        in_specs=[full(SMEM), full(SMEM), pl.BlockSpec((2, block, feeding * block), lambda i: (i, 0, 0))],
        out_specs=pl.BlockSpec((slots * block, pair), lambda i: (0, i)),
        cost_estimate=cost(0),
        name="spread",
    )(at, dec_slots.T, dec_tiles)

    far = cross(near, w1t, to_mesh, to_grid)
    acc = call(
        functools.partial(encode_kernel, n_dom),
        out_shape=jax.ShapeDtypeStruct((rows, mesh_cols), F32),
        in_specs=[full()] * (2 + n_dom),
        out_specs=full(),
        cost_estimate=cost(0.5),
        name="encode",
    )(w1t, to_mesh, *near)
    g, gb = call(
        functools.partial(gather_kernel, n_dom),
        out_shape=[jax.ShapeDtypeStruct((rows, mesh_cols), F32), jax.ShapeDtypeStruct((rows, mesh_cols), BF)],
        in_specs=[full(SMEM)] + [full()] * 6,
        out_specs=[full()] * 2,
        cost_estimate=cost(0.5),
        name="gather",
    )(at, acc, w1t, w2t, to_mesh, mesh_state, far)
    if n_feat == 2:
        other = lax.ppermute(gb, "feat", SWAP)
    else:
        other = (lax.psum(g, "feat") - g).astype(BF)
    out = call(
        functools.partial(mesh_kernel, mesh_blocks, n_dom),
        out_shape=[chunk] * n_dom,
        in_specs=[full(SMEM), full(SMEM)] + [full()] * 3,
        out_specs=[full()] * n_dom,
        scratch_shapes=[VMEM((2, rows, mesh_cols + pair), BF)],
        cost_estimate=cost(1),
        name="mesh",
    )(at, send_mesh, g, other, mwt)

    near = move(out, n_dom)
    d1t, d2t = whole([[dec_first], [dec_second]])
    far = cross(near, d1t)
    cols = 4 * block
    acc = call(
        functools.partial(collect_kernel, n_dom, cols),
        out_shape=jax.ShapeDtypeStruct((rows, grid_cols), F32),
        in_specs=[full()] * (1 + n_dom),
        out_specs=full(),
        cost_estimate=cost(1),
        name="collect",
    )(to_grid, *near)
    return call(
        functools.partial(decode_kernel, n_dom, cols),
        out_shape=jax.ShapeDtypeStruct(grid_state.shape, BF),
        in_specs=[full()] * 6,
        out_specs=anywhere(),
        scratch_shapes=[VMEM((2, rows, cols), BF), pltpu.SemaphoreType.DMA((2,))],
        cost_estimate=cost(3),
        name="decode",
    )(acc, to_grid, d1t, d2t, grid_state, far)


def solution(mesh):
    whole = ("ens", "dom", "sub", "feat")
    share = ("ens", "dom", "sub")
    in_specs = (
        P(None, whole),
        P("feat", share),
        P("feat", None),
        P("feat", None),
        P("feat", None),
        P("feat", None),
        P("feat", None),
        P(share, "feat", None, None),
        P(share, "feat", None, None),
        P(share, "feat", None),
        P(share, "feat", None, None),
        P(whole, None),
        P(whole, None, None),
    )
    return jax.shard_map(
        functools.partial(local, mesh.shape["dom"], mesh.shape["feat"]),
        mesh=mesh, in_specs=in_specs, out_specs=P(None, whole), check_vma=False,
    )
```

time: 190 us -> 85.1 us (0.45)
  the two profiles are of different devices: /device:TPU:0 before, /device:TPU:9 now
where the time goes in v1:
time: 85.1 us; the launch traced here: 84.9 us
  waiting for transfers between devices  49.4 us (58%)
  Pallas kernels  19.2 us (23%)
  starting transfers between devices  12 us (14%)
  local copies, waits for them, and re-layouts  2.82 us (3%)
  other arithmetic  1.22 us (1%)
    ppermute x6, waiting for transfers between devices, move(): lax.ppermute(chunks[k], 'dom', [(i, (i + k) % n_dom) for i in range(n_dom)])  26.5 us
    ppermute x4, waiting for transfers between devices, whole(): lax.ppermute(jnp.concatenate(group, axis=0), 'feat', SWAP)  11.1 us
    ppermute x1, waiting for transfers between devices, local(): other = lax.ppermute(gb, 'feat', SWAP)  10.5 us
    ppermute x6, starting transfers between devices, move(): lax.ppermute(chunks[k], 'dom', [(i, (i + k) % n_dom) for i in range(n_dom)])  6.66 us
    pallas_call x1, Pallas kernels, local(): call(functools.partial(decode_kernel, n_dom, cols), out_shape=jax.ShapeDt...  6.23 us
    pallas_call x1, Pallas kernels, local(): call(functools.partial(spread_kernel, n_dom, feeding), grid=(grid_blocks...  3.24 us
    ppermute x4, starting transfers between devices, whole(): lax.ppermute(jnp.concatenate(group, axis=0), 'feat', SWAP)  3 us
    unnamed x28, local copies, waits for them, and re-layouts  2.82 us
  transfers between devices with their start and end apart: 13, of which 10 were waited for; matrix products, arithmetic and copies ran while one was open for 0% of the time, Pallas kernels for 13%

profile of v1, /device:TPU:9, one launch (start us, length us, event | category | flops | bytes accessed | tf_op | source)
XLA Modules:
  0.0 84.9 jit_solution(7778181081238948336)
XLA Ops:
  0.0 1.1 %pad_maximum_fusion = bf16[512,512]{1,0:T(8,128)(2,1)S(1)} fusion(bf16[256,512]{1,0:T(8,128)(2,1)} %refs_2_.1, bf16[256,512]{1,0:T(8,128)(2,1)} %refs_1_.2), kind=kLoop, calls=%fused_computation | loop fusion | flops 1048576 | bytes 1048576 | tf_op jit(solution)/shard_map/concatenate | solution.py:236
  1.2 1.3 %collective-permute-start.1 = (bf16[512,512]{1,0:T(8,128)(2,1)S(1)}, bf16[512,512]{1,0:T(8,128)(2,1)S(1)}, u32[]{:S(2)}, u32[]{:S(2)}) collective-permute-start(bf16[512,512]{1,0:T(8,128)(2,1)S(1)} %pad_maximum_fusion), channel_id=1, source_target_pairs={{0,2},{2,0},{1,3},{3,1},{4,6},{6,4},{5,7},{7,5},{8,10},{10,8},{9,1... | collective-permute-start | bytes 1572872 | tf_op jit(solution)/shard_map/ppermute | solution.py:236
  2.4 0.3 collective-permute-start
  2.7 0.1 pad_add_fusion.at_ref
  2.8 1.4 %copy-done = bf16[512,1536]{1,0:T(8,128)(2,1)S(1)} copy-done((bf16[512,1536]{1,0:T(8,128)(2,1)S(1)}, bf16[512,1536]{1,0:T(8,128)(2,1)}, u32[]{:S(2)}) %copy-start) | copy-done | bytes 1572888
  4.2 0.7 copy-done.11
  4.9 1.7 %pack.1 = (bf16[2,512,128]{2,1,0:T(8,128)(2,1)S(1)}, bf16[2,512,128]{2,1,0:T(8,128)(2,1)S(1)}, bf16[2,512,128]{2,1,0:T(8,128)(2,1)S(1)}, bf16[2,512,128]{2,1,0:T(8,128)(2,1)S(1)}) custom-call(s32[3]{0:T(128)S(1)} %pad_add_fusion.at_ref, s32[2,8]{1,0:T(2,128)S(1)} %bitcast.14, bf16[512,1536]{1,0:T(8,128)(2,1)S(1)} %copy-done), custom_call_target="tpu_custom_call" | custom-call | flops 400000000 | bytes 1000000 | tf_op jit(solution)/shard_map/pack/pallas_call | solution.py:220
  6.6 1.3 %collective-permute-start.2 = (bf16[2,512,128]{2,1,0:T(8,128)(2,1)S(1)}, bf16[2,512,128]{2,1,0:T(8,128)(2,1)S(1)}, u32[]{:S(2)}, u32[]{:S(2)}) collective-permute-start(bf16[2,512,128]{2,1,0:T(8,128)(2,1)S(1)} %get-tuple-element.22), channel_id=1, source_target_pairs={{0,4},{4,8},{8,12},{12,0},{1,5},{5,9},{9,13},{13,1},{2,6},{6,10},{... | collective-permute-start | bytes 786440 | tf_op jit(solution)/shard_map/ppermute | solution.py:198
  7.9 1.1 %collective-permute-start.3 = (bf16[2,512,128]{2,1,0:T(8,128)(2,1)S(1)}, bf16[2,512,128]{2,1,0:T(8,128)(2,1)S(1)}, u32[]{:S(2)}, u32[]{:S(2)}) collective-permute-start(bf16[2,512,128]{2,1,0:T(8,128)(2,1)S(1)} %get-tuple-element.23), channel_id=1, source_target_pairs={{0,8},{4,12},{8,0},{12,4},{1,9},{5,13},{9,1},{13,5},{2,10},{6,14},... | collective-permute-start | bytes 786440 | tf_op jit(solution)/shard_map/ppermute | solution.py:198
  9.0 1.4 %collective-permute-start.4 = (bf16[2,512,128]{2,1,0:T(8,128)(2,1)S(1)}, bf16[2,512,128]{2,1,0:T(8,128)(2,1)S(1)}, u32[]{:S(2)}, u32[]{:S(2)}) collective-permute-start(bf16[2,512,128]{2,1,0:T(8,128)(2,1)S(1)} %get-tuple-element.24), channel_id=1, source_target_pairs={{0,12},{4,0},{8,4},{12,8},{1,13},{5,1},{9,5},{13,9},{2,14},{6,2},{... | collective-permute-start | bytes 786440 | tf_op jit(solution)/shard_map/ppermute | solution.py:198
  10.4 0.7 copy-done.10
  11.1 3.2 %spread.1.refs_2_.wide_ref = bf16[1024,1536]{1,0:T(8,128)(2,1)S(1)} custom-call(s32[3]{0:T(128)S(1)} %pad_add_fusion.at_ref, s32[4,24]{1,0:T(4,128)S(1)} %bitcast.13, bf16[24,64,256]{2,1,0:T(8,128)(2,1)S(1)} %copy-done.4), custom_call_target="tpu_custom_call" | custom-call | tf_op jit(solution)/shard_map/spread/pallas_call | solution.py:267
  14.3 0.9 %scatter.1.wide_ref.refs_1_ = bf16[2,512,512]{2,1,0:T(8,128)(2,1)S(1)} custom-call(s32[3]{0:T(128)S(1)} %pad_add_fusion.at_ref, s32[16]{0:T(128)S(1)} %bitcast.16, bf16[64,1024]{1,0:T(8,128)(2,1)S(1)} %bitcast.12), custom_call_target="tpu_custom_call" | custom-call | tf_op jit(solution)/shard_map/scatter/pallas_call | solution.py:259
  15.2 4.4 %collective-permute-done.refs_3_ = bf16[256,512]{1,0:T(8,128)(2,1)S(1)} collective-permute-done((bf16[256,512]{1,0:T(8,128)(2,1)}, bf16[256,512]{1,0:T(8,128)(2,1)S(1)}, u32[]{:S(2)}, u32[]{:S(2)}) %collective-permute-start) | collective-permute-done | bytes 262176 | tf_op jit(solution)/shard_map/ppermute | solution.py:236
  19.6 0.0 collective-permute-done.1.refs_4_
  19.6 0.0 copy-done.3
  19.6 0.0 copy-done.6
  19.7 1.0 %assemble.2 = (bf16[512,512]{1,0:T(8,128)(2,1)S(1)}, bf16[512,512]{1,0:T(8,128)(2,1)S(1)}, bf16[512,512]{1,0:T(8,128)(2,1)S(1)}) custom-call(s32[3]{0:T(128)S(1)} %pad_add_fusion.at_ref, bf16[256,512]{1,0:T(8,128)(2,1)S(1)} %copy-done.6, bf16[256,512]{1,0:T(8,128)(2,1)S(1)} %copy-done.2, bf16[256,512]{1,0:T(8,128)(2,1)S(1)} %copy-done.3, ...), custom_call_target="tpu_custom_call" | custom-call | tf_op jit(solution)/shard_map/assemble/pallas_call | solution.py:238
  20.7 0.0 collective-permute-done.2.rest_1_.refs_4_
  20.7 8.4 %collective-permute-done.3.rest_2_.refs_5_ = bf16[2,512,128]{2,1,0:T(8,128)(2,1)S(1)} collective-permute-done((bf16[2,512,128]{2,1,0:T(8,128)(2,1)S(1)}, bf16[2,512,128]{2,1,0:T(8,128)(2,1)S(1)}, u32[]{:S(2)}, u32[]{:S(2)}) %collective-permute-start.3) | collective-permute-done | bytes 262176 | tf_op jit(solution)/shard_map/ppermute | solution.py:198
  29.1 3.5 %collective-permute-done.4.rest_3_.refs_6_ = bf16[2,512,128]{2,1,0:T(8,128)(2,1)S(1)} collective-permute-done((bf16[2,512,128]{2,1,0:T(8,128)(2,1)S(1)}, bf16[2,512,128]{2,1,0:T(8,128)(2,1)S(1)}, u32[]{:S(2)}, u32[]{:S(2)}) %collective-permute-start.4) | collective-permute-done | bytes 262176 | tf_op jit(solution)/shard_map/ppermute | solution.py:198
  32.6 0.0 copy-start.5
  32.6 0.0 copy-start.7
  32.7 0.0 copy-start.8
  32.7 0.0 copy-start.12
  32.7 0.6 collective-permute-start.5
  33.2 0.8 encode.1.acc_ref
  34.0 0.8 collective-permute-done.5.far_ref
  34.8 1.8 %gather.1 = (f32[512,512]{1,0:T(8,128)S(1)}, bf16[512,512]{1,0:T(8,128)(2,1)S(1)}) custom-call(s32[3]{0:T(128)S(1)} %pad_add_fusion.at_ref, f32[512,512]{1,0:T(8,128)S(1)} %encode.1.acc_ref, bf16[512,512]{1,0:T(8,128)(2,1)S(1)} %get-tuple-element.20.w1t_ref.refs_0_, bf16[512,512]{1,0:T(8,128)(2,1)S(1)} %get-tuple-element.25.w2t_ref, ...), custom_call_target="tpu_custom_call" | custom-call | flops 200000000 | bytes 500000 | tf_op jit(solution)/shard_map/gather/pallas_call | solution.py:286
  36.5 1.3 %collective-permute-start.6 = (bf16[512,512]{1,0:T(8,128)(2,1)S(1)}, bf16[512,512]{1,0:T(8,128)(2,1)S(1)}, u32[]{:S(2)}, u32[]{:S(2)}) collective-permute-start(bf16[512,512]{1,0:T(8,128)(2,1)S(1)} %get-tuple-element.27), channel_id=1, source_target_pairs={{0,2},{2,0},{1,3},{3,1},{4,6},{6,4},{5,7},{7,5},{8,10},{10,8},{9,1... | collective-permute-start | bytes 1572872 | tf_op jit(solution)/shard_map/ppermute | solution.py:295
  37.8 0.3 collective-permute-start.10
  38.1 1.2 %collective-permute-start.11 = (bf16[256,512]{1,0:T(8,128)(2,1)S(1)}, bf16[256,512]{1,0:T(8,128)(2,1)S(1)}, u32[]{:S(2)}, u32[]{:S(2)}) collective-permute-start(bf16[256,512]{1,0:T(8,128)(2,1)S(1)} %copy-done.8), channel_id=1, source_target_pairs={{0,2},{2,0},{1,3},{3,1},{4,6},{6,4},{5,7},{7,5},{8,10},{10,8},{9,1... | collective-permute-start | bytes 786440 | tf_op jit(solution)/shard_map/ppermute | solution.py:236
  39.3 10.5 %collective-permute-done.6.other_ref = bf16[512,512]{1,0:T(8,128)(2,1)S(1)} collective-permute-done((bf16[512,512]{1,0:T(8,128)(2,1)S(1)}, bf16[512,512]{1,0:T(8,128)(2,1)S(1)}, u32[]{:S(2)}, u32[]{:S(2)}) %collective-permute-start.6) | collective-permute-done | bytes 524320 | tf_op jit(solution)/shard_map/ppermute | solution.py:295
  49.7 1.7 %mesh.1 = (bf16[2,512,128]{2,1,0:T(8,128)(2,1)S(1)}, bf16[2,512,128]{2,1,0:T(8,128)(2,1)S(1)}, bf16[2,512,128]{2,1,0:T(8,128)(2,1)S(1)}, bf16[2,512,128]{2,1,0:T(8,128)(2,1)S(1)}) custom-call(s32[3]{0:T(128)S(1)} %pad_add_fusion.at_ref, s32[2,8]{1,0:T(2,128)S(1)} %bitcast.15, f32[512,512]{1,0:T(8,128)S(1)} %get-tuple-element.26.g_ref, ...), custom_call_target="tpu_custom_call" | custom-call | flops 400000000 | bytes 1000000 | tf_op jit(solution)/shard_map/mesh/pallas_call | solution.py:298
  51.5 0.1 collective-permute-start.7
  51.6 1.4 %collective-permute-start.8 = (bf16[2,512,128]{2,1,0:T(8,128)(2,1)S(1)}, bf16[2,512,128]{2,1,0:T(8,128)(2,1)S(1)}, u32[]{:S(2)}, u32[]{:S(2)}) collective-permute-start(bf16[2,512,128]{2,1,0:T(8,128)(2,1)S(1)} %get-tuple-element.31), channel_id=1, source_target_pairs={{0,8},{4,12},{8,0},{12,4},{1,9},{5,13},{9,1},{13,5},{2,10},{6,14},... | collective-permute-start | bytes 786440 | tf_op jit(solution)/shard_map/ppermute | solution.py:198
  53.0 1.4 %collective-permute-start.9 = (bf16[2,512,128]{2,1,0:T(8,128)(2,1)S(1)}, bf16[2,512,128]{2,1,0:T(8,128)(2,1)S(1)}, u32[]{:S(2)}, u32[]{:S(2)}) collective-permute-start(bf16[2,512,128]{2,1,0:T(8,128)(2,1)S(1)} %get-tuple-element.32), channel_id=1, source_target_pairs={{0,12},{4,0},{8,4},{12,8},{1,13},{5,1},{9,5},{13,9},{2,14},{6,2},{... | collective-permute-start | bytes 786440 | tf_op jit(solution)/shard_map/ppermute | solution.py:198
  54.3 1.0 %collective-permute-done.10.refs_2_ = bf16[256,512]{1,0:T(8,128)(2,1)S(1)} collective-permute-done((bf16[256,512]{1,0:T(8,128)(2,1)S(1)}, bf16[256,512]{1,0:T(8,128)(2,1)S(1)}, u32[]{:S(2)}, u32[]{:S(2)}) %collective-permute-start.10) | collective-permute-done | bytes 262176 | tf_op jit(solution)/shard_map/ppermute | solution.py:236
  55.4 5.6 %collective-permute-done.11.refs_3_ = bf16[256,512]{1,0:T(8,128)(2,1)S(1)} collective-permute-done((bf16[256,512]{1,0:T(8,128)(2,1)S(1)}, bf16[256,512]{1,0:T(8,128)(2,1)S(1)}, u32[]{:S(2)}, u32[]{:S(2)}) %collective-permute-start.11) | collective-permute-done | bytes 262176 | tf_op jit(solution)/shard_map/ppermute | solution.py:236
  61.0 0.9 %assemble.3 = (bf16[512,512]{1,0:T(8,128)(2,1)S(1)}, bf16[512,512]{1,0:T(8,128)(2,1)S(1)}) custom-call(s32[3]{0:T(128)S(1)} %pad_add_fusion.at_ref, bf16[256,512]{1,0:T(8,128)(2,1)S(1)} %copy-done.7, bf16[256,512]{1,0:T(8,128)(2,1)S(1)} %copy-done.8, bf16[256,512]{1,0:T(8,128)(2,1)S(1)} %collective-permute-done.10.refs_2_, ...), custom_call_target="tpu_custom_call" | custom-call | tf_op jit(solution)/shard_map/assemble/pallas_call | solution.py:238
  61.9 0.0 collective-permute-done.7.rest_1_.refs_2_
  61.9 10.4 %collective-permute-done.8.rest_2_.refs_3_ = bf16[2,512,128]{2,1,0:T(8,128)(2,1)S(1)} collective-permute-done((bf16[2,512,128]{2,1,0:T(8,128)(2,1)S(1)}, bf16[2,512,128]{2,1,0:T(8,128)(2,1)S(1)}, u32[]{:S(2)}, u32[]{:S(2)}) %collective-permute-start.8) | collective-permute-done | bytes 262176 | tf_op jit(solution)/shard_map/ppermute | solution.py:198
  72.3 4.2 %collective-permute-done.9.rest_3_.refs_4_ = bf16[2,512,128]{2,1,0:T(8,128)(2,1)S(1)} collective-permute-done((bf16[2,512,128]{2,1,0:T(8,128)(2,1)S(1)}, bf16[2,512,128]{2,1,0:T(8,128)(2,1)S(1)}, u32[]{:S(2)}, u32[]{:S(2)}) %collective-permute-start.9) | collective-permute-done | bytes 262176 | tf_op jit(solution)/shard_map/ppermute | solution.py:198
  76.6 0.0 copy-start.1
  76.6 0.6 collective-permute-start.12
  77.1 1.0 %collect.1.acc_ref = f32[512,1536]{1,0:T(8,128)S(1)} custom-call(bf16[1024,1536]{1,0:T(8,128)(2,1)S(1)} %spread.1.refs_2_.wide_ref, bf16[2,512,128]{2,1,0:T(8,128)(2,1)S(1)} %get-tuple-element.29.rest_0_.refs_1_, bf16[2,512,128]{2,1,0:T(8,128)(2,1)S(1)} %collective-permute-done.7.rest_1_.refs_2_, ...), custom_call_target="tpu_custom_call" | custom-call | flops 400000000 | bytes 1000000 | tf_op jit(solution)/shard_map/collect/pallas_call | solution.py:312
  78.1 0.6 collective-permute-done.12.far_ref
  78.7 6.2 %decode.1 = bf16[512,1536]{1,0:T(8,128)(2,1)} custom-call(f32[512,1536]{1,0:T(8,128)S(1)} %collect.1.acc_ref, bf16[1024,1536]{1,0:T(8,128)(2,1)S(1)} %spread.1.refs_2_.wide_ref, bf16[512,512]{1,0:T(8,128)(2,1)S(1)} %get-tuple-element.33.refs_0_.d1t_ref, bf16[512,512]{1,0:T(8,128)(2,1)S(1)} %get-tuple-element.34.d2t_ref, bf16[512,1536]{1,0:T(8,128)(2,1)S(1)} %copy-done.1, ...), custom_call_target="tpu_custom_call" | custom-call | flops 1200000000 | bytes 3000000 | tf_op jit(solution)/shard_map/decode/pallas_call | solution.py:320
  (20 shorter events, 0.1 us)
Async XLA Ops:
  0.0 10.4 %copy-start.4 = (bf16[24,64,256]{2,1,0:T(8,128)(2,1)S(1)}, bf16[24,64,256]{2,1,0:T(8,128)(2,1)}, u32[]{:S(2)}) copy-start(bf16[24,64,256]{2,1,0:T(8,128)(2,1)} %tiles_ref.1) | copy-start | bytes 2359300
  0.0 14.3 %copy-start.13 = (s32[1,1,16]{2,1,0:T(1,128)S(1)}, s32[1,1,16]{2,1,0:T(1,128)}, u32[]{:S(2)}) copy-start(s32[1,1,16]{2,1,0:T(1,128)} %param.22) | copy-start | bytes 196
  0.0 14.3 %copy-start.9 = (bf16[1,1,64,1024]{3,2,1,0:T(8,128)(2,1)S(1)}, bf16[1,1,64,1024]{3,2,1,0:T(8,128)(2,1)}, u32[]{:S(2)}) copy-start(bf16[1,1,64,1024]{3,2,1,0:T(8,128)(2,1)} %param.21) | copy-start | bytes 393220
  1.2 18.5 %collective-permute-start.1 = (bf16[512,512]{1,0:T(8,128)(2,1)S(1)}, bf16[512,512]{1,0:T(8,128)(2,1)S(1)}, u32[]{:S(2)}, u32[]{:S(2)}) collective-permute-start(bf16[512,512]{1,0:T(8,128)(2,1)S(1)} %pad_maximum_fusion), channel_id=1, source_target_pairs={{0,2},{2,0},{1,3},{3,1},{4,6},{6,4},{5,7},{7,5},{8,10},{10,8},{9,1... | collective-permute-start | bytes 1572872 | tf_op jit(solution)/shard_map/ppermute | solution.py:236
  2.4 17.2 %collective-permute-start = (bf16[256,512]{1,0:T(8,128)(2,1)}, bf16[256,512]{1,0:T(8,128)(2,1)S(1)}, u32[]{:S(2)}, u32[]{:S(2)}) collective-permute-start(bf16[256,512]{1,0:T(8,128)(2,1)} %refs_0_.2), channel_id=1, source_target_pairs={{0,2},{2,0},{1,3},{3,1},{4,6},{6,4},{5,7},{7,5},{8,10},{10,8},{9,1... | collective-permute-start | bytes 786440 | tf_op jit(solution)/shard_map/ppermute | solution.py:236
  2.8 1.4 %copy-start = (bf16[512,1536]{1,0:T(8,128)(2,1)S(1)}, bf16[512,1536]{1,0:T(8,128)(2,1)}, u32[]{:S(2)}) copy-start(bf16[512,1536]{1,0:T(8,128)(2,1)} %grid_ref.1) | copy-start | bytes 4718596
  4.2 0.7 copy-start.11
  4.9 14.8 %copy-start.2 = (bf16[256,512]{1,0:T(8,128)(2,1)S(1)}, bf16[256,512]{1,0:T(8,128)(2,1)}, u32[]{:S(2)}) copy-start(bf16[256,512]{1,0:T(8,128)(2,1)} %refs_1_.2) | copy-start | bytes 786436
  4.9 14.8 %copy-start.3 = (bf16[256,512]{1,0:T(8,128)(2,1)S(1)}, bf16[256,512]{1,0:T(8,128)(2,1)}, u32[]{:S(2)}) copy-start(bf16[256,512]{1,0:T(8,128)(2,1)} %refs_2_.1) | copy-start | bytes 786436
  4.9 14.8 %copy-start.6 = (bf16[256,512]{1,0:T(8,128)(2,1)S(1)}, bf16[256,512]{1,0:T(8,128)(2,1)}, u32[]{:S(2)}) copy-start(bf16[256,512]{1,0:T(8,128)(2,1)} %refs_0_.2) | copy-start | bytes 786436
  6.6 14.1 %collective-permute-start.2 = (bf16[2,512,128]{2,1,0:T(8,128)(2,1)S(1)}, bf16[2,512,128]{2,1,0:T(8,128)(2,1)S(1)}, u32[]{:S(2)}, u32[]{:S(2)}) collective-permute-start(bf16[2,512,128]{2,1,0:T(8,128)(2,1)S(1)} %get-tuple-element.22), channel_id=1, source_target_pairs={{0,4},{4,8},{8,12},{12,0},{1,5},{5,9},{9,13},{13,1},{2,6},{6,10},{... | collective-permute-start | bytes 786440 | tf_op jit(solution)/shard_map/ppermute | solution.py:198
  7.9 21.2 %collective-permute-start.3 = (bf16[2,512,128]{2,1,0:T(8,128)(2,1)S(1)}, bf16[2,512,128]{2,1,0:T(8,128)(2,1)S(1)}, u32[]{:S(2)}, u32[]{:S(2)}) collective-permute-start(bf16[2,512,128]{2,1,0:T(8,128)(2,1)S(1)} %get-tuple-element.23), channel_id=1, source_target_pairs={{0,8},{4,12},{8,0},{12,4},{1,9},{5,13},{9,1},{13,5},{2,10},{6,14},... | collective-permute-start | bytes 786440 | tf_op jit(solution)/shard_map/ppermute | solution.py:198
  9.0 23.6 %collective-permute-start.4 = (bf16[2,512,128]{2,1,0:T(8,128)(2,1)S(1)}, bf16[2,512,128]{2,1,0:T(8,128)(2,1)S(1)}, u32[]{:S(2)}, u32[]{:S(2)}) collective-permute-start(bf16[2,512,128]{2,1,0:T(8,128)(2,1)S(1)} %get-tuple-element.24), channel_id=1, source_target_pairs={{0,12},{4,0},{8,4},{12,8},{1,13},{5,1},{9,5},{13,9},{2,14},{6,2},{... | collective-permute-start | bytes 786440 | tf_op jit(solution)/shard_map/ppermute | solution.py:198
  10.4 0.7 copy-start.10
  32.6 2.1 %copy-start.5 = (bf16[256,512]{1,0:T(8,128)(2,1)S(1)}, bf16[256,512]{1,0:T(8,128)(2,1)}, u32[]{:S(2)}) copy-start(bf16[256,512]{1,0:T(8,128)(2,1)} %ms_ref.1) | copy-start | bytes 786436
  32.6 5.2 %copy-start.7 = (bf16[256,512]{1,0:T(8,128)(2,1)S(1)}, bf16[256,512]{1,0:T(8,128)(2,1)}, u32[]{:S(2)}) copy-start(bf16[256,512]{1,0:T(8,128)(2,1)} %refs_0_.3) | copy-start | bytes 786436
  32.7 5.5 %copy-start.8 = (bf16[256,512]{1,0:T(8,128)(2,1)S(1)}, bf16[256,512]{1,0:T(8,128)(2,1)}, u32[]{:S(2)}) copy-start(bf16[256,512]{1,0:T(8,128)(2,1)} %refs_1_.3) | copy-start | bytes 786436
  32.7 17.1 %copy-start.12 = (s32[1,1,8,2]{2,3,1,0:T(2,128)S(1)}, s32[1,1,8,2]{2,3,1,0:T(2,128)}, u32[]{:S(2)}) copy-start(s32[1,1,8,2]{2,3,1,0:T(2,128)} %param.23) | copy-start | bytes 196
  32.7 2.1 %collective-permute-start.5 = (bf16[4,512,128]{2,1,0:T(8,128)(2,1)S(1)}, bf16[4,512,128]{2,1,0:T(8,128)(2,1)S(1)}, u32[]{:S(2)}, u32[]{:S(2)}) collective-permute-start(bf16[4,512,128]{2,1,0:T(8,128)(2,1)S(1)} %stack.18), channel_id=1, source_target_pairs={{0,1},{1,0},{2,3},{3,2},{4,5},{5,4},{6,7},{7,6},{8,9},{9,8},{10,11... | collective-permute-start | bytes 1572872 | tf_op jit(solution)/shard_map/ppermute | solution.py:256
  36.5 13.2 %collective-permute-start.6 = (bf16[512,512]{1,0:T(8,128)(2,1)S(1)}, bf16[512,512]{1,0:T(8,128)(2,1)S(1)}, u32[]{:S(2)}, u32[]{:S(2)}) collective-permute-start(bf16[512,512]{1,0:T(8,128)(2,1)S(1)} %get-tuple-element.27), channel_id=1, source_target_pairs={{0,2},{2,0},{1,3},{3,1},{4,6},{6,4},{5,7},{7,5},{8,10},{10,8},{9,1... | collective-permute-start | bytes 1572872 | tf_op jit(solution)/shard_map/ppermute | solution.py:295
  37.8 17.5 %collective-permute-start.10 = (bf16[256,512]{1,0:T(8,128)(2,1)S(1)}, bf16[256,512]{1,0:T(8,128)(2,1)S(1)}, u32[]{:S(2)}, u32[]{:S(2)}) collective-permute-start(bf16[256,512]{1,0:T(8,128)(2,1)S(1)} %copy-done.7), channel_id=1, source_target_pairs={{0,2},{2,0},{1,3},{3,1},{4,6},{6,4},{5,7},{7,5},{8,10},{10,8},{9,1... | collective-permute-start | bytes 786440 | tf_op jit(solution)/shard_map/ppermute | solution.py:236
  38.1 22.9 %collective-permute-start.11 = (bf16[256,512]{1,0:T(8,128)(2,1)S(1)}, bf16[256,512]{1,0:T(8,128)(2,1)S(1)}, u32[]{:S(2)}, u32[]{:S(2)}) collective-permute-start(bf16[256,512]{1,0:T(8,128)(2,1)S(1)} %copy-done.8), channel_id=1, source_target_pairs={{0,2},{2,0},{1,3},{3,1},{4,6},{6,4},{5,7},{7,5},{8,10},{10,8},{9,1... | collective-permute-start | bytes 786440 | tf_op jit(solution)/shard_map/ppermute | solution.py:236
  51.5 10.4 %collective-permute-start.7 = (bf16[2,512,128]{2,1,0:T(8,128)(2,1)S(1)}, bf16[2,512,128]{2,1,0:T(8,128)(2,1)S(1)}, u32[]{:S(2)}, u32[]{:S(2)}) collective-permute-start(bf16[2,512,128]{2,1,0:T(8,128)(2,1)S(1)} %get-tuple-element.30), channel_id=1, source_target_pairs={{0,4},{4,8},{8,12},{12,0},{1,5},{5,9},{9,13},{13,1},{2,6},{6,10},{... | collective-permute-start | bytes 786440 | tf_op jit(solution)/shard_map/ppermute | solution.py:198
  51.6 20.7 %collective-permute-start.8 = (bf16[2,512,128]{2,1,0:T(8,128)(2,1)S(1)}, bf16[2,512,128]{2,1,0:T(8,128)(2,1)S(1)}, u32[]{:S(2)}, u32[]{:S(2)}) collective-permute-start(bf16[2,512,128]{2,1,0:T(8,128)(2,1)S(1)} %get-tuple-element.31), channel_id=1, source_target_pairs={{0,8},{4,12},{8,0},{12,4},{1,9},{5,13},{9,1},{13,5},{2,10},{6,14},... | collective-permute-start | bytes 786440 | tf_op jit(solution)/shard_map/ppermute | solution.py:198
  53.0 23.6 %collective-permute-start.9 = (bf16[2,512,128]{2,1,0:T(8,128)(2,1)S(1)}, bf16[2,512,128]{2,1,0:T(8,128)(2,1)S(1)}, u32[]{:S(2)}, u32[]{:S(2)}) collective-permute-start(bf16[2,512,128]{2,1,0:T(8,128)(2,1)S(1)} %get-tuple-element.32), channel_id=1, source_target_pairs={{0,12},{4,0},{8,4},{12,8},{1,13},{5,1},{9,5},{13,9},{2,14},{6,2},{... | collective-permute-start | bytes 786440 | tf_op jit(solution)/shard_map/ppermute | solution.py:198
  76.6 2.1 %copy-start.1 = (bf16[512,1536]{1,0:T(8,128)(2,1)S(1)}, bf16[512,1536]{1,0:T(8,128)(2,1)}, u32[]{:S(2)}) copy-start(bf16[512,1536]{1,0:T(8,128)(2,1)} %grid_ref.1) | copy-start | bytes 4718596
  76.6 2.1 %collective-permute-start.12 = (bf16[4,512,128]{2,1,0:T(8,128)(2,1)S(1)}, bf16[4,512,128]{2,1,0:T(8,128)(2,1)S(1)}, u32[]{:S(2)}, u32[]{:S(2)}) collective-permute-start(bf16[4,512,128]{2,1,0:T(8,128)(2,1)S(1)} %stack.19), channel_id=1, source_target_pairs={{0,1},{1,0},{2,3},{3,2},{4,5},{5,4},{6,7},{7,6},{8,9},{9,8},{10,11... | collective-permute-start | bytes 1572872 | tf_op jit(solution)/shard_map/ppermute | solution.py:256

commit v2 on v1

v2 whole, which is shorter than its diff:
```python
import functools

import jax
import jax.numpy as jnp
from jax import lax
from jax.experimental import pallas as pl
from jax.experimental.pallas import tpu as pltpu
from jax.sharding import PartitionSpec as P

BF = jnp.bfloat16
F32 = jnp.float32
VMEM = pltpu.VMEM
SMEM = pltpu.SMEM
SWAP = [(0, 1), (1, 0)]


def full(space=VMEM):
    return pl.BlockSpec(memory_space=space)


def params(mib):
    return pltpu.CompilerParams(vmem_limit_bytes=int(mib * 1024 * 1024))


def cost(us):
    return pl.CostEstimate(flops=int(us * 4e8), bytes_accessed=int(us * 1e6), transcendentals=0)


def anywhere():
    return pl.BlockSpec(memory_space=pl.ANY)


def outside():
    return pl.BlockSpec(memory_space=pltpu.HBM)


def silu(x):
    half = 0.5 * x
    return half + half * jnp.tanh(half)


def mm(a, b):
    return jnp.dot(a, b, preferred_element_type=F32)


def mt(w, x):
    return lax.dot_general(w, x, (((0,), (0,)), ((), ())), preferred_element_type=F32)


def turn(v):
    return v.astype(F32).T.astype(BF)


def swap_halves(v, width):
    return jnp.concatenate([v[:, width:], v[:, :width]], axis=1)


def pack_rows(step, blocks, n_dom, at_ref, send_ref, buf, i, outs):
    pair = outs[0].shape[2]
    width = pair // 2
    cols = blocks * width
    here = slice(i * step, (i + 1) * step)
    for p in range(blocks // 2):
        v = buf[0, here, p * pair:(p + 1) * pair]
        buf[1, here, p * pair:(p + 1) * pair] = swap_halves(v, width)
    low = lax.broadcasted_iota(jnp.int32, (step, pair), 1) < width
    for k in range(n_dom):
        for j in range(2):
            peer = (at_ref[0] ^ k) * 2 + (at_ref[2] ^ j)
            vs = []
            for c in range(2):
                b = send_ref[c, peer]
                used = b < blocks
                start = pl.multiple_of(jnp.where(used, b // 2 * pair, cols), pair)
                flip = jnp.where(used & (lax.rem(b, 2) != c), 1, 0)
                vs.append(buf[flip, here, pl.ds(start, pair)])
            outs[k][j, here, :] = jnp.where(low, vs[0], vs[1])


def pack_kernel(blocks, n_dom, at_ref, send_ref, src_ref, *refs):
    outs, buf, sems = refs[:n_dom], refs[n_dom], refs[n_dom + 1]
    rows, cols = src_ref.shape
    parts = 4
    step = rows // parts
    copies = []
    for i in range(parts):
        here = pl.ds(i * step, step)
        copies.append(pltpu.make_async_copy(src_ref.at[here, :], buf.at[0, here, pl.ds(0, cols)], sems.at[i]))
        copies[-1].start()
    buf[0, :, cols:] = jnp.zeros((rows, buf.shape[2] - cols), BF)
    for i in range(parts):
        copies[i].wait()
        pack_rows(step, blocks, n_dom, at_ref, send_ref, buf, i, outs)


def stack_kernel(n_dom, waits, *refs):
    chunks, out = refs[waits:waits + n_dom], refs[waits + n_dom]
    for i, k in enumerate(order_of(n_dom)):
        out[k] = chunks[i][1]


def joined(at_ref, refs):
    if len(refs) == 1:
        return refs[0][...]
    own, got = refs[0][...], refs[1][...]
    first = at_ref[1] == 0
    return jnp.concatenate([jnp.where(first, own, got), jnp.where(first, got, own)], axis=0)


def scatter_kernel(n_dom, mesh_blocks, at_ref, tgt_ref, tiles_ref, ms_ref, out_ref, split_ref):
    block = tiles_ref.shape[0]
    pair, part = 2 * block, block // 2
    wide = mesh_blocks * part
    group = lax.broadcasted_iota(jnp.int32, (1, pair), 1) // part
    for j in range(2):
        for k in range(n_dom):
            peer = (at_ref[0] ^ k) * 2 + (at_ref[2] ^ j)
            t = turn(tiles_ref[:, pl.ds(pl.multiple_of(peer * pair, pair), pair)])
            for h in range(2):
                spread = jnp.concatenate([t[:, h * part:(h + 1) * part]] * 4, axis=1)
                for c in range(2):
                    m = tgt_ref[peer * 2 + c]
                    row = k * pair + c * block
                    for p in range(mesh_blocks // 4):
                        mask = (group + 4 * p == m).astype(F32).astype(BF)
                        at = h * wide + p * pair
                        out_ref[j, row:row + block, at:at + pair] = spread[c * block:(c + 1) * block] * mask
    ms = ms_ref[...]
    for h in range(2):
        for p in range(mesh_blocks // 4):
            split_ref[:, h * wide + p * pair:h * wide + (p + 1) * pair] = jnp.concatenate(
                [ms[:, m * block + h * part:m * block + (h + 1) * part] for m in range(4 * p, 4 * p + 4)], axis=1
            )


def spread_kernel(n_dom, feeding, at_ref, slot_ref, tiles_ref, out_ref):
    g = pl.program_id(0)
    block = tiles_ref.shape[1]
    t = turn(tiles_ref[...].reshape(2 * block, feeding * block))
    half = block // 2
    low = lax.broadcasted_iota(jnp.int32, (half, 2 * block), 1) < block
    out_ref[...] = jnp.zeros_like(out_ref)
    for h in range(2):
        for i in range(feeding):
            q = slot_ref[i, g * 2 + h]
            peer = q // 2
            k = at_ref[0] ^ (peer // 2)
            j = at_ref[2] ^ lax.rem(peer, 2)
            for part in range(2):
                row = part * (out_ref.shape[0] // 2) + ((k * 2 + j) * 2 + lax.rem(q, 2)) * half
                v = t[i * block + part * half:i * block + (part + 1) * half, :]
                v = jnp.where(low if h == 0 else ~low, v, jnp.zeros_like(v))
                out_ref[pl.ds(pl.multiple_of(row, half), half), :] += v


def encode_kernel(n_dom, at_ref, wide_ref, *rest):
    chunks, ws, out_ref = rest[:n_dom], rest[n_dom:-1], rest[-1]
    place = order_of(n_dom).index
    x = jnp.concatenate([chunks[place(k)][0] for k in range(n_dom)], axis=1)
    hid = silu(mt(joined(at_ref, ws), x)).astype(BF)
    out_ref[...] = mm(hid, wide_ref[0])


def gather_kernel(n_dom, at_ref, acc_ref, wide_ref, ms_ref, far_ref, *rest):
    ws, (g_ref, first_ref, second_ref) = rest[:-3], rest[-3:]
    count = len(ws) // 2
    x = jnp.concatenate([far_ref[k] for k in range(n_dom)], axis=1)
    hid = silu(mt(joined(at_ref, ws[:count]), x)).astype(BF)
    acc = acc_ref[...] + mm(hid, wide_ref[1])
    g_ref[...] = mt(joined(at_ref, ws[count:]), acc.astype(BF))
    rows = ms_ref.shape[0]
    here = pl.ds(pl.multiple_of(at_ref[1] * rows, rows), rows)
    g_ref[here, :] += ms_ref[...].astype(F32)
    half = g_ref.shape[1] // 2
    first_ref[...] = g_ref[:, :half].astype(BF)
    second_ref[...] = g_ref[:, half:].astype(BF)


def mesh_kernel(blocks, n_dom, h, at_ref, send_ref, g_ref, other_ref, mw_ref, *rest):
    outs, buf = rest[-1 - n_dom:-1], rest[-1]
    rows = g_ref.shape[0]
    cols = g_ref.shape[1] // 2
    new = (g_ref[:, h * cols:(h + 1) * cols] + other_ref[...].astype(F32)).astype(BF)
    hid = silu(mt(mw_ref[...], new)).astype(BF)
    part = cols // blocks
    for p in range(cols // 128):
        v = hid[:, p * 128:(p + 1) * 128]
        buf[0, :, p * 128:(p + 1) * 128] = v
        for turned in range(1, 4):
            cut = 128 - turned * part
            buf[turned, :, p * 128:(p + 1) * 128] = jnp.concatenate([v[:, cut:], v[:, :cut]], axis=1)
    buf[0, :, cols:] = jnp.zeros((rows, 128), BF)
    step = rows // 4
    group = lax.broadcasted_iota(jnp.int32, (step, 128), 1) // part
    for k in range(n_dom):
        picks = []
        for i in range(4):
            b = send_ref[i % 2, (at_ref[0] ^ k) * 2 + (at_ref[2] ^ (i // 2))]
            used = b < blocks
            start = pl.multiple_of(jnp.where(used, b // 4 * 128, cols), 128)
            picks.append((jnp.where(used, lax.rem(i + 4 - lax.rem(b, 4), 4), 0), start))
        for r in range(4):
            here = slice(r * step, (r + 1) * step)
            vs = [buf[turned, here, pl.ds(start, 128)] for turned, start in picks]
            outs[k][here, :] = jnp.where(
                group < 2, jnp.where(group == 0, vs[0], vs[1]), jnp.where(group == 2, vs[2], vs[3])
            )


def first_mesh_kernel(blocks, n_dom, at_ref, send_ref, g_ref, other_ref, mw_ref, later_ref, *rest):
    outs, later_out, buf = rest[:n_dom], rest[n_dom], rest[n_dom + 1]
    mesh_kernel(blocks, n_dom, 0, at_ref, send_ref, g_ref, other_ref, mw_ref, *outs, buf)
    later_out[...] = later_ref[...]


def hold_kernel(ready_ref, x_ref, out_ref):
    out_ref[...] = x_ref[...]


def join_kernel(n_dom, waits, *refs):
    chunks, out = refs[waits:waits + n_dom], refs[waits + n_dom]
    for i, k in enumerate(order_of(n_dom)):
        out[k] = chunks[i][...]


def pool_of(n_dom, near, far_ref):
    place = order_of(n_dom).index
    low = lax.broadcasted_iota(jnp.int32, far_ref.shape[1:], 1) < far_ref.shape[2] // 2
    return jnp.concatenate([jnp.where(low, near[place(k)][...], far_ref[k]) for k in range(n_dom)], axis=1)


def collect_kernel(n_dom, ready_ref, wide_ref, far_ref, *rest):
    chunks, out_ref = rest[:n_dom], rest[n_dom]
    pool = pool_of(n_dom, chunks, far_ref)
    out_ref[...] = mm(pool, wide_ref[:pool.shape[1], :])


def decode_kernel(n_dom, cols, acc_ref, wide_ref, d1_ref, d2_ref, grid_ref, far_ref, *rest):
    chunks, (out_ref, buf, sems) = rest[:n_dom], rest[n_dom:]
    pool = pool_of(n_dom, chunks, far_ref)
    got = (acc_ref[...] + mm(pool, wide_ref[pool.shape[1]:, :])).astype(BF)
    dec = silu(mt(d1_ref[...], got)).astype(BF)
    copies = []
    for t in range(grid_ref.shape[1] // cols):
        here = slice(t * cols, (t + 1) * cols)
        buf[:, here] = (grid_ref[:, here].astype(F32) + mt(d2_ref[...], dec[:, here])).astype(BF)
        copies.append(pltpu.make_async_copy(
            buf.at[:, pl.ds(t * cols, cols)], out_ref.at[:, pl.ds(t * cols, cols)], sems.at[t]
        ))
        copies[t].start()
    for copy in copies:
        copy.wait()


def order_of(n_dom):
    return [0] + list(range(n_dom // 2, n_dom)) + list(range(1, n_dom // 2))


def move(chunks, n_dom):
    moved = {0: chunks[0]}
    for k in order_of(n_dom)[1:]:
        moved[k] = lax.ppermute(chunks[k], "dom", [(i, i ^ k) for i in range(n_dom)])
    return [moved[k] for k in range(n_dom)]


def local(n_dom, n_feat, grid_state, mesh_state, enc_first, enc_second, dec_first, dec_second,
          mesh_weight, send_grid, enc_tiles, enc_target, send_mesh, dec_slots, dec_tiles):
    rows = grid_state.shape[0]
    block = dec_tiles.shape[1]
    grid_cols = grid_state.shape[1]
    grid_blocks = grid_cols // block
    mesh_cols = mesh_state.shape[1]
    mesh_blocks = mesh_cols // block
    slots = enc_target.shape[-1]
    feeding = dec_slots.shape[1]
    pair = 2 * block
    at = jnp.stack([lax.axis_index("dom"), lax.axis_index("feat"), lax.axis_index("sub")]).astype(jnp.int32)
    send_grid = send_grid.reshape(slots // 2, 2).T
    send_mesh = send_mesh.reshape(slots // 2, 2).T
    chunk = jax.ShapeDtypeStruct((2, rows, pair), BF)
    call = functools.partial(pl.pallas_call, compiler_params=params(12 if n_dom <= 4 else 48))

    out = pl.pallas_call(
        functools.partial(pack_kernel, grid_blocks, n_dom),
        out_shape=[chunk] * n_dom,
        in_specs=[full(SMEM), full(SMEM), outside()],
        out_specs=[full()] * n_dom,
        scratch_shapes=[VMEM((2, rows, grid_cols + pair), BF), pltpu.SemaphoreType.DMA((4,))],
        cost_estimate=cost(1),
        compiler_params=params(12),
        name="pack",
    )(at, send_grid, grid_state)
    near = move(out, n_dom)

    def whole(w):
        return lax.all_gather(w, "feat", axis=0, tiled=True)

    def cross(kernel, chunks, *waits):
        mine = call(
            functools.partial(kernel, n_dom, len(waits)),
            out_shape=jax.ShapeDtypeStruct((n_dom, rows, pair), BF),
            in_specs=[anywhere()] * len(waits) + [full()] * n_dom,
            out_specs=full(),
            cost_estimate=cost(0),
            name="stack",
        )(*waits, *[chunks[k] for k in order_of(n_dom)])
        return lax.ppermute(mine, "sub", SWAP)

    def rows_of(w):
        return [w, lax.ppermute(w, "feat", SWAP)] if n_feat == 2 else [whole(w)]

    w1, w2, mw = rows_of(enc_first), rows_of(enc_second), whole(mesh_weight)
    to_mesh, split_state = call(
        functools.partial(scatter_kernel, n_dom, mesh_blocks),
        out_shape=[
            jax.ShapeDtypeStruct((2, n_dom * pair, mesh_cols), BF),
            jax.ShapeDtypeStruct(mesh_state.shape, BF),
        ],
        in_specs=[full(SMEM), full(SMEM), full(), full()],
        out_specs=[full(), full()],
        cost_estimate=cost(0),
        name="scatter",
    )(at, enc_target.reshape(slots), enc_tiles.reshape(block, slots * block), mesh_state)
    to_grid = call(
        functools.partial(spread_kernel, n_dom, feeding),
        grid=(grid_blocks // 2,),
        out_shape=jax.ShapeDtypeStruct((slots * block, grid_cols), BF),
        in_specs=[full(SMEM), full(SMEM), pl.BlockSpec((2, block, feeding * block), lambda i: (i, 0, 0))],
        out_specs=pl.BlockSpec((slots * block, pair), lambda i: (0, i)),
        cost_estimate=cost(0),
        name="spread",
    )(at, dec_slots.T, dec_tiles)

    d1 = whole(dec_first)
    far = cross(stack_kernel, near, w1[-1], w2[-1], mw, d1, to_mesh)
    acc = call(
        functools.partial(encode_kernel, n_dom),
        out_shape=jax.ShapeDtypeStruct((rows, mesh_cols), F32),
        in_specs=[full(SMEM)] + [full()] * (1 + n_dom + len(w1)),
        out_specs=full(),
        cost_estimate=cost(0.5),
        name="encode",
    )(at, to_mesh, *[near[k] for k in order_of(n_dom)], *w1)
    half = jax.ShapeDtypeStruct((rows, mesh_cols // 2), BF)
    g, first, second = call(
        functools.partial(gather_kernel, n_dom),
        out_shape=[jax.ShapeDtypeStruct((rows, mesh_cols), F32), half, half],
        in_specs=[full(SMEM)] + [full()] * (4 + len(w1) + len(w2)),
        out_specs=[full()] * 3,
        cost_estimate=cost(0.5),
        name="gather",
    )(at, acc, to_mesh, split_state, far, *w1, *w2)

    def other_feat(x):
        if n_feat == 2:
            return lax.ppermute(x, "feat", SWAP)
        return (lax.psum(x.astype(F32), "feat") - x.astype(F32)).astype(BF)

    thin = jax.ShapeDtypeStruct((rows, pair), BF)
    scratch = [VMEM((4, rows, mesh_cols // 2 + pair), BF)]
    *out, second = call(
        functools.partial(first_mesh_kernel, mesh_blocks, n_dom),
        out_shape=[thin] * n_dom + [half],
        in_specs=[full(SMEM), full(SMEM)] + [full()] * 4,
        out_specs=[full()] * (n_dom + 1),
        scratch_shapes=scratch,
        cost_estimate=cost(0.5),
        name="mesh",
    )(at, send_mesh, g, other_feat(first), mw, second)
    near_first = move(out, n_dom)
    out = call(
        functools.partial(mesh_kernel, mesh_blocks, n_dom, 1),
        out_shape=[thin] * n_dom,
        in_specs=[full(SMEM), full(SMEM)] + [full()] * 3,
        out_specs=[full()] * n_dom,
        scratch_shapes=scratch,
        cost_estimate=cost(0.5),
        name="mesh",
    )(at, send_mesh, g, other_feat(second), mw)
    near_second = move(out, n_dom)
    d2 = whole(call(
        hold_kernel,
        out_shape=jax.ShapeDtypeStruct(dec_second.shape, BF),
        in_specs=[anywhere(), full()],
        out_specs=full(),
        cost_estimate=cost(0),
        name="hold",
    )(out[0], dec_second))
    ordered = order_of(n_dom)
    far_first = cross(join_kernel, near_first, to_grid, out[0], d2)
    far_second = cross(join_kernel, near_second)
    acc = call(
        functools.partial(collect_kernel, n_dom),
        out_shape=jax.ShapeDtypeStruct((rows, grid_cols), F32),
        in_specs=[anywhere()] + [full()] * (2 + n_dom),
        out_specs=full(),
        cost_estimate=cost(0.5),
        name="collect",
    )(near_second[ordered[-1]], to_grid, far_first, *[near_first[k] for k in ordered])
    return call(
        functools.partial(decode_kernel, n_dom, grid_cols // 2),
        out_shape=jax.ShapeDtypeStruct(grid_state.shape, BF),
        in_specs=[full()] * (6 + n_dom),
        out_specs=anywhere(),
        scratch_shapes=[VMEM((rows, grid_cols), BF), pltpu.SemaphoreType.DMA((2,))],
        cost_estimate=cost(3),
        name="decode",
    )(acc, to_grid, d1, d2, grid_state, far_second, *[near_second[k] for k in ordered])


def solution(mesh):
    whole = ("ens", "dom", "sub", "feat")
    share = ("ens", "dom", "sub")
    in_specs = (
        P(None, whole),
        P("feat", share),
        P("feat", None),
        P("feat", None),
        P("feat", None),
        P("feat", None),
        P("feat", None),
        P(share, "feat", None, None),
        P(share, "feat", None, None),
        P(share, "feat", None),
        P(share, "feat", None, None),
        P(whole, None),
        P(whole, None, None),
    )
    return jax.shard_map(
        functools.partial(local, mesh.shape["dom"], mesh.shape["feat"]),
        mesh=mesh, in_specs=in_specs, out_specs=P(None, whole), check_vma=False,
    )
```

time: 85.1 us -> 77.4 us (0.910)
  the two profiles are of different devices: /device:TPU:9 before, /device:TPU:0 now
where the time goes in v2:
time: 77.4 us; the launch traced here: 77.2 us
  starting transfers between devices  22.1 us (29%)
  blocking collectives  22.1 us (29%)
  Pallas kernels  17 us (22%)
  waiting for transfers between devices  11.1 us (14%)
  local copies, waits for them, and re-layouts  4.64 us (6%)
    all_gather x3, blocking collectives, whole(): return lax.all_gather(w, 'feat', axis=0, tiled=True)  22.1 us
    ppermute x9, starting transfers between devices, move(): lax.ppermute(chunks[k], 'dom', [(i, i ^ k) for i in range(n_dom)])  15.8 us
    ppermute x2, waiting for transfers between devices, other_feat(): return lax.ppermute(x, 'feat', SWAP)  6.86 us
    unnamed x24, local copies, waits for them, and re-layouts  4.64 us
    pallas_call x1, Pallas kernels, local(): call(functools.partial(decode_kernel, n_dom, grid_cols // 2), out_shape=j...  3.82 us
    pallas_call x1, Pallas kernels, local(): call(functools.partial(spread_kernel, n_dom, feeding), grid=(grid_blocks...  3.42 us
    ppermute x2, starting transfers between devices, other_feat(): return lax.ppermute(x, 'feat', SWAP)  3.12 us
    ppermute x2, starting transfers between devices, rows_of(): return [w, lax.ppermute(w, 'feat', SWAP)] if n_feat == 2 else [whole(w)]  2.97 us
  transfers between devices with their start and end apart: 16, of which 4 were waited for; matrix products, arithmetic and copies ran while one was open for 0% of the time, Pallas kernels for 13%

profile of v2, /device:TPU:0, one launch (start us, length us, event | category | flops | bytes accessed | tf_op | source)
XLA Modules:
  0.0 77.2 jit_solution(1242028816453877011)
XLA Ops:
  0.0 2.9 %collective-permute-start.4 = (bf16[256,512]{1,0:T(8,128)(2,1)}, bf16[256,512]{1,0:T(8,128)(2,1)S(1)}, u32[]{:S(2)}, u32[]{:S(2)}) collective-permute-start(bf16[256,512]{1,0:T(8,128)(2,1)} %rest_2_.1), channel_id=1, source_target_pairs={{0,2},{2,0},{1,3},{3,1},{4,6},{6,4},{5,7},{7,5},{8,10},{10,8},{9,1... | collective-permute-start | bytes 786440 | tf_op jit(solution)/shard_map/ppermute | solution.py:310
  2.9 0.0 collective-permute-start.3
  3.0 0.1 pad_add_fusion.at_ref
  3.1 1.4 %copy-done = bf16[512,1536]{1,0:T(8,128)(2,1)S(1)} copy-done((bf16[512,1536]{1,0:T(8,128)(2,1)S(1)}, bf16[512,1536]{1,0:T(8,128)(2,1)}, u32[]{:S(2)}) %copy-start) | copy-done | bytes 1572888
  4.5 0.7 copy-done.10
  5.1 1.7 %pack.1 = (bf16[2,512,128]{2,1,0:T(8,128)(2,1)S(1)}, bf16[2,512,128]{2,1,0:T(8,128)(2,1)S(1)}, bf16[2,512,128]{2,1,0:T(8,128)(2,1)S(1)}, bf16[2,512,128]{2,1,0:T(8,128)(2,1)S(1)}) custom-call(s32[3]{0:T(128)S(1)} %pad_add_fusion.at_ref, s32[2,8]{1,0:T(2,128)S(1)} %bitcast.16, bf16[512,1536]{1,0:T(8,128)(2,1)S(1)} %copy-done), custom_call_target="tpu_custom_call" | custom-call | flops 400000000 | bytes 1000000 | tf_op jit(solution)/shard_map/pack/pallas_call | solution.py:283
  6.8 0.0 copy-start.2
  6.8 3.2 %collective-permute-start = (bf16[2,512,128]{2,1,0:T(8,128)(2,1)S(1)}, bf16[2,512,128]{2,1,0:T(8,128)(2,1)S(1)}, u32[]{:S(2)}, u32[]{:S(2)}) collective-permute-start(bf16[2,512,128]{2,1,0:T(8,128)(2,1)S(1)} %get-tuple-element.25), channel_id=1, source_target_pairs={{0,8},{4,12},{8,0},{12,4},{1,9},{5,13},{9,1},{13,5},{2,10},{6,14},... | collective-permute-start | bytes 786440 | tf_op jit(solution)/shard_map/ppermute | solution.py:262
  10.0 1.3 %collective-permute-start.1 = (bf16[2,512,128]{2,1,0:T(8,128)(2,1)S(1)}, bf16[2,512,128]{2,1,0:T(8,128)(2,1)S(1)}, u32[]{:S(2)}, u32[]{:S(2)}) collective-permute-start(bf16[2,512,128]{2,1,0:T(8,128)(2,1)S(1)} %get-tuple-element.26), channel_id=1, source_target_pairs={{0,12},{4,8},{8,4},{12,0},{1,13},{5,9},{9,5},{13,1},{2,14},{6,10},... | collective-permute-start | bytes 786440 | tf_op jit(solution)/shard_map/ppermute | solution.py:262
  11.4 0.2 collective-permute-start.2
  11.6 0.9 %copy-done.5 = bf16[256,512]{1,0:T(8,128)(2,1)S(1)} copy-done((bf16[256,512]{1,0:T(8,128)(2,1)S(1)}, bf16[256,512]{1,0:T(8,128)(2,1)}, u32[]{:S(2)}) %copy-start.5) | copy-done | bytes 262168
  12.5 0.9 %copy-done.7 = bf16[1,1,64,1024]{3,2,1,0:T(8,128)(2,1)S(1)} copy-done((bf16[1,1,64,1024]{3,2,1,0:T(8,128)(2,1)S(1)}, bf16[1,1,64,1024]{3,2,1,0:T(8,128)(2,1)}, u32[]{:S(2)}) %copy-start.7) | copy-done | bytes 131096
  13.4 0.7 copy-done.11
  14.1 1.1 %scatter.1 = (bf16[2,512,512]{2,1,0:T(8,128)(2,1)S(1)}, bf16[256,512]{1,0:T(8,128)(2,1)S(1)}) custom-call(s32[3]{0:T(128)S(1)} %pad_add_fusion.at_ref, s32[16]{0:T(128)S(1)} %bitcast.17, bf16[64,1024]{1,0:T(8,128)(2,1)S(1)} %bitcast.12, bf16[256,512]{1,0:T(8,128)(2,1)S(1)} %copy-done.5), custom_call_target="tpu_custom_call" | custom-call | tf_op jit(solution)/shard_map/scatter/pallas_call | solution.py:313
  15.2 7.8 %all_gather.9.refs_2_.mw_ref = bf16[512,512]{1,0:T(8,128)(2,1)S(1)} all-gather(bf16[256,512]{1,0:T(8,128)(2,1)} %param.19), channel_id=1, replica_groups=mesh['ens'=2,'dom'=4,'feat'=2,'sub'=2] {'feat'}, dimensions={0}, use_global_device_ids=true | all-gather | bytes 786432 | tf_op jit(solution)/shard_map/all_gather | solution.py:296
  23.0 7.2 %all_gather.10.refs_3_.d1_ref = bf16[512,512]{1,0:T(8,128)(2,1)S(1)} all-gather(bf16[256,512]{1,0:T(8,128)(2,1)} %param.17), channel_id=1, replica_groups=mesh['ens'=2,'dom'=4,'feat'=2,'sub'=2] {'feat'}, dimensions={0}, use_global_device_ids=true | all-gather | bytes 786432 | tf_op jit(solution)/shard_map/all_gather | solution.py:296
  30.3 0.0 collective-permute-done.4.refs_1_.rest_3_
  30.3 0.0 collective-permute-done.2.rest_3_.refs_8_
  30.3 0.0 copy-start.4
  30.4 0.0 copy-start.8
  30.4 0.1 collective-permute-start.5
  30.5 1.4 %encode.1.acc_ref = f32[512,512]{1,0:T(8,128)S(1)} custom-call(s32[3]{0:T(128)S(1)} %pad_add_fusion.at_ref, bf16[2,512,512]{2,1,0:T(8,128)(2,1)S(1)} %get-tuple-element.23.wide_ref.refs_4_, bf16[2,512,128]{2,1,0:T(8,128)(2,1)S(1)} %get-tuple-element.24.rest_0_.refs_5_, bf16[2,512,128]{2,1,0:T(8,128)(2,1)S(1)} %collective-permute-done.rest_1_.refs_6_, ...), custom_call_target="tpu_custom_call" | custom-call | flops 200000000 | bytes 500000 | tf_op jit(solution)/shard_map/encode/pallas_call | solution.py:336
  31.8 0.0 copy-start.3
  31.8 0.0 copy-start.9
  31.8 0.5 collective-permute-done.5.far_ref
  32.4 1.8 %gather.1 = (f32[512,512]{1,0:T(8,128)S(1)}, bf16[512,256]{1,0:T(8,128)(2,1)S(1)}, bf16[512,256]{1,0:T(8,128)(2,1)S(1)}) custom-call(s32[3]{0:T(128)S(1)} %pad_add_fusion.at_ref, f32[512,512]{1,0:T(8,128)S(1)} %encode.1.acc_ref, bf16[2,512,512]{2,1,0:T(8,128)(2,1)S(1)} %get-tuple-element.23.wide_ref.refs_4_, bf16[256,512]{1,0:T(8,128)(2,1)S(1)} %get-tuple-element.28.ms_ref, ...), custom_call_target="tpu_custom_call" | custom-call | flops 200000000 | bytes 500000 | tf_op jit(solution)/shard_map/gather/pallas_call | solution.py:345
  34.2 1.6 %collective-permute-start.6 = (bf16[512,256]{1,0:T(8,128)(2,1)S(1)}, bf16[512,256]{1,0:T(8,128)(2,1)S(1)}, u32[]{:S(2)}, u32[]{:S(2)}) collective-permute-start(bf16[512,256]{1,0:T(8,128)(2,1)S(1)} %get-tuple-element.30), channel_id=1, source_target_pairs={{0,2},{2,0},{1,3},{3,1},{4,6},{6,4},{5,7},{7,5},{8,10},{10,8},{9,1... | collective-permute-start | bytes 786440 | tf_op jit(solution)/shard_map/ppermute | solution.py:356
  35.8 6.9 %collective-permute-done.6.other_ref = bf16[512,256]{1,0:T(8,128)(2,1)S(1)} collective-permute-done((bf16[512,256]{1,0:T(8,128)(2,1)S(1)}, bf16[512,256]{1,0:T(8,128)(2,1)S(1)}, u32[]{:S(2)}, u32[]{:S(2)}) %collective-permute-start.6) | collective-permute-done | bytes 262176 | tf_op jit(solution)/shard_map/ppermute | solution.py:356
  42.6 1.3 %mesh.2 = (bf16[512,128]{1,0:T(8,128)(2,1)S(1)}, bf16[512,128]{1,0:T(8,128)(2,1)S(1)}, bf16[512,128]{1,0:T(8,128)(2,1)S(1)}, bf16[512,128]{1,0:T(8,128)(2,1)S(1)}, bf16[512,256]{1,0:T(8,128)(2,1)S(1)}) custom-call(s32[3]{0:T(128)S(1)} %pad_add_fusion.at_ref, s32[2,8]{1,0:T(2,128)S(1)} %bitcast.13, f32[512,512]{1,0:T(8,128)S(1)} %get-tuple-element.29.g_ref, ...), custom_call_target="tpu_custom_call" | custom-call | flops 200000000 | bytes 500000 | tf_op jit(solution)/shard_map/mesh/pallas_call | solution.py:361
  44.0 0.0 copy-start.6
  44.0 1.6 %collective-permute-start.7 = (bf16[512,256]{1,0:T(8,128)(2,1)S(1)}, bf16[512,256]{1,0:T(8,128)(2,1)S(1)}, u32[]{:S(2)}, u32[]{:S(2)}) collective-permute-start(bf16[512,256]{1,0:T(8,128)(2,1)S(1)} %get-tuple-element.32), channel_id=1, source_target_pairs={{0,2},{2,0},{1,3},{3,1},{4,6},{6,4},{5,7},{7,5},{8,10},{10,8},{9,1... | collective-permute-start | bytes 786440 | tf_op jit(solution)/shard_map/ppermute | solution.py:356
  45.5 5.0 %collective-permute-start.9 = (bf16[512,128]{1,0:T(8,128)(2,1)S(1)}, bf16[512,128]{1,0:T(8,128)(2,1)S(1)}, u32[]{:S(2)}, u32[]{:S(2)}) collective-permute-start(bf16[512,128]{1,0:T(8,128)(2,1)S(1)} %get-tuple-element.36), channel_id=1, source_target_pairs={{0,8},{4,12},{8,0},{12,4},{1,9},{5,13},{9,1},{13,5},{2,10},{6,14},... | collective-permute-start | bytes 393224 | tf_op jit(solution)/shard_map/ppermute | solution.py:262
  50.5 3.4 %spread.1.refs_0_.wide_ref = bf16[1024,1536]{1,0:T(8,128)(2,1)S(1)} custom-call(s32[3]{0:T(128)S(1)} %pad_add_fusion.at_ref, s32[4,24]{1,0:T(4,128)S(1)} %bitcast.15, bf16[24,64,256]{2,1,0:T(8,128)(2,1)S(1)} %copy-done.3), custom_call_target="tpu_custom_call" | custom-call | tf_op jit(solution)/shard_map/spread/pallas_call | solution.py:324
  53.9 0.5 collective-permute-start.10
  54.4 0.1 collective-permute-start.11
  54.6 1.3 %mesh.3 = (bf16[512,128]{1,0:T(8,128)(2,1)S(1)}, bf16[512,128]{1,0:T(8,128)(2,1)S(1)}, bf16[512,128]{1,0:T(8,128)(2,1)S(1)}, bf16[512,128]{1,0:T(8,128)(2,1)S(1)}) custom-call(s32[3]{0:T(128)S(1)} %pad_add_fusion.at_ref, s32[2,8]{1,0:T(2,128)S(1)} %bitcast.14, f32[512,512]{1,0:T(8,128)S(1)} %get-tuple-element.29.g_ref, ...), custom_call_target="tpu_custom_call" | custom-call | flops 200000000 | bytes 500000 | tf_op jit(solution)/shard_map/mesh/pallas_call | solution.py:371
  55.9 2.0 %collective-permute-start.8 = (bf16[512,128]{1,0:T(8,128)(2,1)S(1)}, bf16[512,128]{1,0:T(8,128)(2,1)S(1)}, u32[]{:S(2)}, u32[]{:S(2)}) collective-permute-start(bf16[512,128]{1,0:T(8,128)(2,1)S(1)} %get-tuple-element.33), channel_id=1, source_target_pairs={{0,4},{4,0},{8,12},{12,8},{1,5},{5,1},{9,13},{13,9},{2,6},{6,2},{1... | collective-permute-start | bytes 393224 | tf_op jit(solution)/shard_map/ppermute | solution.py:262
  57.9 2.0 %collective-permute-start.13 = (bf16[512,128]{1,0:T(8,128)(2,1)S(1)}, bf16[512,128]{1,0:T(8,128)(2,1)S(1)}, u32[]{:S(2)}, u32[]{:S(2)}) collective-permute-start(bf16[512,128]{1,0:T(8,128)(2,1)S(1)} %get-tuple-element.39), channel_id=1, source_target_pairs={{0,8},{4,12},{8,0},{12,4},{1,9},{5,13},{9,1},{13,5},{2,10},{6,14},... | collective-permute-start | bytes 393224 | tf_op jit(solution)/shard_map/ppermute | solution.py:262
  59.9 0.0 collective-permute-done.9.refs_4_.rest_1_
  59.9 1.5 %collective-permute-start.14 = (bf16[512,128]{1,0:T(8,128)(2,1)S(1)}, bf16[512,128]{1,0:T(8,128)(2,1)S(1)}, u32[]{:S(2)}, u32[]{:S(2)}) collective-permute-start(bf16[512,128]{1,0:T(8,128)(2,1)S(1)} %get-tuple-element.40), channel_id=1, source_target_pairs={{0,12},{4,8},{8,4},{12,0},{1,13},{5,9},{9,5},{13,1},{2,14},{6,10},... | collective-permute-start | bytes 393224 | tf_op jit(solution)/shard_map/ppermute | solution.py:262
  61.4 7.0 %all_gather.11.refs_2_.d2_ref = bf16[512,512]{1,0:T(8,128)(2,1)S(1)} all-gather(bf16[256,512]{1,0:T(8,128)(2,1)S(1)} %hold.1), channel_id=1, replica_groups=mesh['ens'=2,'dom'=4,'feat'=2,'sub'=2] {'feat'}, dimensions={0}, use_global_device_ids=true | all-gather | bytes 786432 | tf_op jit(solution)/shard_map/all_gather | solution.py:296
  68.4 0.1 collective-permute-start.12
  68.5 2.8 %collective-permute-done.14.refs_2_.rest_2_ = bf16[512,128]{1,0:T(8,128)(2,1)S(1)} collective-permute-done((bf16[512,128]{1,0:T(8,128)(2,1)S(1)}, bf16[512,128]{1,0:T(8,128)(2,1)S(1)}, u32[]{:S(2)}, u32[]{:S(2)}) %collective-permute-start.14) | collective-permute-done | bytes 131104 | tf_op jit(solution)/shard_map/ppermute | solution.py:262
  71.4 0.0 copy-start.1
  71.4 0.1 collective-permute-start.15
  71.5 1.0 %collect.1.acc_ref = f32[512,1536]{1,0:T(8,128)S(1)} custom-call(bf16[512,128]{1,0:T(8,128)(2,1)S(1)} %collective-permute-done.8.ready_ref.refs_3_.rest_3_, bf16[1024,1536]{1,0:T(8,128)(2,1)S(1)} %spread.1.refs_0_.wide_ref, bf16[4,512,128]{2,1,0:T(8,128)(2,1)S(1)} %collective-permute-done.12.far_ref, bf16[512,128]{1,0:T(8,128)(2,1)S(1)} %get-tuple-element.35.refs_3_.rest_0_, ...), custom_call_target="tpu_custom_call" | custom-call | flops 200000000 | bytes 500000 | tf_op jit(solution)/shard_map/collect/pallas_call | solution.py:392
  72.5 0.9 %collective-permute-done.15.far_ref = bf16[4,512,128]{2,1,0:T(8,128)(2,1)S(1)} collective-permute-done((bf16[4,512,128]{2,1,0:T(8,128)(2,1)S(1)}, bf16[4,512,128]{2,1,0:T(8,128)(2,1)S(1)}, u32[]{:S(2)}, u32[]{:S(2)}) %collective-permute-start.15) | collective-permute-done | bytes 524320 | tf_op jit(solution)/shard_map/ppermute | solution.py:307
  73.4 3.8 %decode.1 = bf16[512,1536]{1,0:T(8,128)(2,1)} custom-call(f32[512,1536]{1,0:T(8,128)S(1)} %collect.1.acc_ref, bf16[1024,1536]{1,0:T(8,128)(2,1)S(1)} %spread.1.refs_0_.wide_ref, bf16[512,512]{1,0:T(8,128)(2,1)S(1)} %all_gather.10.refs_3_.d1_ref, bf16[512,512]{1,0:T(8,128)(2,1)S(1)} %all_gather.11.refs_2_.d2_ref, bf16[512,1536]{1,0:T(8,128)(2,1)S(1)} %copy-done.1, ...), custom_call_target="tpu_custom_call" | custom-call | flops 1200000000 | bytes 3000000 | tf_op jit(solution)/shard_map/decode/pallas_call | solution.py:400
  (25 shorter events, 0.2 us)
Async XLA Ops:
  0.0 30.3 %collective-permute-start.4 = (bf16[256,512]{1,0:T(8,128)(2,1)}, bf16[256,512]{1,0:T(8,128)(2,1)S(1)}, u32[]{:S(2)}, u32[]{:S(2)}) collective-permute-start(bf16[256,512]{1,0:T(8,128)(2,1)} %rest_2_.1), channel_id=1, source_target_pairs={{0,2},{2,0},{1,3},{3,1},{4,6},{6,4},{5,7},{7,5},{8,10},{10,8},{9,1... | collective-permute-start | bytes 786440 | tf_op jit(solution)/shard_map/ppermute | solution.py:310
  2.9 27.3 %collective-permute-start.3 = (bf16[256,512]{1,0:T(8,128)(2,1)}, bf16[256,512]{1,0:T(8,128)(2,1)S(1)}, u32[]{:S(2)}, u32[]{:S(2)}) collective-permute-start(bf16[256,512]{1,0:T(8,128)(2,1)} %rest_0_.1), channel_id=1, source_target_pairs={{0,2},{2,0},{1,3},{3,1},{4,6},{6,4},{5,7},{7,5},{8,10},{10,8},{9,1... | collective-permute-start | bytes 786440 | tf_op jit(solution)/shard_map/ppermute | solution.py:310
  3.0 1.4 %copy-start = (bf16[512,1536]{1,0:T(8,128)(2,1)S(1)}, bf16[512,1536]{1,0:T(8,128)(2,1)}, u32[]{:S(2)}) copy-start(bf16[512,1536]{1,0:T(8,128)(2,1)} %grid_ref.1) | copy-start | bytes 4718596
  4.5 0.7 copy-start.10
  6.8 23.6 %copy-start.2 = (bf16[256,512]{1,0:T(8,128)(2,1)S(1)}, bf16[256,512]{1,0:T(8,128)(2,1)}, u32[]{:S(2)}) copy-start(bf16[256,512]{1,0:T(8,128)(2,1)} %rest_0_.1) | copy-start | bytes 786436
  6.8 23.4 %collective-permute-start = (bf16[2,512,128]{2,1,0:T(8,128)(2,1)S(1)}, bf16[2,512,128]{2,1,0:T(8,128)(2,1)S(1)}, u32[]{:S(2)}, u32[]{:S(2)}) collective-permute-start(bf16[2,512,128]{2,1,0:T(8,128)(2,1)S(1)} %get-tuple-element.25), channel_id=1, source_target_pairs={{0,8},{4,12},{8,0},{12,4},{1,9},{5,13},{9,1},{13,5},{2,10},{6,14},... | collective-permute-start | bytes 786440 | tf_op jit(solution)/shard_map/ppermute | solution.py:262
  10.0 20.3 %collective-permute-start.1 = (bf16[2,512,128]{2,1,0:T(8,128)(2,1)S(1)}, bf16[2,512,128]{2,1,0:T(8,128)(2,1)S(1)}, u32[]{:S(2)}, u32[]{:S(2)}) collective-permute-start(bf16[2,512,128]{2,1,0:T(8,128)(2,1)S(1)} %get-tuple-element.26), channel_id=1, source_target_pairs={{0,12},{4,8},{8,4},{12,0},{1,13},{5,9},{9,5},{13,1},{2,14},{6,10},... | collective-permute-start | bytes 786440 | tf_op jit(solution)/shard_map/ppermute | solution.py:262
  11.4 18.9 %collective-permute-start.2 = (bf16[2,512,128]{2,1,0:T(8,128)(2,1)S(1)}, bf16[2,512,128]{2,1,0:T(8,128)(2,1)S(1)}, u32[]{:S(2)}, u32[]{:S(2)}) collective-permute-start(bf16[2,512,128]{2,1,0:T(8,128)(2,1)S(1)} %get-tuple-element.27), channel_id=1, source_target_pairs={{0,4},{4,0},{8,12},{12,8},{1,5},{5,1},{9,13},{13,9},{2,6},{6,2},{1... | collective-permute-start | bytes 786440 | tf_op jit(solution)/shard_map/ppermute | solution.py:262
  11.6 0.9 %copy-start.5 = (bf16[256,512]{1,0:T(8,128)(2,1)S(1)}, bf16[256,512]{1,0:T(8,128)(2,1)}, u32[]{:S(2)}) copy-start(bf16[256,512]{1,0:T(8,128)(2,1)} %ms_ref.1) | copy-start | bytes 786436
  12.5 0.9 %copy-start.7 = (bf16[1,1,64,1024]{3,2,1,0:T(8,128)(2,1)S(1)}, bf16[1,1,64,1024]{3,2,1,0:T(8,128)(2,1)}, u32[]{:S(2)}) copy-start(bf16[1,1,64,1024]{3,2,1,0:T(8,128)(2,1)} %param.21) | copy-start | bytes 393220
  13.4 0.7 copy-start.11
  30.3 2.0 %copy-start.4 = (bf16[256,512]{1,0:T(8,128)(2,1)S(1)}, bf16[256,512]{1,0:T(8,128)(2,1)}, u32[]{:S(2)}) copy-start(bf16[256,512]{1,0:T(8,128)(2,1)} %rest_2_.1) | copy-start | bytes 786436
  30.4 12.2 %copy-start.8 = (s32[1,1,8,2]{2,3,1,0:T(2,128)S(1)}, s32[1,1,8,2]{2,3,1,0:T(2,128)}, u32[]{:S(2)}) copy-start(s32[1,1,8,2]{2,3,1,0:T(2,128)} %param.23) | copy-start | bytes 196
  30.4 2.0 %collective-permute-start.5 = (bf16[4,512,128]{2,1,0:T(8,128)(2,1)S(1)}, bf16[4,512,128]{2,1,0:T(8,128)(2,1)S(1)}, u32[]{:S(2)}, u32[]{:S(2)}) collective-permute-start(bf16[4,512,128]{2,1,0:T(8,128)(2,1)S(1)} %stack.19), channel_id=1, source_target_pairs={{0,1},{1,0},{2,3},{3,2},{4,5},{5,4},{6,7},{7,6},{8,9},{9,8},{10,11... | collective-permute-start | bytes 1572872 | tf_op jit(solution)/shard_map/ppermute | solution.py:307
  31.8 18.7 %copy-start.3 = (bf16[24,64,256]{2,1,0:T(8,128)(2,1)S(1)}, bf16[24,64,256]{2,1,0:T(8,128)(2,1)}, u32[]{:S(2)}) copy-start(bf16[24,64,256]{2,1,0:T(8,128)(2,1)} %tiles_ref.1) | copy-start | bytes 2359300
  31.8 18.7 %copy-start.9 = (s32[24,4]{0,1:T(4,128)S(1)}, s32[24,4]{0,1:T(4,128)}, u32[]{:S(2)}) copy-start(s32[24,4]{0,1:T(4,128)} %param.24) | copy-start | bytes 1156
  34.2 8.4 %collective-permute-start.6 = (bf16[512,256]{1,0:T(8,128)(2,1)S(1)}, bf16[512,256]{1,0:T(8,128)(2,1)S(1)}, u32[]{:S(2)}, u32[]{:S(2)}) collective-permute-start(bf16[512,256]{1,0:T(8,128)(2,1)S(1)} %get-tuple-element.30), channel_id=1, source_target_pairs={{0,2},{2,0},{1,3},{3,1},{4,6},{6,4},{5,7},{7,5},{8,10},{10,8},{9,1... | collective-permute-start | bytes 786440 | tf_op jit(solution)/shard_map/ppermute | solution.py:356
  44.0 15.9 %copy-start.6 = (bf16[256,512]{1,0:T(8,128)(2,1)S(1)}, bf16[256,512]{1,0:T(8,128)(2,1)}, u32[]{:S(2)}) copy-start(bf16[256,512]{1,0:T(8,128)(2,1)} %x_ref.1) | copy-start | bytes 786436
  44.0 10.6 %collective-permute-start.7 = (bf16[512,256]{1,0:T(8,128)(2,1)S(1)}, bf16[512,256]{1,0:T(8,128)(2,1)S(1)}, u32[]{:S(2)}, u32[]{:S(2)}) collective-permute-start(bf16[512,256]{1,0:T(8,128)(2,1)S(1)} %get-tuple-element.32), channel_id=1, source_target_pairs={{0,2},{2,0},{1,3},{3,1},{4,6},{6,4},{5,7},{7,5},{8,10},{10,8},{9,1... | collective-permute-start | bytes 786440 | tf_op jit(solution)/shard_map/ppermute | solution.py:356
  45.5 14.4 %collective-permute-start.9 = (bf16[512,128]{1,0:T(8,128)(2,1)S(1)}, bf16[512,128]{1,0:T(8,128)(2,1)S(1)}, u32[]{:S(2)}, u32[]{:S(2)}) collective-permute-start(bf16[512,128]{1,0:T(8,128)(2,1)S(1)} %get-tuple-element.36), channel_id=1, source_target_pairs={{0,8},{4,12},{8,0},{12,4},{1,9},{5,13},{9,1},{13,5},{2,10},{6,14},... | collective-permute-start | bytes 393224 | tf_op jit(solution)/shard_map/ppermute | solution.py:262
  53.9 14.5 %collective-permute-start.10 = (bf16[512,128]{1,0:T(8,128)(2,1)S(1)}, bf16[512,128]{1,0:T(8,128)(2,1)S(1)}, u32[]{:S(2)}, u32[]{:S(2)}) collective-permute-start(bf16[512,128]{1,0:T(8,128)(2,1)S(1)} %get-tuple-element.37), channel_id=1, source_target_pairs={{0,12},{4,8},{8,4},{12,0},{1,13},{5,9},{9,5},{13,1},{2,14},{6,10},... | collective-permute-start | bytes 393224 | tf_op jit(solution)/shard_map/ppermute | solution.py:262
  54.4 14.0 %collective-permute-start.11 = (bf16[512,128]{1,0:T(8,128)(2,1)S(1)}, bf16[512,128]{1,0:T(8,128)(2,1)S(1)}, u32[]{:S(2)}, u32[]{:S(2)}) collective-permute-start(bf16[512,128]{1,0:T(8,128)(2,1)S(1)} %get-tuple-element.38), channel_id=1, source_target_pairs={{0,4},{4,0},{8,12},{12,8},{1,5},{5,1},{9,13},{13,9},{2,6},{6,2},{1... | collective-permute-start | bytes 393224 | tf_op jit(solution)/shard_map/ppermute | solution.py:262
  55.9 12.6 %collective-permute-start.8 = (bf16[512,128]{1,0:T(8,128)(2,1)S(1)}, bf16[512,128]{1,0:T(8,128)(2,1)S(1)}, u32[]{:S(2)}, u32[]{:S(2)}) collective-permute-start(bf16[512,128]{1,0:T(8,128)(2,1)S(1)} %get-tuple-element.33), channel_id=1, source_target_pairs={{0,4},{4,0},{8,12},{12,8},{1,5},{5,1},{9,13},{13,9},{2,6},{6,2},{1... | collective-permute-start | bytes 393224 | tf_op jit(solution)/shard_map/ppermute | solution.py:262
  57.9 10.7 %collective-permute-start.13 = (bf16[512,128]{1,0:T(8,128)(2,1)S(1)}, bf16[512,128]{1,0:T(8,128)(2,1)S(1)}, u32[]{:S(2)}, u32[]{:S(2)}) collective-permute-start(bf16[512,128]{1,0:T(8,128)(2,1)S(1)} %get-tuple-element.39), channel_id=1, source_target_pairs={{0,8},{4,12},{8,0},{12,4},{1,9},{5,13},{9,1},{13,5},{2,10},{6,14},... | collective-permute-start | bytes 393224 | tf_op jit(solution)/shard_map/ppermute | solution.py:262
  59.9 11.4 %collective-permute-start.14 = (bf16[512,128]{1,0:T(8,128)(2,1)S(1)}, bf16[512,128]{1,0:T(8,128)(2,1)S(1)}, u32[]{:S(2)}, u32[]{:S(2)}) collective-permute-start(bf16[512,128]{1,0:T(8,128)(2,1)S(1)} %get-tuple-element.40), channel_id=1, source_target_pairs={{0,12},{4,8},{8,4},{12,0},{1,13},{5,9},{9,5},{13,1},{2,14},{6,10},... | collective-permute-start | bytes 393224 | tf_op jit(solution)/shard_map/ppermute | solution.py:262
  68.4 3.0 %collective-permute-start.12 = (bf16[4,512,128]{2,1,0:T(8,128)(2,1)S(1)}, bf16[4,512,128]{2,1,0:T(8,128)(2,1)S(1)}, u32[]{:S(2)}, u32[]{:S(2)}) collective-permute-start(bf16[4,512,128]{2,1,0:T(8,128)(2,1)S(1)} %stack.20), channel_id=1, source_target_pairs={{0,1},{1,0},{2,3},{3,2},{4,5},{5,4},{6,7},{7,6},{8,9},{9,8},{10,11... | collective-permute-start | bytes 1572872 | tf_op jit(solution)/shard_map/ppermute | solution.py:307
  71.4 2.0 %copy-start.1 = (bf16[512,1536]{1,0:T(8,128)(2,1)S(1)}, bf16[512,1536]{1,0:T(8,128)(2,1)}, u32[]{:S(2)}) copy-start(bf16[512,1536]{1,0:T(8,128)(2,1)} %grid_ref.1) | copy-start | bytes 4718596
  71.4 2.0 %collective-permute-start.15 = (bf16[4,512,128]{2,1,0:T(8,128)(2,1)S(1)}, bf16[4,512,128]{2,1,0:T(8,128)(2,1)S(1)}, u32[]{:S(2)}, u32[]{:S(2)}) collective-permute-start(bf16[4,512,128]{2,1,0:T(8,128)(2,1)S(1)} %stack.21), channel_id=1, source_target_pairs={{0,1},{1,0},{2,3},{3,2},{4,5},{5,4},{6,7},{7,6},{8,9},{9,8},{10,11... | collective-permute-start | bytes 1572872 | tf_op jit(solution)/shard_map/ppermute | solution.py:307

commit v3 on v2

--- a/solution.py
+++ b/solution.py
@@ -30,10 +30,6 @@
     return pl.BlockSpec(memory_space=pl.ANY)
 
 
-def outside():
-    return pl.BlockSpec(memory_space=pltpu.HBM)
-
-
 def silu(x):
     half = 0.5 * x
     return half + half * jnp.tanh(half)
@@ -55,13 +51,14 @@
     return jnp.concatenate([v[:, width:], v[:, :width]], axis=1)
 
 
-def pack_rows(step, blocks, n_dom, at_ref, send_ref, buf, i, outs):
+def pack_rows(step, blocks, n_dom, at_ref, send_ref, src_ref, buf, i, outs):
     pair = outs[0].shape[2]
     width = pair // 2
     cols = blocks * width
     here = slice(i * step, (i + 1) * step)
     for p in range(blocks // 2):
-        v = buf[0, here, p * pair:(p + 1) * pair]
+        v = src_ref[here, p * pair:(p + 1) * pair]
+        buf[0, here, p * pair:(p + 1) * pair] = v
         buf[1, here, p * pair:(p + 1) * pair] = swap_halves(v, width)
     low = lax.broadcasted_iota(jnp.int32, (step, pair), 1) < width
     for k in range(n_dom):
@@ -78,23 +75,15 @@
 
 
 def pack_kernel(blocks, n_dom, at_ref, send_ref, src_ref, *refs):
-    outs, buf, sems = refs[:n_dom], refs[n_dom], refs[n_dom + 1]
+    outs, buf = refs[:n_dom], refs[n_dom]
     rows, cols = src_ref.shape
-    parts = 4
-    step = rows // parts
-    copies = []
-    for i in range(parts):
-        here = pl.ds(i * step, step)
-        copies.append(pltpu.make_async_copy(src_ref.at[here, :], buf.at[0, here, pl.ds(0, cols)], sems.at[i]))
-        copies[-1].start()
     buf[0, :, cols:] = jnp.zeros((rows, buf.shape[2] - cols), BF)
-    for i in range(parts):
-        copies[i].wait()
-        pack_rows(step, blocks, n_dom, at_ref, send_ref, buf, i, outs)
+    for i in range(4):
+        pack_rows(rows // 4, blocks, n_dom, at_ref, send_ref, src_ref, buf, i, outs)
 
 
 def stack_kernel(n_dom, waits, *refs):
-    chunks, out = refs[waits:waits + n_dom], refs[waits + n_dom]
+    chunks, out = refs[:n_dom], refs[n_dom + waits]
     for i, k in enumerate(order_of(n_dom)):
         out[k] = chunks[i][1]
 
@@ -147,7 +136,7 @@
             k = at_ref[0] ^ (peer // 2)
             j = at_ref[2] ^ lax.rem(peer, 2)
             for part in range(2):
-                row = part * (out_ref.shape[0] // 2) + ((k * 2 + j) * 2 + lax.rem(q, 2)) * half
+                row = part * (out_ref.shape[0] // 2) + ((j * n_dom + k) * 2 + lax.rem(q, 2)) * half
                 v = t[i * block + part * half:i * block + (part + 1) * half, :]
                 v = jnp.where(low if h == 0 else ~low, v, jnp.zeros_like(v))
                 out_ref[pl.ds(pl.multiple_of(row, half), half), :] += v
@@ -161,27 +150,38 @@
     out_ref[...] = mm(hid, wide_ref[0])
 
 
+def messages(at_ref, ws, h, total, ms_ref, g_ref, out_ref):
+    g_ref[...] = mt(joined(at_ref, ws), total)
+    rows = ms_ref.shape[0]
+    cols = g_ref.shape[1]
+    here = pl.ds(pl.multiple_of(at_ref[1] * rows, rows), rows)
+    g_ref[here, :] += ms_ref[:, h * cols:(h + 1) * cols].astype(F32)
+    out_ref[...] = g_ref[...].astype(BF)
+
+
 def gather_kernel(n_dom, at_ref, acc_ref, wide_ref, ms_ref, far_ref, *rest):
-    ws, (g_ref, first_ref, second_ref) = rest[:-3], rest[-3:]
+    ws, (g_ref, first_ref, later_ref) = rest[:-3], rest[-3:]
     count = len(ws) // 2
+    half = g_ref.shape[1]
     x = jnp.concatenate([far_ref[k] for k in range(n_dom)], axis=1)
     hid = silu(mt(joined(at_ref, ws[:count]), x)).astype(BF)
-    acc = acc_ref[...] + mm(hid, wide_ref[1])
-    g_ref[...] = mt(joined(at_ref, ws[count:]), acc.astype(BF))
-    rows = ms_ref.shape[0]
-    here = pl.ds(pl.multiple_of(at_ref[1] * rows, rows), rows)
-    g_ref[here, :] += ms_ref[...].astype(F32)
-    half = g_ref.shape[1] // 2
-    first_ref[...] = g_ref[:, :half].astype(BF)
-    second_ref[...] = g_ref[:, half:].astype(BF)
-
-
-def mesh_kernel(blocks, n_dom, h, at_ref, send_ref, g_ref, other_ref, mw_ref, *rest):
+    total = (acc_ref[...] + mm(hid, wide_ref[1])).astype(BF)
+    messages(at_ref, ws[count:], 0, total[:, :half], ms_ref, g_ref, first_ref)
+    later_ref[...] = total[:, half:]
+
+
+def later_kernel(at_ref, total_ref, ms_ref, *rest):
+    ws, (g_ref, out_ref) = rest[:-2], rest[-2:]
+    messages(at_ref, ws, 1, total_ref[...], ms_ref, g_ref, out_ref)
+
+
+def mesh_kernel(blocks, n_dom, at_ref, send_ref, g_ref, other_ref, mw_ref, d1_ref, *rest):
     outs, buf = rest[-1 - n_dom:-1], rest[-1]
     rows = g_ref.shape[0]
-    cols = g_ref.shape[1] // 2
-    new = (g_ref[:, h * cols:(h + 1) * cols] + other_ref[...].astype(F32)).astype(BF)
+    cols = g_ref.shape[1]
+    new = (g_ref[...] + other_ref[...].astype(F32)).astype(BF)
     hid = silu(mt(mw_ref[...], new)).astype(BF)
+    hid = mt(d1_ref[...], hid).astype(BF)
     part = cols // blocks
     for p in range(cols // 128):
         v = hid[:, p * 128:(p + 1) * 128]
@@ -207,9 +207,9 @@
             )
 
 
-def first_mesh_kernel(blocks, n_dom, at_ref, send_ref, g_ref, other_ref, mw_ref, later_ref, *rest):
+def first_mesh_kernel(blocks, n_dom, at_ref, send_ref, g_ref, other_ref, mw_ref, d1_ref, later_ref, ready_ref, *rest):
     outs, later_out, buf = rest[:n_dom], rest[n_dom], rest[n_dom + 1]
-    mesh_kernel(blocks, n_dom, 0, at_ref, send_ref, g_ref, other_ref, mw_ref, *outs, buf)
+    mesh_kernel(blocks, n_dom, at_ref, send_ref, g_ref, other_ref, mw_ref, d1_ref, *outs, buf)
     later_out[...] = later_ref[...]
 
 
@@ -217,29 +217,36 @@
     out_ref[...] = x_ref[...]
 
 
+def paired(chunks, upper):
+    width = chunks[0].shape[1] // 2
+    low = lax.broadcasted_iota(jnp.int32, chunks[0].shape, 1) < width
+    out = []
+    for a, b in zip(chunks[::2], chunks[1::2]):
+        a, b = (swap_halves(a, width), b) if upper else (a, swap_halves(b, width))
+        out.append(jnp.where(low, a, b))
+    return out
+
+
 def join_kernel(n_dom, waits, *refs):
-    chunks, out = refs[waits:waits + n_dom], refs[waits + n_dom]
-    for i, k in enumerate(order_of(n_dom)):
-        out[k] = chunks[i][...]
-
-
-def pool_of(n_dom, near, far_ref):
+    chunks, out = refs[:n_dom], refs[n_dom + waits]
     place = order_of(n_dom).index
-    low = lax.broadcasted_iota(jnp.int32, far_ref.shape[1:], 1) < far_ref.shape[2] // 2
-    return jnp.concatenate([jnp.where(low, near[place(k)][...], far_ref[k]) for k in range(n_dom)], axis=1)
+    for i, v in enumerate(paired([chunks[place(k)][...] for k in range(n_dom)], True)):
+        out[i] = v
 
 
 def collect_kernel(n_dom, ready_ref, wide_ref, far_ref, *rest):
-    chunks, out_ref = rest[:n_dom], rest[n_dom]
-    pool = pool_of(n_dom, chunks, far_ref)
+    firsts, seconds, out_ref = rest[:n_dom], rest[n_dom:-1], rest[-1]
+    place = order_of(n_dom).index
+    pool = paired([firsts[place(k)][...] for k in range(n_dom)], False)
+    pool += [far_ref[i] for i in range(n_dom // 2)]
+    pool += paired([seconds[place(k)][...] for k in range(n_dom)], False)
+    pool = jnp.concatenate(pool, axis=1)
     out_ref[...] = mm(pool, wide_ref[:pool.shape[1], :])
 
 
-def decode_kernel(n_dom, cols, acc_ref, wide_ref, d1_ref, d2_ref, grid_ref, far_ref, *rest):
-    chunks, (out_ref, buf, sems) = rest[:n_dom], rest[n_dom:]
-    pool = pool_of(n_dom, chunks, far_ref)
-    got = (acc_ref[...] + mm(pool, wide_ref[pool.shape[1]:, :])).astype(BF)
-    dec = silu(mt(d1_ref[...], got)).astype(BF)
+def decode_kernel(n_dom, cols, acc_ref, wide_ref, d2_ref, grid_ref, far_ref, out_ref, buf, sems):
+    pool = jnp.concatenate([far_ref[i] for i in range(n_dom // 2)], axis=1)
+    dec = silu(acc_ref[...] + mm(pool, wide_ref[wide_ref.shape[0] - pool.shape[1]:, :])).astype(BF)
     copies = []
     for t in range(grid_ref.shape[1] // cols):
         here = slice(t * cols, (t + 1) * cols)
@@ -283,9 +290,9 @@
     out = pl.pallas_call(
         functools.partial(pack_kernel, grid_blocks, n_dom),
         out_shape=[chunk] * n_dom,
-        in_specs=[full(SMEM), full(SMEM), outside()],
+        in_specs=[full(SMEM), full(SMEM), full()],
         out_specs=[full()] * n_dom,
-        scratch_shapes=[VMEM((2, rows, grid_cols + pair), BF), pltpu.SemaphoreType.DMA((4,))],
+        scratch_shapes=[VMEM((2, rows, grid_cols + pair), BF)],
         cost_estimate=cost(1),
         compiler_params=params(12),
         name="pack",
@@ -295,16 +302,16 @@
     def whole(w):
         return lax.all_gather(w, "feat", axis=0, tiled=True)
 
-    def cross(kernel, chunks, *waits):
+    def cross(kernel, count, chunks, *waits):
         mine = call(
             functools.partial(kernel, n_dom, len(waits)),
-            out_shape=jax.ShapeDtypeStruct((n_dom, rows, pair), BF),
-            in_specs=[anywhere()] * len(waits) + [full()] * n_dom,
+            out_shape=jax.ShapeDtypeStruct((count, rows, pair), BF),
+            in_specs=[full()] * n_dom + [anywhere()] * len(waits),
             out_specs=full(),
             cost_estimate=cost(0),
             name="stack",
-        )(*waits, *[chunks[k] for k in order_of(n_dom)])
-        return lax.ppermute(mine, "sub", SWAP)
+        )(*[chunks[k] for k in order_of(n_dom)], *waits)
+        return lax.ppermute(mine, "sub", SWAP), mine
 
     def rows_of(w):
         return [w, lax.ppermute(w, "feat", SWAP)] if n_feat == 2 else [whole(w)]
@@ -332,7 +339,7 @@
     )(at, dec_slots.T, dec_tiles)
 
     d1 = whole(dec_first)
-    far = cross(stack_kernel, near, w1[-1], w2[-1], mw, d1, to_mesh)
+    far, _ = cross(stack_kernel, n_dom, near, w1[-1], w2[-1], mw, d1, to_mesh)
     acc = call(
         functools.partial(encode_kernel, n_dom),
         out_shape=jax.ShapeDtypeStruct((rows, mesh_cols), F32),
@@ -342,14 +349,23 @@
         name="encode",
     )(at, to_mesh, *[near[k] for k in order_of(n_dom)], *w1)
     half = jax.ShapeDtypeStruct((rows, mesh_cols // 2), BF)
-    g, first, second = call(
+    sums = jax.ShapeDtypeStruct((rows, mesh_cols // 2), F32)
+    g_first, first, later = call(
         functools.partial(gather_kernel, n_dom),
-        out_shape=[jax.ShapeDtypeStruct((rows, mesh_cols), F32), half, half],
+        out_shape=[sums, half, half],
         in_specs=[full(SMEM)] + [full()] * (4 + len(w1) + len(w2)),
         out_specs=[full()] * 3,
         cost_estimate=cost(0.5),
         name="gather",
     )(at, acc, to_mesh, split_state, far, *w1, *w2)
+    g_second, second = call(
+        later_kernel,
+        out_shape=[sums, half],
+        in_specs=[full(SMEM)] + [full()] * (2 + len(w2)),
+        out_specs=[full()] * 2,
+        cost_estimate=cost(0.5),
+        name="later",
+    )(at, later, split_state, *w2)
 
     def other_feat(x):
         if n_feat == 2:
@@ -361,22 +377,22 @@
     *out, second = call(
         functools.partial(first_mesh_kernel, mesh_blocks, n_dom),
         out_shape=[thin] * n_dom + [half],
-        in_specs=[full(SMEM), full(SMEM)] + [full()] * 4,
+        in_specs=[full(SMEM), full(SMEM)] + [full()] * 5 + [anywhere()],
         out_specs=[full()] * (n_dom + 1),
         scratch_shapes=scratch,
         cost_estimate=cost(0.5),
         name="mesh",
-    )(at, send_mesh, g, other_feat(first), mw, second)
+    )(at, send_mesh, g_first, other_feat(first), mw, d1, second, to_grid)
     near_first = move(out, n_dom)
     out = call(
-        functools.partial(mesh_kernel, mesh_blocks, n_dom, 1),
+        functools.partial(mesh_kernel, mesh_blocks, n_dom),
         out_shape=[thin] * n_dom,
-        in_specs=[full(SMEM), full(SMEM)] + [full()] * 3,
+        in_specs=[full(SMEM), full(SMEM)] + [full()] * 4,
         out_specs=[full()] * n_dom,
         scratch_shapes=scratch,
         cost_estimate=cost(0.5),
         name="mesh",
-    )(at, send_mesh, g, other_feat(second), mw)
+    )(at, send_mesh, g_second, other_feat(second), mw, d1)
     near_second = move(out, n_dom)
     d2 = whole(call(
         hold_kernel,
@@ -387,25 +403,25 @@
         name="hold",
     )(out[0], dec_second))
     ordered = order_of(n_dom)
-    far_first = cross(join_kernel, near_first, to_grid, out[0], d2)
-    far_second = cross(join_kernel, near_second)
+    far_first, _ = cross(join_kernel, n_dom // 2, near_first, out[0], d2)
+    far_second, ready = cross(join_kernel, n_dom // 2, near_second)
     acc = call(
         functools.partial(collect_kernel, n_dom),
         out_shape=jax.ShapeDtypeStruct((rows, grid_cols), F32),
-        in_specs=[anywhere()] + [full()] * (2 + n_dom),
+        in_specs=[anywhere()] + [full()] * (2 + 2 * n_dom),
         out_specs=full(),
         cost_estimate=cost(0.5),
         name="collect",
-    )(near_second[ordered[-1]], to_grid, far_first, *[near_first[k] for k in ordered])
+    )(ready, to_grid, far_first, *[near_first[k] for k in ordered], *[near_second[k] for k in ordered])
     return call(
-        functools.partial(decode_kernel, n_dom, grid_cols // 2),
+        functools.partial(decode_kernel, n_dom, grid_cols // 3),
         out_shape=jax.ShapeDtypeStruct(grid_state.shape, BF),
-        in_specs=[full()] * (6 + n_dom),
+        in_specs=[full()] * 5,
         out_specs=anywhere(),
-        scratch_shapes=[VMEM((rows, grid_cols), BF), pltpu.SemaphoreType.DMA((2,))],
+        scratch_shapes=[VMEM((rows, grid_cols), BF), pltpu.SemaphoreType.DMA((3,))],
         cost_estimate=cost(3),
         name="decode",
-    )(acc, to_grid, d1, d2, grid_state, far_second, *[near_second[k] for k in ordered])
+    )(acc, to_grid, d2, grid_state, far_second)
 
 
 def solution(mesh):

time: 77.4 us -> 75.9 us (0.981)
  waiting for transfers between devices: 11.1 us -> 6.93 us
  Pallas kernels: 17 us -> 18 us
  blocking collectives: 22.1 us -> 23 us
    ppermute x2, waiting for transfers between devices: 6.86 us -> 2.94 us  [other_feat(): return lax.ppermute(x, 'feat', SWAP)]
    all_gather x3, blocking collectives: 22.1 us -> 23 us  [whole(): return lax.all_gather(w, 'feat', axis=0, tiled=True)]
    ppermute x3, waiting for transfers between devices: 1.41 us -> 0.61 us  [cross(): return (lax.ppermute(mine, 'sub', SWAP), mine)]
    pallas_call x3 -> x4, Pallas kernels: 6.99 us -> 6.96 us  [the longest x1 2.63 us: local(): call(functools.partial(decode_kernel, n_dom, grid_cols // 3), out_shape=j...]
  transfers between devices with their start and end apart: 16 -> 16, of which waited for: 4 -> 6; matrix products, arithmetic and copies ran while one was open for 0% -> 0% of each run, Pallas kernels for 13% -> 16%
where the time goes in v3:
time: 75.9 us; the launch traced here: 74.9 us
  blocking collectives  23 us (30%)
  starting transfers between devices  22 us (29%)
  Pallas kernels  18 us (24%)
  waiting for transfers between devices  6.93 us (9%)
  local copies, waits for them, and re-layouts  4.64 us (6%)
    all_gather x3, blocking collectives, whole(): return lax.all_gather(w, 'feat', axis=0, tiled=True)  23 us
    ppermute x9, starting transfers between devices, move(): lax.ppermute(chunks[k], 'dom', [(i, i ^ k) for i in range(n_dom)])  15.8 us
    unnamed x24, local copies, waits for them, and re-layouts  4.64 us
    pallas_call x1, Pallas kernels, local(): call(functools.partial(spread_kernel, n_dom, feeding), grid=(grid_blocks...  3.46 us
    ppermute x9, waiting for transfers between devices, move(): lax.ppermute(chunks[k], 'dom', [(i, i ^ k) for i in range(n_dom)])  3.38 us
    ppermute x2, starting transfers between devices, other_feat(): return lax.ppermute(x, 'feat', SWAP)  3.1 us
    ppermute x2, starting transfers between devices, rows_of(): return [w, lax.ppermute(w, 'feat', SWAP)] if n_feat == 2 else [whole(w)]  2.97 us
    ppermute x2, waiting for transfers between devices, other_feat(): return lax.ppermute(x, 'feat', SWAP)  2.94 us
  transfers between devices with their start and end apart: 16, of which 6 were waited for; matrix products, arithmetic and copies ran while one was open for 0% of the time, Pallas kernels for 16%

profile of v3, /device:TPU:0, one launch (start us, length us, event | category | flops | bytes accessed | tf_op | source)
XLA Modules:
  0.0 74.9 jit_solution(10619093977867459408)
XLA Ops:
  0.0 2.9 %collective-permute-start.3 = (bf16[256,512]{1,0:T(8,128)(2,1)}, bf16[256,512]{1,0:T(8,128)(2,1)S(1)}, u32[]{:S(2)}, u32[]{:S(2)}) collective-permute-start(bf16[256,512]{1,0:T(8,128)(2,1)} %rest_0_.2), channel_id=1, source_target_pairs={{0,2},{2,0},{1,3},{3,1},{4,6},{6,4},{5,7},{7,5},{8,10},{10,8},{9,1... | collective-permute-start | bytes 786440 | tf_op jit(solution)/shard_map/ppermute | solution.py:317
  2.9 0.0 collective-permute-start.4
  3.0 0.1 pad_add_fusion.at_ref
  3.1 1.4 %copy-done = bf16[512,1536]{1,0:T(8,128)(2,1)S(1)} copy-done((bf16[512,1536]{1,0:T(8,128)(2,1)S(1)}, bf16[512,1536]{1,0:T(8,128)(2,1)}, u32[]{:S(2)}) %copy-start) | copy-done | bytes 1572888
  4.5 0.7 copy-done.10
  5.1 1.7 %pack.1 = (bf16[2,512,128]{2,1,0:T(8,128)(2,1)S(1)}, bf16[2,512,128]{2,1,0:T(8,128)(2,1)S(1)}, bf16[2,512,128]{2,1,0:T(8,128)(2,1)S(1)}, bf16[2,512,128]{2,1,0:T(8,128)(2,1)S(1)}) custom-call(s32[3]{0:T(128)S(1)} %pad_add_fusion.at_ref, s32[2,8]{1,0:T(2,128)S(1)} %bitcast.16, bf16[512,1536]{1,0:T(8,128)(2,1)S(1)} %copy-done), custom_call_target="tpu_custom_call" | custom-call | flops 400000000 | bytes 1000000 | tf_op jit(solution)/shard_map/pack/pallas_call | solution.py:290
  6.8 0.0 copy-start.3
  6.8 3.2 %collective-permute-start = (bf16[2,512,128]{2,1,0:T(8,128)(2,1)S(1)}, bf16[2,512,128]{2,1,0:T(8,128)(2,1)S(1)}, u32[]{:S(2)}, u32[]{:S(2)}) collective-permute-start(bf16[2,512,128]{2,1,0:T(8,128)(2,1)S(1)} %get-tuple-element.27), channel_id=1, source_target_pairs={{0,8},{4,12},{8,0},{12,4},{1,9},{5,13},{9,1},{13,5},{2,10},{6,14},... | collective-permute-start | bytes 786440 | tf_op jit(solution)/shard_map/ppermute | solution.py:269
  10.0 1.3 %collective-permute-start.1 = (bf16[2,512,128]{2,1,0:T(8,128)(2,1)S(1)}, bf16[2,512,128]{2,1,0:T(8,128)(2,1)S(1)}, u32[]{:S(2)}, u32[]{:S(2)}) collective-permute-start(bf16[2,512,128]{2,1,0:T(8,128)(2,1)S(1)} %get-tuple-element.28), channel_id=1, source_target_pairs={{0,12},{4,8},{8,4},{12,0},{1,13},{5,9},{9,5},{13,1},{2,14},{6,10},... | collective-permute-start | bytes 786440 | tf_op jit(solution)/shard_map/ppermute | solution.py:269
  11.3 0.2 collective-permute-start.2
  11.6 0.9 %copy-done.5 = bf16[256,512]{1,0:T(8,128)(2,1)S(1)} copy-done((bf16[256,512]{1,0:T(8,128)(2,1)S(1)}, bf16[256,512]{1,0:T(8,128)(2,1)}, u32[]{:S(2)}) %copy-start.5) | copy-done | bytes 262168
  12.5 0.9 %copy-done.7 = bf16[1,1,64,1024]{3,2,1,0:T(8,128)(2,1)S(1)} copy-done((bf16[1,1,64,1024]{3,2,1,0:T(8,128)(2,1)S(1)}, bf16[1,1,64,1024]{3,2,1,0:T(8,128)(2,1)}, u32[]{:S(2)}) %copy-start.7) | copy-done | bytes 131096
  13.4 0.7 copy-done.11
  14.1 1.1 %scatter.1 = (bf16[2,512,512]{2,1,0:T(8,128)(2,1)S(1)}, bf16[256,512]{1,0:T(8,128)(2,1)S(1)}) custom-call(s32[3]{0:T(128)S(1)} %pad_add_fusion.at_ref, s32[16]{0:T(128)S(1)} %bitcast.17, bf16[64,1024]{1,0:T(8,128)(2,1)S(1)} %bitcast.12, bf16[256,512]{1,0:T(8,128)(2,1)S(1)} %copy-done.5), custom_call_target="tpu_custom_call" | custom-call | tf_op jit(solution)/shard_map/scatter/pallas_call | solution.py:320
  15.2 7.8 %all_gather.10.refs_7_.d1_ref = bf16[512,512]{1,0:T(8,128)(2,1)S(1)} all-gather(bf16[256,512]{1,0:T(8,128)(2,1)} %param.17), channel_id=1, replica_groups=mesh['ens'=2,'dom'=4,'feat'=2,'sub'=2] {'feat'}, dimensions={0}, use_global_device_ids=true | all-gather | bytes 786432 | tf_op jit(solution)/shard_map/all_gather | solution.py:303
  23.0 7.2 %all_gather.9.refs_6_.mw_ref = bf16[512,512]{1,0:T(8,128)(2,1)S(1)} all-gather(bf16[256,512]{1,0:T(8,128)(2,1)} %param.19), channel_id=1, replica_groups=mesh['ens'=2,'dom'=4,'feat'=2,'sub'=2] {'feat'}, dimensions={0}, use_global_device_ids=true | all-gather | bytes 786432 | tf_op jit(solution)/shard_map/all_gather | solution.py:303
  30.3 0.0 copy-start.2
  30.3 0.0 copy-start.4
  30.3 0.0 copy-start.9
  30.4 0.1 collective-permute-start.5
  30.4 1.4 %encode.1.acc_ref = f32[512,512]{1,0:T(8,128)S(1)} custom-call(s32[3]{0:T(128)S(1)} %pad_add_fusion.at_ref, bf16[2,512,512]{2,1,0:T(8,128)(2,1)S(1)} %get-tuple-element.25.wide_ref.refs_8_, bf16[2,512,128]{2,1,0:T(8,128)(2,1)S(1)} %get-tuple-element.26.rest_0_.refs_0_, bf16[2,512,128]{2,1,0:T(8,128)(2,1)S(1)} %collective-permute-done.rest_1_.refs_1_, ...), custom_call_target="tpu_custom_call" | custom-call | flops 200000000 | bytes 500000 | tf_op jit(solution)/shard_map/encode/pallas_call | solution.py:343
  31.8 0.5 collective-permute-done.5.far_ref
  32.3 1.7 %gather.1 = (f32[512,256]{1,0:T(8,128)S(1)}, bf16[512,256]{1,0:T(8,128)(2,1)S(1)}, bf16[512,256]{1,0:T(8,128)(2,1)S(1)}) custom-call(s32[3]{0:T(128)S(1)} %pad_add_fusion.at_ref, f32[512,512]{1,0:T(8,128)S(1)} %encode.1.acc_ref, bf16[2,512,512]{2,1,0:T(8,128)(2,1)S(1)} %get-tuple-element.25.wide_ref.refs_8_, bf16[256,512]{1,0:T(8,128)(2,1)S(1)} %get-tuple-element.30.ms_ref, ...), custom_call_target="tpu_custom_call" | custom-call | flops 200000000 | bytes 500000 | tf_op jit(solution)/shard_map/gather/pallas_call | solution.py:353
  34.0 0.0 copy-start.8
  34.0 1.5 %collective-permute-start.6 = (bf16[512,256]{1,0:T(8,128)(2,1)S(1)}, bf16[512,256]{1,0:T(8,128)(2,1)S(1)}, u32[]{:S(2)}, u32[]{:S(2)}) collective-permute-start(bf16[512,256]{1,0:T(8,128)(2,1)S(1)} %get-tuple-element.34), channel_id=1, source_target_pairs={{0,2},{2,0},{1,3},{3,1},{4,6},{6,4},{5,7},{7,5},{8,10},{10,8},{9,1... | collective-permute-start | bytes 786440 | tf_op jit(solution)/shard_map/ppermute | solution.py:372
  35.6 3.5 %spread.1.ready_ref.wide_ref = bf16[1024,1536]{1,0:T(8,128)(2,1)S(1)} custom-call(s32[3]{0:T(128)S(1)} %pad_add_fusion.at_ref, s32[4,24]{1,0:T(4,128)S(1)} %bitcast.15, bf16[24,64,256]{2,1,0:T(8,128)(2,1)S(1)} %copy-done.4), custom_call_target="tpu_custom_call" | custom-call | tf_op jit(solution)/shard_map/spread/pallas_call | solution.py:331
  39.0 0.9 %later.1 = (f32[512,256]{1,0:T(8,128)S(1)}, bf16[512,256]{1,0:T(8,128)(2,1)S(1)}) custom-call(s32[3]{0:T(128)S(1)} %pad_add_fusion.at_ref, bf16[512,256]{1,0:T(8,128)(2,1)S(1)} %get-tuple-element.31.total_ref, bf16[256,512]{1,0:T(8,128)(2,1)S(1)} %get-tuple-element.30.ms_ref, bf16[256,512]{1,0:T(8,128)(2,1)S(1)} %copy-done.2, ...), custom_call_target="tpu_custom_call" | custom-call | flops 200000000 | bytes 500000 | tf_op jit(solution)/shard_map/later/pallas_call | solution.py:361
  40.0 2.4 %collective-permute-done.6.other_ref = bf16[512,256]{1,0:T(8,128)(2,1)S(1)} collective-permute-done((bf16[512,256]{1,0:T(8,128)(2,1)S(1)}, bf16[512,256]{1,0:T(8,128)(2,1)S(1)}, u32[]{:S(2)}, u32[]{:S(2)}) %collective-permute-start.6) | collective-permute-done | bytes 262176 | tf_op jit(solution)/shard_map/ppermute | solution.py:372
  42.4 1.7 %mesh.2 = (bf16[512,128]{1,0:T(8,128)(2,1)S(1)}, bf16[512,128]{1,0:T(8,128)(2,1)S(1)}, bf16[512,128]{1,0:T(8,128)(2,1)S(1)}, bf16[512,128]{1,0:T(8,128)(2,1)S(1)}, bf16[512,256]{1,0:T(8,128)(2,1)S(1)}) custom-call(s32[3]{0:T(128)S(1)} %pad_add_fusion.at_ref, s32[2,8]{1,0:T(2,128)S(1)} %bitcast.13, f32[512,256]{1,0:T(8,128)S(1)} %get-tuple-element.33.g_ref, ...), custom_call_target="tpu_custom_call" | custom-call | flops 200000000 | bytes 500000 | tf_op jit(solution)/shard_map/mesh/pallas_call | solution.py:377
  44.2 1.5 %collective-permute-start.7 = (bf16[512,256]{1,0:T(8,128)(2,1)S(1)}, bf16[512,256]{1,0:T(8,128)(2,1)S(1)}, u32[]{:S(2)}, u32[]{:S(2)}) collective-permute-start(bf16[512,256]{1,0:T(8,128)(2,1)S(1)} %get-tuple-element.36), channel_id=1, source_target_pairs={{0,2},{2,0},{1,3},{3,1},{4,6},{6,4},{5,7},{7,5},{8,10},{10,8},{9,1... | collective-permute-start | bytes 786440 | tf_op jit(solution)/shard_map/ppermute | solution.py:372
  45.7 5.0 %collective-permute-start.11 = (bf16[512,128]{1,0:T(8,128)(2,1)S(1)}, bf16[512,128]{1,0:T(8,128)(2,1)S(1)}, u32[]{:S(2)}, u32[]{:S(2)}) collective-permute-start(bf16[512,128]{1,0:T(8,128)(2,1)S(1)} %get-tuple-element.42), channel_id=1, source_target_pairs={{0,8},{4,12},{8,0},{12,4},{1,9},{5,13},{9,1},{13,5},{2,10},{6,14},... | collective-permute-start | bytes 393224 | tf_op jit(solution)/shard_map/ppermute | solution.py:269
  50.7 0.4 collective-permute-start.12
  51.1 0.1 collective-permute-start.13
  51.3 0.5 collective-permute-done.7.other_ref
  51.8 1.7 %mesh.3 = (bf16[512,128]{1,0:T(8,128)(2,1)S(1)}, bf16[512,128]{1,0:T(8,128)(2,1)S(1)}, bf16[512,128]{1,0:T(8,128)(2,1)S(1)}, bf16[512,128]{1,0:T(8,128)(2,1)S(1)}) custom-call(s32[3]{0:T(128)S(1)} %pad_add_fusion.at_ref, s32[2,8]{1,0:T(2,128)S(1)} %bitcast.14, f32[512,256]{1,0:T(8,128)S(1)} %get-tuple-element.32.g_ref, ...), custom_call_target="tpu_custom_call" | custom-call | flops 200000000 | bytes 500000 | tf_op jit(solution)/shard_map/mesh/pallas_call | solution.py:387
  53.5 5.0 %collective-permute-start.8 = (bf16[512,128]{1,0:T(8,128)(2,1)S(1)}, bf16[512,128]{1,0:T(8,128)(2,1)S(1)}, u32[]{:S(2)}, u32[]{:S(2)}) collective-permute-start(bf16[512,128]{1,0:T(8,128)(2,1)S(1)} %get-tuple-element.38), channel_id=1, source_target_pairs={{0,8},{4,12},{8,0},{12,4},{1,9},{5,13},{9,1},{13,5},{2,10},{6,14},... | collective-permute-start | bytes 393224 | tf_op jit(solution)/shard_map/ppermute | solution.py:269
  58.5 0.4 collective-permute-start.9
  59.0 1.6 %collective-permute-done.11.refs_1_.rest_1_ = bf16[512,128]{1,0:T(8,128)(2,1)S(1)} collective-permute-done((bf16[512,128]{1,0:T(8,128)(2,1)S(1)}, bf16[512,128]{1,0:T(8,128)(2,1)S(1)}, u32[]{:S(2)}, u32[]{:S(2)}) %collective-permute-start.11) | collective-permute-done | bytes 131104 | tf_op jit(solution)/shard_map/ppermute | solution.py:269
  60.6 7.9 %all_gather.11.refs_5_.d2_ref = bf16[512,512]{1,0:T(8,128)(2,1)S(1)} all-gather(bf16[256,512]{1,0:T(8,128)(2,1)S(1)} %hold.1), channel_id=1, replica_groups=mesh['ens'=2,'dom'=4,'feat'=2,'sub'=2] {'feat'}, dimensions={0}, use_global_device_ids=true | all-gather | bytes 786432 | tf_op jit(solution)/shard_map/all_gather | solution.py:303
  68.6 0.1 stack.21
  68.7 0.1 collective-permute-start.14
  68.8 1.7 %collective-permute-done.8.refs_1_.rest_5_ = bf16[512,128]{1,0:T(8,128)(2,1)S(1)} collective-permute-done((bf16[512,128]{1,0:T(8,128)(2,1)S(1)}, bf16[512,128]{1,0:T(8,128)(2,1)S(1)}, u32[]{:S(2)}, u32[]{:S(2)}) %collective-permute-start.8) | collective-permute-done | bytes 131104 | tf_op jit(solution)/shard_map/ppermute | solution.py:269
  70.5 0.1 stack.20.ready_ref
  70.7 0.0 copy-start.1
  70.7 0.1 collective-permute-start.15
  70.8 1.4 %collect.1.acc_ref = f32[512,1536]{1,0:T(8,128)S(1)} custom-call(bf16[2,512,128]{2,1,0:T(8,128)(2,1)S(1)} %stack.20.ready_ref, bf16[1024,1536]{1,0:T(8,128)(2,1)S(1)} %spread.1.ready_ref.wide_ref, bf16[2,512,128]{2,1,0:T(8,128)(2,1)S(1)} %collective-permute-done.14.far_ref, bf16[512,128]{1,0:T(8,128)(2,1)S(1)} %get-tuple-element.41.refs_0_.rest_0_, ...), custom_call_target="tpu_custom_call" | custom-call | flops 200000000 | bytes 500000 | tf_op jit(solution)/shard_map/collect/pallas_call | solution.py:408
  72.2 0.1 collective-permute-done.15.far_ref
  72.3 2.6 %decode.1 = bf16[512,1536]{1,0:T(8,128)(2,1)} custom-call(f32[512,1536]{1,0:T(8,128)S(1)} %collect.1.acc_ref, bf16[1024,1536]{1,0:T(8,128)(2,1)S(1)} %spread.1.ready_ref.wide_ref, bf16[512,512]{1,0:T(8,128)(2,1)S(1)} %all_gather.11.refs_5_.d2_ref, bf16[512,1536]{1,0:T(8,128)(2,1)S(1)} %copy-done.1, bf16[2,512,128]{2,1,0:T(8,128)(2,1)S(1)} %collective-permute-done.15.far_ref), custom_call_target="tpu_custom_call" | custom-call | flops 1200000000 | bytes 3000000 | tf_op jit(solution)/shard_map/decode/pallas_call | solution.py:416
  (26 shorter events, 0.1 us)
Async XLA Ops:
  0.0 30.2 %collective-permute-start.3 = (bf16[256,512]{1,0:T(8,128)(2,1)}, bf16[256,512]{1,0:T(8,128)(2,1)S(1)}, u32[]{:S(2)}, u32[]{:S(2)}) collective-permute-start(bf16[256,512]{1,0:T(8,128)(2,1)} %rest_0_.2), channel_id=1, source_target_pairs={{0,2},{2,0},{1,3},{3,1},{4,6},{6,4},{5,7},{7,5},{8,10},{10,8},{9,1... | collective-permute-start | bytes 786440 | tf_op jit(solution)/shard_map/ppermute | solution.py:317
  2.9 27.3 %collective-permute-start.4 = (bf16[256,512]{1,0:T(8,128)(2,1)}, bf16[256,512]{1,0:T(8,128)(2,1)S(1)}, u32[]{:S(2)}, u32[]{:S(2)}) collective-permute-start(bf16[256,512]{1,0:T(8,128)(2,1)} %rest_0_.3), channel_id=1, source_target_pairs={{0,2},{2,0},{1,3},{3,1},{4,6},{6,4},{5,7},{7,5},{8,10},{10,8},{9,1... | collective-permute-start | bytes 786440 | tf_op jit(solution)/shard_map/ppermute | solution.py:317
  3.0 1.4 %copy-start = (bf16[512,1536]{1,0:T(8,128)(2,1)S(1)}, bf16[512,1536]{1,0:T(8,128)(2,1)}, u32[]{:S(2)}) copy-start(bf16[512,1536]{1,0:T(8,128)(2,1)} %grid_ref.1) | copy-start | bytes 4718596
  4.5 0.7 copy-start.10
  6.8 23.6 %copy-start.3 = (bf16[256,512]{1,0:T(8,128)(2,1)S(1)}, bf16[256,512]{1,0:T(8,128)(2,1)}, u32[]{:S(2)}) copy-start(bf16[256,512]{1,0:T(8,128)(2,1)} %rest_0_.2) | copy-start | bytes 786436
  6.8 23.4 %collective-permute-start = (bf16[2,512,128]{2,1,0:T(8,128)(2,1)S(1)}, bf16[2,512,128]{2,1,0:T(8,128)(2,1)S(1)}, u32[]{:S(2)}, u32[]{:S(2)}) collective-permute-start(bf16[2,512,128]{2,1,0:T(8,128)(2,1)S(1)} %get-tuple-element.27), channel_id=1, source_target_pairs={{0,8},{4,12},{8,0},{12,4},{1,9},{5,13},{9,1},{13,5},{2,10},{6,14},... | collective-permute-start | bytes 786440 | tf_op jit(solution)/shard_map/ppermute | solution.py:269
  10.0 20.3 %collective-permute-start.1 = (bf16[2,512,128]{2,1,0:T(8,128)(2,1)S(1)}, bf16[2,512,128]{2,1,0:T(8,128)(2,1)S(1)}, u32[]{:S(2)}, u32[]{:S(2)}) collective-permute-start(bf16[2,512,128]{2,1,0:T(8,128)(2,1)S(1)} %get-tuple-element.28), channel_id=1, source_target_pairs={{0,12},{4,8},{8,4},{12,0},{1,13},{5,9},{9,5},{13,1},{2,14},{6,10},... | collective-permute-start | bytes 786440 | tf_op jit(solution)/shard_map/ppermute | solution.py:269
  11.3 19.0 %collective-permute-start.2 = (bf16[2,512,128]{2,1,0:T(8,128)(2,1)S(1)}, bf16[2,512,128]{2,1,0:T(8,128)(2,1)S(1)}, u32[]{:S(2)}, u32[]{:S(2)}) collective-permute-start(bf16[2,512,128]{2,1,0:T(8,128)(2,1)S(1)} %get-tuple-element.29), channel_id=1, source_target_pairs={{0,4},{4,0},{8,12},{12,8},{1,5},{5,1},{9,13},{13,9},{2,6},{6,2},{1... | collective-permute-start | bytes 786440 | tf_op jit(solution)/shard_map/ppermute | solution.py:269
  11.6 0.9 %copy-start.5 = (bf16[256,512]{1,0:T(8,128)(2,1)S(1)}, bf16[256,512]{1,0:T(8,128)(2,1)}, u32[]{:S(2)}) copy-start(bf16[256,512]{1,0:T(8,128)(2,1)} %ms_ref.1) | copy-start | bytes 786436
  12.5 0.9 %copy-start.7 = (bf16[1,1,64,1024]{3,2,1,0:T(8,128)(2,1)S(1)}, bf16[1,1,64,1024]{3,2,1,0:T(8,128)(2,1)}, u32[]{:S(2)}) copy-start(bf16[1,1,64,1024]{3,2,1,0:T(8,128)(2,1)} %param.21) | copy-start | bytes 393220
  13.4 0.7 copy-start.11
  30.3 2.1 %copy-start.2 = (bf16[256,512]{1,0:T(8,128)(2,1)S(1)}, bf16[256,512]{1,0:T(8,128)(2,1)}, u32[]{:S(2)}) copy-start(bf16[256,512]{1,0:T(8,128)(2,1)} %rest_0_.3) | copy-start | bytes 786436
  30.3 5.2 %copy-start.4 = (bf16[24,64,256]{2,1,0:T(8,128)(2,1)S(1)}, bf16[24,64,256]{2,1,0:T(8,128)(2,1)}, u32[]{:S(2)}) copy-start(bf16[24,64,256]{2,1,0:T(8,128)(2,1)} %tiles_ref.1) | copy-start | bytes 2359300
  30.3 5.2 %copy-start.9 = (s32[24,4]{0,1:T(4,128)S(1)}, s32[24,4]{0,1:T(4,128)}, u32[]{:S(2)}) copy-start(s32[24,4]{0,1:T(4,128)} %param.24) | copy-start | bytes 1156
  30.4 2.0 %collective-permute-start.5 = (bf16[4,512,128]{2,1,0:T(8,128)(2,1)S(1)}, bf16[4,512,128]{2,1,0:T(8,128)(2,1)S(1)}, u32[]{:S(2)}, u32[]{:S(2)}) collective-permute-start(bf16[4,512,128]{2,1,0:T(8,128)(2,1)S(1)} %stack.19), channel_id=1, source_target_pairs={{0,1},{1,0},{2,3},{3,2},{4,5},{5,4},{6,7},{7,6},{8,9},{9,8},{10,11... | collective-permute-start | bytes 1572872 | tf_op jit(solution)/shard_map/ppermute | solution.py:314
  34.0 8.4 %copy-start.8 = (s32[1,1,8,2]{2,3,1,0:T(2,128)S(1)}, s32[1,1,8,2]{2,3,1,0:T(2,128)}, u32[]{:S(2)}) copy-start(s32[1,1,8,2]{2,3,1,0:T(2,128)} %param.23) | copy-start | bytes 196
  34.0 8.4 %collective-permute-start.6 = (bf16[512,256]{1,0:T(8,128)(2,1)S(1)}, bf16[512,256]{1,0:T(8,128)(2,1)S(1)}, u32[]{:S(2)}, u32[]{:S(2)}) collective-permute-start(bf16[512,256]{1,0:T(8,128)(2,1)S(1)} %get-tuple-element.34), channel_id=1, source_target_pairs={{0,2},{2,0},{1,3},{3,1},{4,6},{6,4},{5,7},{7,5},{8,10},{10,8},{9,1... | collective-permute-start | bytes 786440 | tf_op jit(solution)/shard_map/ppermute | solution.py:372
  42.4 16.6 %copy-start.6 = (bf16[256,512]{1,0:T(8,128)(2,1)S(1)}, bf16[256,512]{1,0:T(8,128)(2,1)}, u32[]{:S(2)}) copy-start(bf16[256,512]{1,0:T(8,128)(2,1)} %x_ref.1) | copy-start | bytes 786436
  44.2 7.6 %collective-permute-start.7 = (bf16[512,256]{1,0:T(8,128)(2,1)S(1)}, bf16[512,256]{1,0:T(8,128)(2,1)S(1)}, u32[]{:S(2)}, u32[]{:S(2)}) collective-permute-start(bf16[512,256]{1,0:T(8,128)(2,1)S(1)} %get-tuple-element.36), channel_id=1, source_target_pairs={{0,2},{2,0},{1,3},{3,1},{4,6},{6,4},{5,7},{7,5},{8,10},{10,8},{9,1... | collective-permute-start | bytes 786440 | tf_op jit(solution)/shard_map/ppermute | solution.py:372
  45.7 14.9 %collective-permute-start.11 = (bf16[512,128]{1,0:T(8,128)(2,1)S(1)}, bf16[512,128]{1,0:T(8,128)(2,1)S(1)}, u32[]{:S(2)}, u32[]{:S(2)}) collective-permute-start(bf16[512,128]{1,0:T(8,128)(2,1)S(1)} %get-tuple-element.42), channel_id=1, source_target_pairs={{0,8},{4,12},{8,0},{12,4},{1,9},{5,13},{9,1},{13,5},{2,10},{6,14},... | collective-permute-start | bytes 393224 | tf_op jit(solution)/shard_map/ppermute | solution.py:269
  50.7 17.9 %collective-permute-start.12 = (bf16[512,128]{1,0:T(8,128)(2,1)S(1)}, bf16[512,128]{1,0:T(8,128)(2,1)S(1)}, u32[]{:S(2)}, u32[]{:S(2)}) collective-permute-start(bf16[512,128]{1,0:T(8,128)(2,1)S(1)} %get-tuple-element.43), channel_id=1, source_target_pairs={{0,12},{4,8},{8,4},{12,0},{1,13},{5,9},{9,5},{13,1},{2,14},{6,10},... | collective-permute-start | bytes 393224 | tf_op jit(solution)/shard_map/ppermute | solution.py:269
  51.1 17.4 %collective-permute-start.13 = (bf16[512,128]{1,0:T(8,128)(2,1)S(1)}, bf16[512,128]{1,0:T(8,128)(2,1)S(1)}, u32[]{:S(2)}, u32[]{:S(2)}) collective-permute-start(bf16[512,128]{1,0:T(8,128)(2,1)S(1)} %get-tuple-element.44), channel_id=1, source_target_pairs={{0,4},{4,0},{8,12},{12,8},{1,5},{5,1},{9,13},{13,9},{2,6},{6,2},{1... | collective-permute-start | bytes 393224 | tf_op jit(solution)/shard_map/ppermute | solution.py:269
  53.5 17.0 %collective-permute-start.8 = (bf16[512,128]{1,0:T(8,128)(2,1)S(1)}, bf16[512,128]{1,0:T(8,128)(2,1)S(1)}, u32[]{:S(2)}, u32[]{:S(2)}) collective-permute-start(bf16[512,128]{1,0:T(8,128)(2,1)S(1)} %get-tuple-element.38), channel_id=1, source_target_pairs={{0,8},{4,12},{8,0},{12,4},{1,9},{5,13},{9,1},{13,5},{2,10},{6,14},... | collective-permute-start | bytes 393224 | tf_op jit(solution)/shard_map/ppermute | solution.py:269
  58.5 12.0 %collective-permute-start.9 = (bf16[512,128]{1,0:T(8,128)(2,1)S(1)}, bf16[512,128]{1,0:T(8,128)(2,1)S(1)}, u32[]{:S(2)}, u32[]{:S(2)}) collective-permute-start(bf16[512,128]{1,0:T(8,128)(2,1)S(1)} %get-tuple-element.39), channel_id=1, source_target_pairs={{0,12},{4,8},{8,4},{12,0},{1,13},{5,9},{9,5},{13,1},{2,14},{6,10},... | collective-permute-start | bytes 393224 | tf_op jit(solution)/shard_map/ppermute | solution.py:269
  60.6 9.9 %collective-permute-start.10 = (bf16[512,128]{1,0:T(8,128)(2,1)S(1)}, bf16[512,128]{1,0:T(8,128)(2,1)S(1)}, u32[]{:S(2)}, u32[]{:S(2)}) collective-permute-start(bf16[512,128]{1,0:T(8,128)(2,1)S(1)} %get-tuple-element.40), channel_id=1, source_target_pairs={{0,4},{4,0},{8,12},{12,8},{1,5},{5,1},{9,13},{13,9},{2,6},{6,2},{1... | collective-permute-start | bytes 393224 | tf_op jit(solution)/shard_map/ppermute | solution.py:269
  68.7 2.1 %collective-permute-start.14 = (bf16[2,512,128]{2,1,0:T(8,128)(2,1)S(1)}, bf16[2,512,128]{2,1,0:T(8,128)(2,1)S(1)}, u32[]{:S(2)}, u32[]{:S(2)}) collective-permute-start(bf16[2,512,128]{2,1,0:T(8,128)(2,1)S(1)} %stack.21), channel_id=1, source_target_pairs={{0,1},{1,0},{2,3},{3,2},{4,5},{5,4},{6,7},{7,6},{8,9},{9,8},{10,11... | collective-permute-start | bytes 786440 | tf_op jit(solution)/shard_map/ppermute | solution.py:314
  70.7 1.6 %copy-start.1 = (bf16[512,1536]{1,0:T(8,128)(2,1)S(1)}, bf16[512,1536]{1,0:T(8,128)(2,1)}, u32[]{:S(2)}) copy-start(bf16[512,1536]{1,0:T(8,128)(2,1)} %grid_ref.1) | copy-start | bytes 4718596
  70.7 1.6 %collective-permute-start.15 = (bf16[2,512,128]{2,1,0:T(8,128)(2,1)S(1)}, bf16[2,512,128]{2,1,0:T(8,128)(2,1)S(1)}, u32[]{:S(2)}, u32[]{:S(2)}) collective-permute-start(bf16[2,512,128]{2,1,0:T(8,128)(2,1)S(1)} %stack.20.ready_ref), channel_id=1, source_target_pairs={{0,1},{1,0},{2,3},{3,2},{4,5},{5,4},{6,7},{7,6},{8,9},{9,8},{10,11... | collective-permute-start | bytes 786440 | tf_op jit(solution)/shard_map/ppermute | solution.py:314

commit v4 on v3

--- a/solution.py
+++ b/solution.py
@@ -75,11 +75,19 @@
 
 
 def pack_kernel(blocks, n_dom, at_ref, send_ref, src_ref, *refs):
-    outs, buf = refs[:n_dom], refs[n_dom]
+    outs, src, buf, sems = refs[:n_dom], refs[n_dom], refs[n_dom + 1], refs[n_dom + 2]
     rows, cols = src_ref.shape
+    parts = 4
+    step = rows // parts
+    copies = []
+    for i in range(parts):
+        here = pl.ds(i * step, step)
+        copies.append(pltpu.make_async_copy(src_ref.at[here, :], src.at[here, :], sems.at[i]))
+        copies[i].start()
     buf[0, :, cols:] = jnp.zeros((rows, buf.shape[2] - cols), BF)
-    for i in range(4):
-        pack_rows(rows // 4, blocks, n_dom, at_ref, send_ref, src_ref, buf, i, outs)
+    for i in range(parts):
+        copies[i].wait()
+        pack_rows(step, blocks, n_dom, at_ref, send_ref, src, buf, i, outs)
 
 
 def stack_kernel(n_dom, waits, *refs):
@@ -290,11 +298,11 @@
     out = pl.pallas_call(
         functools.partial(pack_kernel, grid_blocks, n_dom),
         out_shape=[chunk] * n_dom,
-        in_specs=[full(SMEM), full(SMEM), full()],
+        in_specs=[full(SMEM), full(SMEM), anywhere()],
         out_specs=[full()] * n_dom,
-        scratch_shapes=[VMEM((2, rows, grid_cols + pair), BF)],
+        scratch_shapes=[VMEM((rows, grid_cols), BF), VMEM((2, rows, grid_cols + pair), BF), pltpu.SemaphoreType.DMA((4,))],
         cost_estimate=cost(1),
-        compiler_params=params(12),
+        compiler_params=params(52),
         name="pack",
     )(at, send_grid, grid_state)
     near = move(out, n_dom)

time: 75.9 us -> 75.4 us (level)
  local copies, waits for them, and re-layouts: 4.64 us -> 3.23 us
  Pallas kernels: 18 us -> 19 us
    unnamed x24 -> x22, local copies, waits for them, and re-layouts: 4.64 us -> 3.23 us
    pallas_call x1, Pallas kernels: 1.66 us -> 2.64 us  [local(): pl.pallas_call(functools.partial(pack_kernel, grid_blocks, n_dom), out_sh...]
  transfers between devices with their start and end apart: 16 -> 16, of which waited for: 6 -> 6; matrix products, arithmetic and copies ran while one was open for 0% -> 0% of each run, Pallas kernels for 16% -> 17%
where the time goes in v4:
time: 75.4 us; the launch traced here: 74.5 us
  blocking collectives  23 us (31%)
  starting transfers between devices  22.1 us (29%)
  Pallas kernels  19 us (25%)
  waiting for transfers between devices  6.89 us (9%)
  local copies, waits for them, and re-layouts  3.23 us (4%)
    all_gather x3, blocking collectives, whole(): return lax.all_gather(w, 'feat', axis=0, tiled=True)  23 us
    ppermute x9, starting transfers between devices, move(): lax.ppermute(chunks[k], 'dom', [(i, i ^ k) for i in range(n_dom)])  15.7 us
    pallas_call x1, Pallas kernels, local(): call(functools.partial(spread_kernel, n_dom, feeding), grid=(grid_blocks...  3.46 us
    ppermute x9, waiting for transfers between devices, move(): lax.ppermute(chunks[k], 'dom', [(i, i ^ k) for i in range(n_dom)])  3.35 us
    unnamed x22, local copies, waits for them, and re-layouts  3.23 us
    ppermute x2, starting transfers between devices, other_feat(): return lax.ppermute(x, 'feat', SWAP)  3.12 us
    ppermute x2, starting transfers between devices, rows_of(): return [w, lax.ppermute(w, 'feat', SWAP)] if n_feat == 2 else [whole(w)]  2.97 us
    ppermute x2, waiting for transfers between devices, other_feat(): return lax.ppermute(x, 'feat', SWAP)  2.93 us
  transfers between devices with their start and end apart: 16, of which 6 were waited for; matrix products, arithmetic and copies ran while one was open for 0% of the time, Pallas kernels for 17%

profile of v4, /device:TPU:0, one launch (start us, length us, event | category | flops | bytes accessed | tf_op | source)
XLA Modules:
  0.0 74.5 jit_solution(13001468876612181133)
XLA Ops:
  0.0 2.9 %collective-permute-start.3 = (bf16[256,512]{1,0:T(8,128)(2,1)}, bf16[256,512]{1,0:T(8,128)(2,1)S(1)}, u32[]{:S(2)}, u32[]{:S(2)}) collective-permute-start(bf16[256,512]{1,0:T(8,128)(2,1)} %rest_0_.2), channel_id=1, source_target_pairs={{0,2},{2,0},{1,3},{3,1},{4,6},{6,4},{5,7},{7,5},{8,10},{10,8},{9,1... | collective-permute-start | bytes 786440 | tf_op jit(solution)/shard_map/ppermute | solution.py:325
  2.9 0.0 collective-permute-start.4
  3.0 0.1 pad_add_fusion.at_ref
  3.1 0.7 copy-done.9
  3.7 2.6 %pack.1 = (bf16[2,512,128]{2,1,0:T(8,128)(2,1)S(1)}, bf16[2,512,128]{2,1,0:T(8,128)(2,1)S(1)}, bf16[2,512,128]{2,1,0:T(8,128)(2,1)S(1)}, bf16[2,512,128]{2,1,0:T(8,128)(2,1)S(1)}) custom-call(s32[3]{0:T(128)S(1)} %pad_add_fusion.at_ref, s32[2,8]{1,0:T(2,128)S(1)} %bitcast.16, bf16[512,1536]{1,0:T(8,128)(2,1)} %grid_ref.1), custom_call_target="tpu_custom_call" | custom-call | flops 400000000 | bytes 1000000 | tf_op jit(solution)/shard_map/pack/pallas_call | solution.py:298
  6.4 0.0 copy-start.2
  6.4 3.2 %collective-permute-start = (bf16[2,512,128]{2,1,0:T(8,128)(2,1)S(1)}, bf16[2,512,128]{2,1,0:T(8,128)(2,1)S(1)}, u32[]{:S(2)}, u32[]{:S(2)}) collective-permute-start(bf16[2,512,128]{2,1,0:T(8,128)(2,1)S(1)} %get-tuple-element.27), channel_id=1, source_target_pairs={{0,8},{4,12},{8,0},{12,4},{1,9},{5,13},{9,1},{13,5},{2,10},{6,14},... | collective-permute-start | bytes 786440 | tf_op jit(solution)/shard_map/ppermute | solution.py:277
  9.5 1.3 %collective-permute-start.1 = (bf16[2,512,128]{2,1,0:T(8,128)(2,1)S(1)}, bf16[2,512,128]{2,1,0:T(8,128)(2,1)S(1)}, u32[]{:S(2)}, u32[]{:S(2)}) collective-permute-start(bf16[2,512,128]{2,1,0:T(8,128)(2,1)S(1)} %get-tuple-element.28), channel_id=1, source_target_pairs={{0,12},{4,8},{8,4},{12,0},{1,13},{5,9},{9,5},{13,1},{2,14},{6,10},... | collective-permute-start | bytes 786440 | tf_op jit(solution)/shard_map/ppermute | solution.py:277
  10.9 0.2 collective-permute-start.2
  11.1 0.9 %copy-done.4 = bf16[256,512]{1,0:T(8,128)(2,1)S(1)} copy-done((bf16[256,512]{1,0:T(8,128)(2,1)S(1)}, bf16[256,512]{1,0:T(8,128)(2,1)}, u32[]{:S(2)}) %copy-start.4) | copy-done | bytes 262168
  12.1 0.9 %copy-done.6 = bf16[1,1,64,1024]{3,2,1,0:T(8,128)(2,1)S(1)} copy-done((bf16[1,1,64,1024]{3,2,1,0:T(8,128)(2,1)S(1)}, bf16[1,1,64,1024]{3,2,1,0:T(8,128)(2,1)}, u32[]{:S(2)}) %copy-start.6) | copy-done | bytes 131096
  13.0 0.7 copy-done.10
  13.6 1.1 %scatter.1 = (bf16[2,512,512]{2,1,0:T(8,128)(2,1)S(1)}, bf16[256,512]{1,0:T(8,128)(2,1)S(1)}) custom-call(s32[3]{0:T(128)S(1)} %pad_add_fusion.at_ref, s32[16]{0:T(128)S(1)} %bitcast.17, bf16[64,1024]{1,0:T(8,128)(2,1)S(1)} %bitcast.12, bf16[256,512]{1,0:T(8,128)(2,1)S(1)} %copy-done.4), custom_call_target="tpu_custom_call" | custom-call | tf_op jit(solution)/shard_map/scatter/pallas_call | solution.py:328
  14.7 7.8 %all_gather.10.refs_7_.d1_ref = bf16[512,512]{1,0:T(8,128)(2,1)S(1)} all-gather(bf16[256,512]{1,0:T(8,128)(2,1)} %param.17), channel_id=1, replica_groups=mesh['ens'=2,'dom'=4,'feat'=2,'sub'=2] {'feat'}, dimensions={0}, use_global_device_ids=true | all-gather | bytes 786432 | tf_op jit(solution)/shard_map/all_gather | solution.py:311
  22.6 7.2 %all_gather.9.refs_6_.mw_ref = bf16[512,512]{1,0:T(8,128)(2,1)S(1)} all-gather(bf16[256,512]{1,0:T(8,128)(2,1)} %param.19), channel_id=1, replica_groups=mesh['ens'=2,'dom'=4,'feat'=2,'sub'=2] {'feat'}, dimensions={0}, use_global_device_ids=true | all-gather | bytes 786432 | tf_op jit(solution)/shard_map/all_gather | solution.py:311
  29.8 0.0 collective-permute-done.rest_1_.refs_1_
  29.8 0.0 copy-start.1
  29.9 0.0 copy-start.3
  29.9 0.0 copy-start.8
  29.9 0.1 collective-permute-start.5
  30.0 1.4 %encode.1.acc_ref = f32[512,512]{1,0:T(8,128)S(1)} custom-call(s32[3]{0:T(128)S(1)} %pad_add_fusion.at_ref, bf16[2,512,512]{2,1,0:T(8,128)(2,1)S(1)} %get-tuple-element.25.wide_ref.refs_8_, bf16[2,512,128]{2,1,0:T(8,128)(2,1)S(1)} %get-tuple-element.26.rest_0_.refs_0_, bf16[2,512,128]{2,1,0:T(8,128)(2,1)S(1)} %collective-permute-done.rest_1_.refs_1_, ...), custom_call_target="tpu_custom_call" | custom-call | flops 200000000 | bytes 500000 | tf_op jit(solution)/shard_map/encode/pallas_call | solution.py:351
  31.4 0.5 collective-permute-done.5.far_ref
  31.9 1.7 %gather.1 = (f32[512,256]{1,0:T(8,128)S(1)}, bf16[512,256]{1,0:T(8,128)(2,1)S(1)}, bf16[512,256]{1,0:T(8,128)(2,1)S(1)}) custom-call(s32[3]{0:T(128)S(1)} %pad_add_fusion.at_ref, f32[512,512]{1,0:T(8,128)S(1)} %encode.1.acc_ref, bf16[2,512,512]{2,1,0:T(8,128)(2,1)S(1)} %get-tuple-element.25.wide_ref.refs_8_, bf16[256,512]{1,0:T(8,128)(2,1)S(1)} %get-tuple-element.30.ms_ref, ...), custom_call_target="tpu_custom_call" | custom-call | flops 200000000 | bytes 500000 | tf_op jit(solution)/shard_map/gather/pallas_call | solution.py:361
  33.6 0.0 copy-start.7
  33.6 1.6 %collective-permute-start.6 = (bf16[512,256]{1,0:T(8,128)(2,1)S(1)}, bf16[512,256]{1,0:T(8,128)(2,1)S(1)}, u32[]{:S(2)}, u32[]{:S(2)}) collective-permute-start(bf16[512,256]{1,0:T(8,128)(2,1)S(1)} %get-tuple-element.34), channel_id=1, source_target_pairs={{0,2},{2,0},{1,3},{3,1},{4,6},{6,4},{5,7},{7,5},{8,10},{10,8},{9,1... | collective-permute-start | bytes 786440 | tf_op jit(solution)/shard_map/ppermute | solution.py:380
  35.1 3.5 %spread.1.ready_ref.wide_ref = bf16[1024,1536]{1,0:T(8,128)(2,1)S(1)} custom-call(s32[3]{0:T(128)S(1)} %pad_add_fusion.at_ref, s32[4,24]{1,0:T(4,128)S(1)} %bitcast.15, bf16[24,64,256]{2,1,0:T(8,128)(2,1)S(1)} %copy-done.3), custom_call_target="tpu_custom_call" | custom-call | tf_op jit(solution)/shard_map/spread/pallas_call | solution.py:339
  38.6 0.9 %later.1 = (f32[512,256]{1,0:T(8,128)S(1)}, bf16[512,256]{1,0:T(8,128)(2,1)S(1)}) custom-call(s32[3]{0:T(128)S(1)} %pad_add_fusion.at_ref, bf16[512,256]{1,0:T(8,128)(2,1)S(1)} %get-tuple-element.31.total_ref, bf16[256,512]{1,0:T(8,128)(2,1)S(1)} %get-tuple-element.30.ms_ref, bf16[256,512]{1,0:T(8,128)(2,1)S(1)} %copy-done.1, ...), custom_call_target="tpu_custom_call" | custom-call | flops 200000000 | bytes 500000 | tf_op jit(solution)/shard_map/later/pallas_call | solution.py:369
  39.6 2.4 %collective-permute-done.6.other_ref = bf16[512,256]{1,0:T(8,128)(2,1)S(1)} collective-permute-done((bf16[512,256]{1,0:T(8,128)(2,1)S(1)}, bf16[512,256]{1,0:T(8,128)(2,1)S(1)}, u32[]{:S(2)}, u32[]{:S(2)}) %collective-permute-start.6) | collective-permute-done | bytes 262176 | tf_op jit(solution)/shard_map/ppermute | solution.py:380
  42.0 1.7 %mesh.2 = (bf16[512,128]{1,0:T(8,128)(2,1)S(1)}, bf16[512,128]{1,0:T(8,128)(2,1)S(1)}, bf16[512,128]{1,0:T(8,128)(2,1)S(1)}, bf16[512,128]{1,0:T(8,128)(2,1)S(1)}, bf16[512,256]{1,0:T(8,128)(2,1)S(1)}) custom-call(s32[3]{0:T(128)S(1)} %pad_add_fusion.at_ref, s32[2,8]{1,0:T(2,128)S(1)} %bitcast.13, f32[512,256]{1,0:T(8,128)S(1)} %get-tuple-element.33.g_ref, ...), custom_call_target="tpu_custom_call" | custom-call | flops 200000000 | bytes 500000 | tf_op jit(solution)/shard_map/mesh/pallas_call | solution.py:385
  43.7 1.6 %collective-permute-start.7 = (bf16[512,256]{1,0:T(8,128)(2,1)S(1)}, bf16[512,256]{1,0:T(8,128)(2,1)S(1)}, u32[]{:S(2)}, u32[]{:S(2)}) collective-permute-start(bf16[512,256]{1,0:T(8,128)(2,1)S(1)} %get-tuple-element.36), channel_id=1, source_target_pairs={{0,2},{2,0},{1,3},{3,1},{4,6},{6,4},{5,7},{7,5},{8,10},{10,8},{9,1... | collective-permute-start | bytes 786440 | tf_op jit(solution)/shard_map/ppermute | solution.py:380
  45.3 5.0 %collective-permute-start.11 = (bf16[512,128]{1,0:T(8,128)(2,1)S(1)}, bf16[512,128]{1,0:T(8,128)(2,1)S(1)}, u32[]{:S(2)}, u32[]{:S(2)}) collective-permute-start(bf16[512,128]{1,0:T(8,128)(2,1)S(1)} %get-tuple-element.42), channel_id=1, source_target_pairs={{0,8},{4,12},{8,0},{12,4},{1,9},{5,13},{9,1},{13,5},{2,10},{6,14},... | collective-permute-start | bytes 393224 | tf_op jit(solution)/shard_map/ppermute | solution.py:277
  50.3 0.4 collective-permute-start.12
  50.7 0.1 collective-permute-start.13
  50.8 0.5 collective-permute-done.7.other_ref
  51.3 1.7 %mesh.3 = (bf16[512,128]{1,0:T(8,128)(2,1)S(1)}, bf16[512,128]{1,0:T(8,128)(2,1)S(1)}, bf16[512,128]{1,0:T(8,128)(2,1)S(1)}, bf16[512,128]{1,0:T(8,128)(2,1)S(1)}) custom-call(s32[3]{0:T(128)S(1)} %pad_add_fusion.at_ref, s32[2,8]{1,0:T(2,128)S(1)} %bitcast.14, f32[512,256]{1,0:T(8,128)S(1)} %get-tuple-element.32.g_ref, ...), custom_call_target="tpu_custom_call" | custom-call | flops 200000000 | bytes 500000 | tf_op jit(solution)/shard_map/mesh/pallas_call | solution.py:395
  53.1 5.0 %collective-permute-start.8 = (bf16[512,128]{1,0:T(8,128)(2,1)S(1)}, bf16[512,128]{1,0:T(8,128)(2,1)S(1)}, u32[]{:S(2)}, u32[]{:S(2)}) collective-permute-start(bf16[512,128]{1,0:T(8,128)(2,1)S(1)} %get-tuple-element.38), channel_id=1, source_target_pairs={{0,8},{4,12},{8,0},{12,4},{1,9},{5,13},{9,1},{13,5},{2,10},{6,14},... | collective-permute-start | bytes 393224 | tf_op jit(solution)/shard_map/ppermute | solution.py:277
  58.1 0.5 collective-permute-start.9
  58.6 1.6 %collective-permute-done.11.refs_1_.rest_1_ = bf16[512,128]{1,0:T(8,128)(2,1)S(1)} collective-permute-done((bf16[512,128]{1,0:T(8,128)(2,1)S(1)}, bf16[512,128]{1,0:T(8,128)(2,1)S(1)}, u32[]{:S(2)}, u32[]{:S(2)}) %collective-permute-start.11) | collective-permute-done | bytes 131104 | tf_op jit(solution)/shard_map/ppermute | solution.py:277
  60.2 8.0 %all_gather.11.refs_5_.d2_ref = bf16[512,512]{1,0:T(8,128)(2,1)S(1)} all-gather(bf16[256,512]{1,0:T(8,128)(2,1)S(1)} %hold.1), channel_id=1, replica_groups=mesh['ens'=2,'dom'=4,'feat'=2,'sub'=2] {'feat'}, dimensions={0}, use_global_device_ids=true | all-gather | bytes 786432 | tf_op jit(solution)/shard_map/all_gather | solution.py:311
  68.2 0.1 stack.21
  68.3 0.1 collective-permute-start.14
  68.4 1.7 %collective-permute-done.8.refs_1_.rest_5_ = bf16[512,128]{1,0:T(8,128)(2,1)S(1)} collective-permute-done((bf16[512,128]{1,0:T(8,128)(2,1)S(1)}, bf16[512,128]{1,0:T(8,128)(2,1)S(1)}, u32[]{:S(2)}, u32[]{:S(2)}) %collective-permute-start.8) | collective-permute-done | bytes 131104 | tf_op jit(solution)/shard_map/ppermute | solution.py:277
  70.1 0.1 stack.20.ready_ref
  70.3 0.0 copy-start
  70.3 0.1 collective-permute-start.15
  70.4 1.4 %collect.1.acc_ref = f32[512,1536]{1,0:T(8,128)S(1)} custom-call(bf16[2,512,128]{2,1,0:T(8,128)(2,1)S(1)} %stack.20.ready_ref, bf16[1024,1536]{1,0:T(8,128)(2,1)S(1)} %spread.1.ready_ref.wide_ref, bf16[2,512,128]{2,1,0:T(8,128)(2,1)S(1)} %collective-permute-done.14.far_ref, bf16[512,128]{1,0:T(8,128)(2,1)S(1)} %get-tuple-element.41.refs_0_.rest_0_, ...), custom_call_target="tpu_custom_call" | custom-call | flops 200000000 | bytes 500000 | tf_op jit(solution)/shard_map/collect/pallas_call | solution.py:416
  71.8 0.1 collective-permute-done.15.far_ref
  71.9 2.6 %decode.1 = bf16[512,1536]{1,0:T(8,128)(2,1)} custom-call(f32[512,1536]{1,0:T(8,128)S(1)} %collect.1.acc_ref, bf16[1024,1536]{1,0:T(8,128)(2,1)S(1)} %spread.1.ready_ref.wide_ref, bf16[512,512]{1,0:T(8,128)(2,1)S(1)} %all_gather.11.refs_5_.d2_ref, bf16[512,1536]{1,0:T(8,128)(2,1)S(1)} %copy-done, bf16[2,512,128]{2,1,0:T(8,128)(2,1)S(1)} %collective-permute-done.15.far_ref), custom_call_target="tpu_custom_call" | custom-call | flops 1200000000 | bytes 3000000 | tf_op jit(solution)/shard_map/decode/pallas_call | solution.py:424
  (24 shorter events, 0.1 us)
Async XLA Ops:
  0.0 29.8 %collective-permute-start.3 = (bf16[256,512]{1,0:T(8,128)(2,1)}, bf16[256,512]{1,0:T(8,128)(2,1)S(1)}, u32[]{:S(2)}, u32[]{:S(2)}) collective-permute-start(bf16[256,512]{1,0:T(8,128)(2,1)} %rest_0_.2), channel_id=1, source_target_pairs={{0,2},{2,0},{1,3},{3,1},{4,6},{6,4},{5,7},{7,5},{8,10},{10,8},{9,1... | collective-permute-start | bytes 786440 | tf_op jit(solution)/shard_map/ppermute | solution.py:325
  2.9 26.9 %collective-permute-start.4 = (bf16[256,512]{1,0:T(8,128)(2,1)}, bf16[256,512]{1,0:T(8,128)(2,1)S(1)}, u32[]{:S(2)}, u32[]{:S(2)}) collective-permute-start(bf16[256,512]{1,0:T(8,128)(2,1)} %rest_0_.3), channel_id=1, source_target_pairs={{0,2},{2,0},{1,3},{3,1},{4,6},{6,4},{5,7},{7,5},{8,10},{10,8},{9,1... | collective-permute-start | bytes 786440 | tf_op jit(solution)/shard_map/ppermute | solution.py:325
  3.0 0.7 copy-start.9
  6.4 23.6 %copy-start.2 = (bf16[256,512]{1,0:T(8,128)(2,1)S(1)}, bf16[256,512]{1,0:T(8,128)(2,1)}, u32[]{:S(2)}) copy-start(bf16[256,512]{1,0:T(8,128)(2,1)} %rest_0_.2) | copy-start | bytes 786436
  6.4 23.4 %collective-permute-start = (bf16[2,512,128]{2,1,0:T(8,128)(2,1)S(1)}, bf16[2,512,128]{2,1,0:T(8,128)(2,1)S(1)}, u32[]{:S(2)}, u32[]{:S(2)}) collective-permute-start(bf16[2,512,128]{2,1,0:T(8,128)(2,1)S(1)} %get-tuple-element.27), channel_id=1, source_target_pairs={{0,8},{4,12},{8,0},{12,4},{1,9},{5,13},{9,1},{13,5},{2,10},{6,14},... | collective-permute-start | bytes 786440 | tf_op jit(solution)/shard_map/ppermute | solution.py:277
  9.5 20.3 %collective-permute-start.1 = (bf16[2,512,128]{2,1,0:T(8,128)(2,1)S(1)}, bf16[2,512,128]{2,1,0:T(8,128)(2,1)S(1)}, u32[]{:S(2)}, u32[]{:S(2)}) collective-permute-start(bf16[2,512,128]{2,1,0:T(8,128)(2,1)S(1)} %get-tuple-element.28), channel_id=1, source_target_pairs={{0,12},{4,8},{8,4},{12,0},{1,13},{5,9},{9,5},{13,1},{2,14},{6,10},... | collective-permute-start | bytes 786440 | tf_op jit(solution)/shard_map/ppermute | solution.py:277
  10.9 19.0 %collective-permute-start.2 = (bf16[2,512,128]{2,1,0:T(8,128)(2,1)S(1)}, bf16[2,512,128]{2,1,0:T(8,128)(2,1)S(1)}, u32[]{:S(2)}, u32[]{:S(2)}) collective-permute-start(bf16[2,512,128]{2,1,0:T(8,128)(2,1)S(1)} %get-tuple-element.29), channel_id=1, source_target_pairs={{0,4},{4,0},{8,12},{12,8},{1,5},{5,1},{9,13},{13,9},{2,6},{6,2},{1... | collective-permute-start | bytes 786440 | tf_op jit(solution)/shard_map/ppermute | solution.py:277
  11.1 0.9 %copy-start.4 = (bf16[256,512]{1,0:T(8,128)(2,1)S(1)}, bf16[256,512]{1,0:T(8,128)(2,1)}, u32[]{:S(2)}) copy-start(bf16[256,512]{1,0:T(8,128)(2,1)} %ms_ref.1) | copy-start | bytes 786436
  12.1 0.9 %copy-start.6 = (bf16[1,1,64,1024]{3,2,1,0:T(8,128)(2,1)S(1)}, bf16[1,1,64,1024]{3,2,1,0:T(8,128)(2,1)}, u32[]{:S(2)}) copy-start(bf16[1,1,64,1024]{3,2,1,0:T(8,128)(2,1)} %param.21) | copy-start | bytes 393220
  13.0 0.7 copy-start.10
  29.8 2.1 %copy-start.1 = (bf16[256,512]{1,0:T(8,128)(2,1)S(1)}, bf16[256,512]{1,0:T(8,128)(2,1)}, u32[]{:S(2)}) copy-start(bf16[256,512]{1,0:T(8,128)(2,1)} %rest_0_.3) | copy-start | bytes 786436
  29.9 5.2 %copy-start.3 = (bf16[24,64,256]{2,1,0:T(8,128)(2,1)S(1)}, bf16[24,64,256]{2,1,0:T(8,128)(2,1)}, u32[]{:S(2)}) copy-start(bf16[24,64,256]{2,1,0:T(8,128)(2,1)} %tiles_ref.1) | copy-start | bytes 2359300
  29.9 5.2 %copy-start.8 = (s32[24,4]{0,1:T(4,128)S(1)}, s32[24,4]{0,1:T(4,128)}, u32[]{:S(2)}) copy-start(s32[24,4]{0,1:T(4,128)} %param.24) | copy-start | bytes 1156
  29.9 2.0 %collective-permute-start.5 = (bf16[4,512,128]{2,1,0:T(8,128)(2,1)S(1)}, bf16[4,512,128]{2,1,0:T(8,128)(2,1)S(1)}, u32[]{:S(2)}, u32[]{:S(2)}) collective-permute-start(bf16[4,512,128]{2,1,0:T(8,128)(2,1)S(1)} %stack.19), channel_id=1, source_target_pairs={{0,1},{1,0},{2,3},{3,2},{4,5},{5,4},{6,7},{7,6},{8,9},{9,8},{10,11... | collective-permute-start | bytes 1572872 | tf_op jit(solution)/shard_map/ppermute | solution.py:322
  33.6 8.4 %copy-start.7 = (s32[1,1,8,2]{2,3,1,0:T(2,128)S(1)}, s32[1,1,8,2]{2,3,1,0:T(2,128)}, u32[]{:S(2)}) copy-start(s32[1,1,8,2]{2,3,1,0:T(2,128)} %param.23) | copy-start | bytes 196
  33.6 8.4 %collective-permute-start.6 = (bf16[512,256]{1,0:T(8,128)(2,1)S(1)}, bf16[512,256]{1,0:T(8,128)(2,1)S(1)}, u32[]{:S(2)}, u32[]{:S(2)}) collective-permute-start(bf16[512,256]{1,0:T(8,128)(2,1)S(1)} %get-tuple-element.34), channel_id=1, source_target_pairs={{0,2},{2,0},{1,3},{3,1},{4,6},{6,4},{5,7},{7,5},{8,10},{10,8},{9,1... | collective-permute-start | bytes 786440 | tf_op jit(solution)/shard_map/ppermute | solution.py:380
  42.0 16.6 %copy-start.5 = (bf16[256,512]{1,0:T(8,128)(2,1)S(1)}, bf16[256,512]{1,0:T(8,128)(2,1)}, u32[]{:S(2)}) copy-start(bf16[256,512]{1,0:T(8,128)(2,1)} %x_ref.1) | copy-start | bytes 786436
  43.7 7.6 %collective-permute-start.7 = (bf16[512,256]{1,0:T(8,128)(2,1)S(1)}, bf16[512,256]{1,0:T(8,128)(2,1)S(1)}, u32[]{:S(2)}, u32[]{:S(2)}) collective-permute-start(bf16[512,256]{1,0:T(8,128)(2,1)S(1)} %get-tuple-element.36), channel_id=1, source_target_pairs={{0,2},{2,0},{1,3},{3,1},{4,6},{6,4},{5,7},{7,5},{8,10},{10,8},{9,1... | collective-permute-start | bytes 786440 | tf_op jit(solution)/shard_map/ppermute | solution.py:380
  45.3 14.9 %collective-permute-start.11 = (bf16[512,128]{1,0:T(8,128)(2,1)S(1)}, bf16[512,128]{1,0:T(8,128)(2,1)S(1)}, u32[]{:S(2)}, u32[]{:S(2)}) collective-permute-start(bf16[512,128]{1,0:T(8,128)(2,1)S(1)} %get-tuple-element.42), channel_id=1, source_target_pairs={{0,8},{4,12},{8,0},{12,4},{1,9},{5,13},{9,1},{13,5},{2,10},{6,14},... | collective-permute-start | bytes 393224 | tf_op jit(solution)/shard_map/ppermute | solution.py:277
  50.3 17.9 %collective-permute-start.12 = (bf16[512,128]{1,0:T(8,128)(2,1)S(1)}, bf16[512,128]{1,0:T(8,128)(2,1)S(1)}, u32[]{:S(2)}, u32[]{:S(2)}) collective-permute-start(bf16[512,128]{1,0:T(8,128)(2,1)S(1)} %get-tuple-element.43), channel_id=1, source_target_pairs={{0,12},{4,8},{8,4},{12,0},{1,13},{5,9},{9,5},{13,1},{2,14},{6,10},... | collective-permute-start | bytes 393224 | tf_op jit(solution)/shard_map/ppermute | solution.py:277
  50.7 17.5 %collective-permute-start.13 = (bf16[512,128]{1,0:T(8,128)(2,1)S(1)}, bf16[512,128]{1,0:T(8,128)(2,1)S(1)}, u32[]{:S(2)}, u32[]{:S(2)}) collective-permute-start(bf16[512,128]{1,0:T(8,128)(2,1)S(1)} %get-tuple-element.44), channel_id=1, source_target_pairs={{0,4},{4,0},{8,12},{12,8},{1,5},{5,1},{9,13},{13,9},{2,6},{6,2},{1... | collective-permute-start | bytes 393224 | tf_op jit(solution)/shard_map/ppermute | solution.py:277
  53.1 17.0 %collective-permute-start.8 = (bf16[512,128]{1,0:T(8,128)(2,1)S(1)}, bf16[512,128]{1,0:T(8,128)(2,1)S(1)}, u32[]{:S(2)}, u32[]{:S(2)}) collective-permute-start(bf16[512,128]{1,0:T(8,128)(2,1)S(1)} %get-tuple-element.38), channel_id=1, source_target_pairs={{0,8},{4,12},{8,0},{12,4},{1,9},{5,13},{9,1},{13,5},{2,10},{6,14},... | collective-permute-start | bytes 393224 | tf_op jit(solution)/shard_map/ppermute | solution.py:277
  58.1 12.0 %collective-permute-start.9 = (bf16[512,128]{1,0:T(8,128)(2,1)S(1)}, bf16[512,128]{1,0:T(8,128)(2,1)S(1)}, u32[]{:S(2)}, u32[]{:S(2)}) collective-permute-start(bf16[512,128]{1,0:T(8,128)(2,1)S(1)} %get-tuple-element.39), channel_id=1, source_target_pairs={{0,12},{4,8},{8,4},{12,0},{1,13},{5,9},{9,5},{13,1},{2,14},{6,10},... | collective-permute-start | bytes 393224 | tf_op jit(solution)/shard_map/ppermute | solution.py:277
  60.2 9.9 %collective-permute-start.10 = (bf16[512,128]{1,0:T(8,128)(2,1)S(1)}, bf16[512,128]{1,0:T(8,128)(2,1)S(1)}, u32[]{:S(2)}, u32[]{:S(2)}) collective-permute-start(bf16[512,128]{1,0:T(8,128)(2,1)S(1)} %get-tuple-element.40), channel_id=1, source_target_pairs={{0,4},{4,0},{8,12},{12,8},{1,5},{5,1},{9,13},{13,9},{2,6},{6,2},{1... | collective-permute-start | bytes 393224 | tf_op jit(solution)/shard_map/ppermute | solution.py:277
  68.3 2.0 %collective-permute-start.14 = (bf16[2,512,128]{2,1,0:T(8,128)(2,1)S(1)}, bf16[2,512,128]{2,1,0:T(8,128)(2,1)S(1)}, u32[]{:S(2)}, u32[]{:S(2)}) collective-permute-start(bf16[2,512,128]{2,1,0:T(8,128)(2,1)S(1)} %stack.21), channel_id=1, source_target_pairs={{0,1},{1,0},{2,3},{3,2},{4,5},{5,4},{6,7},{7,6},{8,9},{9,8},{10,11... | collective-permute-start | bytes 786440 | tf_op jit(solution)/shard_map/ppermute | solution.py:322
  70.3 1.6 %copy-start = (bf16[512,1536]{1,0:T(8,128)(2,1)S(1)}, bf16[512,1536]{1,0:T(8,128)(2,1)}, u32[]{:S(2)}) copy-start(bf16[512,1536]{1,0:T(8,128)(2,1)} %grid_ref.1) | copy-start | bytes 4718596
  70.3 1.6 %collective-permute-start.15 = (bf16[2,512,128]{2,1,0:T(8,128)(2,1)S(1)}, bf16[2,512,128]{2,1,0:T(8,128)(2,1)S(1)}, u32[]{:S(2)}, u32[]{:S(2)}) collective-permute-start(bf16[2,512,128]{2,1,0:T(8,128)(2,1)S(1)} %stack.20.ready_ref), channel_id=1, source_target_pairs={{0,1},{1,0},{2,3},{3,2},{4,5},{5,4},{6,7},{7,6},{8,9},{9,8},{10,11... | collective-permute-start | bytes 786440 | tf_op jit(solution)/shard_map/ppermute | solution.py:322

commit v5 on v4

--- a/solution.py
+++ b/solution.py
@@ -215,10 +215,8 @@
             )
 
 
-def first_mesh_kernel(blocks, n_dom, at_ref, send_ref, g_ref, other_ref, mw_ref, d1_ref, later_ref, ready_ref, *rest):
-    outs, later_out, buf = rest[:n_dom], rest[n_dom], rest[n_dom + 1]
-    mesh_kernel(blocks, n_dom, at_ref, send_ref, g_ref, other_ref, mw_ref, d1_ref, *outs, buf)
-    later_out[...] = later_ref[...]
+def after_kernel(blocks, n_dom, ready_ref, *refs):
+    mesh_kernel(blocks, n_dom, *refs)
 
 
 def hold_kernel(ready_ref, x_ref, out_ref):
@@ -382,25 +380,25 @@
 
     thin = jax.ShapeDtypeStruct((rows, pair), BF)
     scratch = [VMEM((4, rows, mesh_cols // 2 + pair), BF)]
-    *out, second = call(
-        functools.partial(first_mesh_kernel, mesh_blocks, n_dom),
-        out_shape=[thin] * n_dom + [half],
-        in_specs=[full(SMEM), full(SMEM)] + [full()] * 5 + [anywhere()],
-        out_specs=[full()] * (n_dom + 1),
+    out = call(
+        functools.partial(after_kernel, mesh_blocks, n_dom),
+        out_shape=[thin] * n_dom,
+        in_specs=[anywhere(), full(SMEM), full(SMEM)] + [full()] * 4,
+        out_specs=[full()] * n_dom,
         scratch_shapes=scratch,
         cost_estimate=cost(0.5),
         name="mesh",
-    )(at, send_mesh, g_first, other_feat(first), mw, d1, second, to_grid)
+    )(to_grid, at, send_mesh, g_first, other_feat(first), mw, d1)
     near_first = move(out, n_dom)
     out = call(
-        functools.partial(mesh_kernel, mesh_blocks, n_dom),
+        functools.partial(after_kernel, mesh_blocks, n_dom),
         out_shape=[thin] * n_dom,
-        in_specs=[full(SMEM), full(SMEM)] + [full()] * 4,
+        in_specs=[anywhere(), full(SMEM), full(SMEM)] + [full()] * 4,
         out_specs=[full()] * n_dom,
         scratch_shapes=scratch,
         cost_estimate=cost(0.5),
         name="mesh",
-    )(at, send_mesh, g_second, other_feat(second), mw, d1)
+    )(out[0], at, send_mesh, g_second, other_feat(second), mw, d1)
     near_second = move(out, n_dom)
     d2 = whole(call(
         hold_kernel,

time: 75.4 us -> 74.1 us (0.983)
  waiting for transfers between devices: 6.89 us -> 9.19 us
  starting transfers between devices: 22.1 us -> 20 us
  blocking collectives: 23 us -> 22.1 us
    ppermute x9, waiting for transfers between devices: 3.35 us -> 5.95 us  [move(): lax.ppermute(chunks[k], 'dom', [(i, i ^ k) for i in range(n_dom)])]
    ppermute x9, starting transfers between devices: 15.7 us -> 14.7 us  [move(): lax.ppermute(chunks[k], 'dom', [(i, i ^ k) for i in range(n_dom)])]
    ppermute x2, starting transfers between devices: 3.12 us -> 2.16 us  [other_feat(): return lax.ppermute(x, 'feat', SWAP)]
    all_gather x3, blocking collectives: 23 us -> 22.1 us  [whole(): return lax.all_gather(w, 'feat', axis=0, tiled=True)]
  transfers between devices with their start and end apart: 16 -> 16, of which waited for: 6 -> 5; matrix products, arithmetic and copies ran while one was open for 0% -> 0% of each run, Pallas kernels for 17% -> 20%
where the time goes in v5:
time: 74.1 us; the launch traced here: 73.8 us
  blocking collectives  22.1 us (30%)
  starting transfers between devices  20 us (27%)
  Pallas kernels  19 us (26%)
  waiting for transfers between devices  9.19 us (12%)
  local copies, waits for them, and re-layouts  3.23 us (4%)
    all_gather x3, blocking collectives, whole(): return lax.all_gather(w, 'feat', axis=0, tiled=True)  22.1 us
    ppermute x9, starting transfers between devices, move(): lax.ppermute(chunks[k], 'dom', [(i, i ^ k) for i in range(n_dom)])  14.7 us
    ppermute x9, waiting for transfers between devices, move(): lax.ppermute(chunks[k], 'dom', [(i, i ^ k) for i in range(n_dom)])  5.95 us
    pallas_call x2, Pallas kernels, local(): call(functools.partial(after_kernel, mesh_blocks, n_dom), out_shape=[thin...  3.46 us
    pallas_call x1, Pallas kernels, local(): call(functools.partial(spread_kernel, n_dom, feeding), grid=(grid_blocks...  3.46 us
    unnamed x22, local copies, waits for them, and re-layouts  3.23 us
    ppermute x2, starting transfers between devices, rows_of(): return [w, lax.ppermute(w, 'feat', SWAP)] if n_feat == 2 else [whole(w)]  2.97 us
    ppermute x2, waiting for transfers between devices, other_feat(): return lax.ppermute(x, 'feat', SWAP)  2.65 us
  transfers between devices with their start and end apart: 16, of which 5 were waited for; matrix products, arithmetic and copies ran while one was open for 0% of the time, Pallas kernels for 20%

profile of v5, /device:TPU:0, one launch (start us, length us, event | category | flops | bytes accessed | tf_op | source)
XLA Modules:
  0.0 73.8 jit_solution(8514500745667933603)
XLA Ops:
  0.0 2.9 %collective-permute-start.3 = (bf16[256,512]{1,0:T(8,128)(2,1)}, bf16[256,512]{1,0:T(8,128)(2,1)S(1)}, u32[]{:S(2)}, u32[]{:S(2)}) collective-permute-start(bf16[256,512]{1,0:T(8,128)(2,1)} %rest_0_.2), channel_id=1, source_target_pairs={{0,2},{2,0},{1,3},{3,1},{4,6},{6,4},{5,7},{7,5},{8,10},{10,8},{9,1... | collective-permute-start | bytes 786440 | tf_op jit(solution)/shard_map/ppermute | solution.py:323
  2.9 0.0 collective-permute-start.4
  3.0 0.1 pad_add_fusion.at_ref.refs_0_
  3.1 0.7 copy-done.9
  3.7 2.6 %pack.1 = (bf16[2,512,128]{2,1,0:T(8,128)(2,1)S(1)}, bf16[2,512,128]{2,1,0:T(8,128)(2,1)S(1)}, bf16[2,512,128]{2,1,0:T(8,128)(2,1)S(1)}, bf16[2,512,128]{2,1,0:T(8,128)(2,1)S(1)}) custom-call(s32[3]{0:T(128)S(1)} %pad_add_fusion.at_ref.refs_0_, s32[2,8]{1,0:T(2,128)S(1)} %bitcast.16, bf16[512,1536]{1,0:T(8,128)(2,1)} %grid_ref.1), custom_call_target="tpu_custom_call" | custom-call | flops 400000000 | bytes 1000000 | tf_op jit(solution)/shard_map/pack/pallas_call | solution.py:296
  6.4 0.0 copy-start.2
  6.4 3.2 %collective-permute-start = (bf16[2,512,128]{2,1,0:T(8,128)(2,1)S(1)}, bf16[2,512,128]{2,1,0:T(8,128)(2,1)S(1)}, u32[]{:S(2)}, u32[]{:S(2)}) collective-permute-start(bf16[2,512,128]{2,1,0:T(8,128)(2,1)S(1)} %get-tuple-element.26), channel_id=1, source_target_pairs={{0,8},{4,12},{8,0},{12,4},{1,9},{5,13},{9,1},{13,5},{2,10},{6,14},... | collective-permute-start | bytes 786440 | tf_op jit(solution)/shard_map/ppermute | solution.py:275
  9.5 1.4 %collective-permute-start.1 = (bf16[2,512,128]{2,1,0:T(8,128)(2,1)S(1)}, bf16[2,512,128]{2,1,0:T(8,128)(2,1)S(1)}, u32[]{:S(2)}, u32[]{:S(2)}) collective-permute-start(bf16[2,512,128]{2,1,0:T(8,128)(2,1)S(1)} %get-tuple-element.27), channel_id=1, source_target_pairs={{0,12},{4,8},{8,4},{12,0},{1,13},{5,9},{9,5},{13,1},{2,14},{6,10},... | collective-permute-start | bytes 786440 | tf_op jit(solution)/shard_map/ppermute | solution.py:275
  10.9 0.2 collective-permute-start.2
  11.1 0.9 %copy-done.4 = bf16[256,512]{1,0:T(8,128)(2,1)S(1)} copy-done((bf16[256,512]{1,0:T(8,128)(2,1)S(1)}, bf16[256,512]{1,0:T(8,128)(2,1)}, u32[]{:S(2)}) %copy-start.4) | copy-done | bytes 262168
  12.1 0.9 %copy-done.6 = bf16[1,1,64,1024]{3,2,1,0:T(8,128)(2,1)S(1)} copy-done((bf16[1,1,64,1024]{3,2,1,0:T(8,128)(2,1)S(1)}, bf16[1,1,64,1024]{3,2,1,0:T(8,128)(2,1)}, u32[]{:S(2)}) %copy-start.6) | copy-done | bytes 131096
  13.0 0.7 copy-done.10
  13.6 1.1 %scatter.1 = (bf16[2,512,512]{2,1,0:T(8,128)(2,1)S(1)}, bf16[256,512]{1,0:T(8,128)(2,1)S(1)}) custom-call(s32[3]{0:T(128)S(1)} %pad_add_fusion.at_ref.refs_0_, s32[16]{0:T(128)S(1)} %bitcast.17, bf16[64,1024]{1,0:T(8,128)(2,1)S(1)} %bitcast.12, bf16[256,512]{1,0:T(8,128)(2,1)S(1)} %copy-done.4), custom_call_target="tpu_custom_call" | custom-call | tf_op jit(solution)/shard_map/scatter/pallas_call | solution.py:326
  14.8 7.8 %all_gather.10.refs_7_.refs_5_ = bf16[512,512]{1,0:T(8,128)(2,1)S(1)} all-gather(bf16[256,512]{1,0:T(8,128)(2,1)} %param.17), channel_id=1, replica_groups=mesh['ens'=2,'dom'=4,'feat'=2,'sub'=2] {'feat'}, dimensions={0}, use_global_device_ids=true | all-gather | bytes 786432 | tf_op jit(solution)/shard_map/all_gather | solution.py:309
  22.6 7.2 %all_gather.9.refs_6_.refs_4_ = bf16[512,512]{1,0:T(8,128)(2,1)S(1)} all-gather(bf16[256,512]{1,0:T(8,128)(2,1)} %param.19), channel_id=1, replica_groups=mesh['ens'=2,'dom'=4,'feat'=2,'sub'=2] {'feat'}, dimensions={0}, use_global_device_ids=true | all-gather | bytes 786432 | tf_op jit(solution)/shard_map/all_gather | solution.py:309
  29.8 0.0 collective-permute-done.3.rest_5_.refs_4_.rest_1_
  29.8 0.0 collective-permute-done.4.refs_5_.rest_3_.rest_1_
  29.9 0.0 copy-start.1
  29.9 0.1 collective-permute-start.5
  30.0 1.4 %encode.1.acc_ref = f32[512,512]{1,0:T(8,128)S(1)} custom-call(s32[3]{0:T(128)S(1)} %pad_add_fusion.at_ref.refs_0_, bf16[2,512,512]{2,1,0:T(8,128)(2,1)S(1)} %get-tuple-element.24.wide_ref.refs_8_, bf16[2,512,128]{2,1,0:T(8,128)(2,1)S(1)} %get-tuple-element.25.rest_0_.refs_0_, bf16[2,512,128]{2,1,0:T(8,128)(2,1)S(1)} %collective-permute-done.rest_1_.refs_1_, ...), custom_call_target="tpu_custom_call" | custom-call | flops 200000000 | bytes 500000 | tf_op jit(solution)/shard_map/encode/pallas_call | solution.py:349
  31.4 0.0 copy-start.3
  31.4 0.0 copy-start.8
  31.4 0.5 collective-permute-done.5.far_ref
  31.9 1.7 %gather.1 = (f32[512,256]{1,0:T(8,128)S(1)}, bf16[512,256]{1,0:T(8,128)(2,1)S(1)}, bf16[512,256]{1,0:T(8,128)(2,1)S(1)}) custom-call(s32[3]{0:T(128)S(1)} %pad_add_fusion.at_ref.refs_0_, f32[512,512]{1,0:T(8,128)S(1)} %encode.1.acc_ref, bf16[2,512,512]{2,1,0:T(8,128)(2,1)S(1)} %get-tuple-element.24.wide_ref.refs_8_, ...), custom_call_target="tpu_custom_call" | custom-call | flops 200000000 | bytes 500000 | tf_op jit(solution)/shard_map/gather/pallas_call | solution.py:359
  33.6 0.0 copy-start.7
  33.6 1.5 %collective-permute-start.6 = (bf16[512,256]{1,0:T(8,128)(2,1)S(1)}, bf16[512,256]{1,0:T(8,128)(2,1)S(1)}, u32[]{:S(2)}, u32[]{:S(2)}) collective-permute-start(bf16[512,256]{1,0:T(8,128)(2,1)S(1)} %get-tuple-element.31), channel_id=1, source_target_pairs={{0,2},{2,0},{1,3},{3,1},{4,6},{6,4},{5,7},{7,5},{8,10},{10,8},{9,1... | collective-permute-start | bytes 786440 | tf_op jit(solution)/shard_map/ppermute | solution.py:378
  35.1 0.9 %later.1 = (f32[512,256]{1,0:T(8,128)S(1)}, bf16[512,256]{1,0:T(8,128)(2,1)S(1)}) custom-call(s32[3]{0:T(128)S(1)} %pad_add_fusion.at_ref.refs_0_, bf16[512,256]{1,0:T(8,128)(2,1)S(1)} %get-tuple-element.33.total_ref, bf16[256,512]{1,0:T(8,128)(2,1)S(1)} %get-tuple-element.29.ms_ref, bf16[256,512]{1,0:T(8,128)(2,1)S(1)} %copy-done.1, ...), custom_call_target="tpu_custom_call" | custom-call | flops 200000000 | bytes 500000 | tf_op jit(solution)/shard_map/later/pallas_call | solution.py:367
  36.1 0.6 collective-permute-start.7
  36.7 3.5 %spread.1.ready_ref.wide_ref = bf16[1024,1536]{1,0:T(8,128)(2,1)S(1)} custom-call(s32[3]{0:T(128)S(1)} %pad_add_fusion.at_ref.refs_0_, s32[4,24]{1,0:T(4,128)S(1)} %bitcast.15, bf16[24,64,256]{2,1,0:T(8,128)(2,1)S(1)} %copy-done.3), custom_call_target="tpu_custom_call" | custom-call | tf_op jit(solution)/shard_map/spread/pallas_call | solution.py:337
  40.1 2.6 %collective-permute-done.6.refs_3_ = bf16[512,256]{1,0:T(8,128)(2,1)S(1)} collective-permute-done((bf16[512,256]{1,0:T(8,128)(2,1)S(1)}, bf16[512,256]{1,0:T(8,128)(2,1)S(1)}, u32[]{:S(2)}, u32[]{:S(2)}) %collective-permute-start.6) | collective-permute-done | bytes 262176 | tf_op jit(solution)/shard_map/ppermute | solution.py:378
  42.8 1.7 %mesh.2 = (bf16[512,128]{1,0:T(8,128)(2,1)S(1)}, bf16[512,128]{1,0:T(8,128)(2,1)S(1)}, bf16[512,128]{1,0:T(8,128)(2,1)S(1)}, bf16[512,128]{1,0:T(8,128)(2,1)S(1)}) custom-call(bf16[1024,1536]{1,0:T(8,128)(2,1)S(1)} %spread.1.ready_ref.wide_ref, s32[3]{0:T(128)S(1)} %pad_add_fusion.at_ref.refs_0_, s32[2,8]{1,0:T(2,128)S(1)} %bitcast.13, ...), custom_call_target="tpu_custom_call" | custom-call | flops 200000000 | bytes 500000 | tf_op jit(solution)/shard_map/mesh/pallas_call | solution.py:383
  44.5 5.0 %collective-permute-start.11 = (bf16[512,128]{1,0:T(8,128)(2,1)S(1)}, bf16[512,128]{1,0:T(8,128)(2,1)S(1)}, u32[]{:S(2)}, u32[]{:S(2)}) collective-permute-start(bf16[512,128]{1,0:T(8,128)(2,1)S(1)} %get-tuple-element.40), channel_id=1, source_target_pairs={{0,8},{4,12},{8,0},{12,4},{1,9},{5,13},{9,1},{13,5},{2,10},{6,14},... | collective-permute-start | bytes 393224 | tf_op jit(solution)/shard_map/ppermute | solution.py:275
  49.5 0.4 collective-permute-start.12
  50.0 0.2 collective-permute-start.13
  50.2 1.7 %mesh.3 = (bf16[512,128]{1,0:T(8,128)(2,1)S(1)}, bf16[512,128]{1,0:T(8,128)(2,1)S(1)}, bf16[512,128]{1,0:T(8,128)(2,1)S(1)}, bf16[512,128]{1,0:T(8,128)(2,1)S(1)}) custom-call(bf16[512,128]{1,0:T(8,128)(2,1)S(1)} %get-tuple-element.32.ready_ref.refs_0_.rest_0_, s32[3]{0:T(128)S(1)} %pad_add_fusion.at_ref.refs_0_, s32[2,8]{1,0:T(2,128)S(1)} %bitcast.14, ...), custom_call_target="tpu_custom_call" | custom-call | flops 200000000 | bytes 500000 | tf_op jit(solution)/shard_map/mesh/pallas_call | solution.py:393
  51.9 3.8 %collective-permute-start.8 = (bf16[512,128]{1,0:T(8,128)(2,1)S(1)}, bf16[512,128]{1,0:T(8,128)(2,1)S(1)}, u32[]{:S(2)}, u32[]{:S(2)}) collective-permute-start(bf16[512,128]{1,0:T(8,128)(2,1)S(1)} %get-tuple-element.37), channel_id=1, source_target_pairs={{0,8},{4,12},{8,0},{12,4},{1,9},{5,13},{9,1},{13,5},{2,10},{6,14},... | collective-permute-start | bytes 393224 | tf_op jit(solution)/shard_map/ppermute | solution.py:275
  55.7 0.5 collective-permute-start.9
  56.2 3.5 %collective-permute-done.11.refs_1_.rest_1_ = bf16[512,128]{1,0:T(8,128)(2,1)S(1)} collective-permute-done((bf16[512,128]{1,0:T(8,128)(2,1)S(1)}, bf16[512,128]{1,0:T(8,128)(2,1)S(1)}, u32[]{:S(2)}, u32[]{:S(2)}) %collective-permute-start.11) | collective-permute-done | bytes 131104 | tf_op jit(solution)/shard_map/ppermute | solution.py:275
  59.7 7.0 %all_gather.11.refs_5_.d2_ref = bf16[512,512]{1,0:T(8,128)(2,1)S(1)} all-gather(bf16[256,512]{1,0:T(8,128)(2,1)S(1)} %hold.1), channel_id=1, replica_groups=mesh['ens'=2,'dom'=4,'feat'=2,'sub'=2] {'feat'}, dimensions={0}, use_global_device_ids=true | all-gather | bytes 786432 | tf_op jit(solution)/shard_map/all_gather | solution.py:309
  66.8 0.1 stack.21
  66.9 0.1 collective-permute-start.14
  67.0 2.4 %collective-permute-done.8.refs_1_.rest_5_ = bf16[512,128]{1,0:T(8,128)(2,1)S(1)} collective-permute-done((bf16[512,128]{1,0:T(8,128)(2,1)S(1)}, bf16[512,128]{1,0:T(8,128)(2,1)S(1)}, u32[]{:S(2)}, u32[]{:S(2)}) %collective-permute-start.8) | collective-permute-done | bytes 131104 | tf_op jit(solution)/shard_map/ppermute | solution.py:275
  69.4 0.1 stack.20.ready_ref
  69.6 0.0 copy-start
  69.6 0.1 collective-permute-start.15
  69.7 1.4 %collect.1.acc_ref = f32[512,1536]{1,0:T(8,128)S(1)} custom-call(bf16[2,512,128]{2,1,0:T(8,128)(2,1)S(1)} %stack.20.ready_ref, bf16[1024,1536]{1,0:T(8,128)(2,1)S(1)} %spread.1.ready_ref.wide_ref, bf16[2,512,128]{2,1,0:T(8,128)(2,1)S(1)} %collective-permute-done.14.far_ref, bf16[512,128]{1,0:T(8,128)(2,1)S(1)} %get-tuple-element.32.ready_ref.refs_0_.rest_0_, ...), custom_call_target="tpu_custom_call" | custom-call | flops 200000000 | bytes 500000 | tf_op jit(solution)/shard_map/collect/pallas_call | solution.py:414
  71.1 0.1 collective-permute-done.15.far_ref
  71.2 2.6 %decode.1 = bf16[512,1536]{1,0:T(8,128)(2,1)} custom-call(f32[512,1536]{1,0:T(8,128)S(1)} %collect.1.acc_ref, bf16[1024,1536]{1,0:T(8,128)(2,1)S(1)} %spread.1.ready_ref.wide_ref, bf16[512,512]{1,0:T(8,128)(2,1)S(1)} %all_gather.11.refs_5_.d2_ref, bf16[512,1536]{1,0:T(8,128)(2,1)S(1)} %copy-done, bf16[2,512,128]{2,1,0:T(8,128)(2,1)S(1)} %collective-permute-done.15.far_ref), custom_call_target="tpu_custom_call" | custom-call | flops 1200000000 | bytes 3000000 | tf_op jit(solution)/shard_map/decode/pallas_call | solution.py:422
  (24 shorter events, 0.1 us)
Async XLA Ops:
  0.0 29.8 %collective-permute-start.3 = (bf16[256,512]{1,0:T(8,128)(2,1)}, bf16[256,512]{1,0:T(8,128)(2,1)S(1)}, u32[]{:S(2)}, u32[]{:S(2)}) collective-permute-start(bf16[256,512]{1,0:T(8,128)(2,1)} %rest_0_.2), channel_id=1, source_target_pairs={{0,2},{2,0},{1,3},{3,1},{4,6},{6,4},{5,7},{7,5},{8,10},{10,8},{9,1... | collective-permute-start | bytes 786440 | tf_op jit(solution)/shard_map/ppermute | solution.py:323
  2.9 26.9 %collective-permute-start.4 = (bf16[256,512]{1,0:T(8,128)(2,1)}, bf16[256,512]{1,0:T(8,128)(2,1)S(1)}, u32[]{:S(2)}, u32[]{:S(2)}) collective-permute-start(bf16[256,512]{1,0:T(8,128)(2,1)} %rest_0_.3), channel_id=1, source_target_pairs={{0,2},{2,0},{1,3},{3,1},{4,6},{6,4},{5,7},{7,5},{8,10},{10,8},{9,1... | collective-permute-start | bytes 786440 | tf_op jit(solution)/shard_map/ppermute | solution.py:323
  3.0 0.7 copy-start.9
  6.4 23.6 %copy-start.2 = (bf16[256,512]{1,0:T(8,128)(2,1)S(1)}, bf16[256,512]{1,0:T(8,128)(2,1)}, u32[]{:S(2)}) copy-start(bf16[256,512]{1,0:T(8,128)(2,1)} %rest_0_.2) | copy-start | bytes 786436
  6.4 23.4 %collective-permute-start = (bf16[2,512,128]{2,1,0:T(8,128)(2,1)S(1)}, bf16[2,512,128]{2,1,0:T(8,128)(2,1)S(1)}, u32[]{:S(2)}, u32[]{:S(2)}) collective-permute-start(bf16[2,512,128]{2,1,0:T(8,128)(2,1)S(1)} %get-tuple-element.26), channel_id=1, source_target_pairs={{0,8},{4,12},{8,0},{12,4},{1,9},{5,13},{9,1},{13,5},{2,10},{6,14},... | collective-permute-start | bytes 786440 | tf_op jit(solution)/shard_map/ppermute | solution.py:275
  9.5 20.3 %collective-permute-start.1 = (bf16[2,512,128]{2,1,0:T(8,128)(2,1)S(1)}, bf16[2,512,128]{2,1,0:T(8,128)(2,1)S(1)}, u32[]{:S(2)}, u32[]{:S(2)}) collective-permute-start(bf16[2,512,128]{2,1,0:T(8,128)(2,1)S(1)} %get-tuple-element.27), channel_id=1, source_target_pairs={{0,12},{4,8},{8,4},{12,0},{1,13},{5,9},{9,5},{13,1},{2,14},{6,10},... | collective-permute-start | bytes 786440 | tf_op jit(solution)/shard_map/ppermute | solution.py:275
  10.9 18.9 %collective-permute-start.2 = (bf16[2,512,128]{2,1,0:T(8,128)(2,1)S(1)}, bf16[2,512,128]{2,1,0:T(8,128)(2,1)S(1)}, u32[]{:S(2)}, u32[]{:S(2)}) collective-permute-start(bf16[2,512,128]{2,1,0:T(8,128)(2,1)S(1)} %get-tuple-element.28), channel_id=1, source_target_pairs={{0,4},{4,0},{8,12},{12,8},{1,5},{5,1},{9,13},{13,9},{2,6},{6,2},{1... | collective-permute-start | bytes 786440 | tf_op jit(solution)/shard_map/ppermute | solution.py:275
  11.1 0.9 %copy-start.4 = (bf16[256,512]{1,0:T(8,128)(2,1)S(1)}, bf16[256,512]{1,0:T(8,128)(2,1)}, u32[]{:S(2)}) copy-start(bf16[256,512]{1,0:T(8,128)(2,1)} %ms_ref.1) | copy-start | bytes 786436
  12.1 0.9 %copy-start.6 = (bf16[1,1,64,1024]{3,2,1,0:T(8,128)(2,1)S(1)}, bf16[1,1,64,1024]{3,2,1,0:T(8,128)(2,1)}, u32[]{:S(2)}) copy-start(bf16[1,1,64,1024]{3,2,1,0:T(8,128)(2,1)} %param.21) | copy-start | bytes 393220
  13.0 0.7 copy-start.10
  29.9 2.0 %copy-start.1 = (bf16[256,512]{1,0:T(8,128)(2,1)S(1)}, bf16[256,512]{1,0:T(8,128)(2,1)}, u32[]{:S(2)}) copy-start(bf16[256,512]{1,0:T(8,128)(2,1)} %rest_0_.3) | copy-start | bytes 786436
  29.9 2.0 %collective-permute-start.5 = (bf16[4,512,128]{2,1,0:T(8,128)(2,1)S(1)}, bf16[4,512,128]{2,1,0:T(8,128)(2,1)S(1)}, u32[]{:S(2)}, u32[]{:S(2)}) collective-permute-start(bf16[4,512,128]{2,1,0:T(8,128)(2,1)S(1)} %stack.19), channel_id=1, source_target_pairs={{0,1},{1,0},{2,3},{3,2},{4,5},{5,4},{6,7},{7,6},{8,9},{9,8},{10,11... | collective-permute-start | bytes 1572872 | tf_op jit(solution)/shard_map/ppermute | solution.py:320
  31.4 5.3 %copy-start.3 = (bf16[24,64,256]{2,1,0:T(8,128)(2,1)S(1)}, bf16[24,64,256]{2,1,0:T(8,128)(2,1)}, u32[]{:S(2)}) copy-start(bf16[24,64,256]{2,1,0:T(8,128)(2,1)} %tiles_ref.1) | copy-start | bytes 2359300
  31.4 5.3 %copy-start.8 = (s32[24,4]{0,1:T(4,128)S(1)}, s32[24,4]{0,1:T(4,128)}, u32[]{:S(2)}) copy-start(s32[24,4]{0,1:T(4,128)} %param.24) | copy-start | bytes 1156
  33.6 9.2 %copy-start.7 = (s32[1,1,8,2]{2,3,1,0:T(2,128)S(1)}, s32[1,1,8,2]{2,3,1,0:T(2,128)}, u32[]{:S(2)}) copy-start(s32[1,1,8,2]{2,3,1,0:T(2,128)} %param.23) | copy-start | bytes 196
  33.6 9.2 %collective-permute-start.6 = (bf16[512,256]{1,0:T(8,128)(2,1)S(1)}, bf16[512,256]{1,0:T(8,128)(2,1)S(1)}, u32[]{:S(2)}, u32[]{:S(2)}) collective-permute-start(bf16[512,256]{1,0:T(8,128)(2,1)S(1)} %get-tuple-element.31), channel_id=1, source_target_pairs={{0,2},{2,0},{1,3},{3,1},{4,6},{6,4},{5,7},{7,5},{8,10},{10,8},{9,1... | collective-permute-start | bytes 786440 | tf_op jit(solution)/shard_map/ppermute | solution.py:378
  36.1 14.1 %collective-permute-start.7 = (bf16[512,256]{1,0:T(8,128)(2,1)S(1)}, bf16[512,256]{1,0:T(8,128)(2,1)S(1)}, u32[]{:S(2)}, u32[]{:S(2)}) collective-permute-start(bf16[512,256]{1,0:T(8,128)(2,1)S(1)} %get-tuple-element.35), channel_id=1, source_target_pairs={{0,2},{2,0},{1,3},{3,1},{4,6},{6,4},{5,7},{7,5},{8,10},{10,8},{9,1... | collective-permute-start | bytes 786440 | tf_op jit(solution)/shard_map/ppermute | solution.py:378
  42.8 13.4 %copy-start.5 = (bf16[256,512]{1,0:T(8,128)(2,1)S(1)}, bf16[256,512]{1,0:T(8,128)(2,1)}, u32[]{:S(2)}) copy-start(bf16[256,512]{1,0:T(8,128)(2,1)} %x_ref.1) | copy-start | bytes 786436
  44.5 15.2 %collective-permute-start.11 = (bf16[512,128]{1,0:T(8,128)(2,1)S(1)}, bf16[512,128]{1,0:T(8,128)(2,1)S(1)}, u32[]{:S(2)}, u32[]{:S(2)}) collective-permute-start(bf16[512,128]{1,0:T(8,128)(2,1)S(1)} %get-tuple-element.40), channel_id=1, source_target_pairs={{0,8},{4,12},{8,0},{12,4},{1,9},{5,13},{9,1},{13,5},{2,10},{6,14},... | collective-permute-start | bytes 393224 | tf_op jit(solution)/shard_map/ppermute | solution.py:275
  49.5 17.2 %collective-permute-start.12 = (bf16[512,128]{1,0:T(8,128)(2,1)S(1)}, bf16[512,128]{1,0:T(8,128)(2,1)S(1)}, u32[]{:S(2)}, u32[]{:S(2)}) collective-permute-start(bf16[512,128]{1,0:T(8,128)(2,1)S(1)} %get-tuple-element.41), channel_id=1, source_target_pairs={{0,12},{4,8},{8,4},{12,0},{1,13},{5,9},{9,5},{13,1},{2,14},{6,10},... | collective-permute-start | bytes 393224 | tf_op jit(solution)/shard_map/ppermute | solution.py:275
  50.0 16.8 %collective-permute-start.13 = (bf16[512,128]{1,0:T(8,128)(2,1)S(1)}, bf16[512,128]{1,0:T(8,128)(2,1)S(1)}, u32[]{:S(2)}, u32[]{:S(2)}) collective-permute-start(bf16[512,128]{1,0:T(8,128)(2,1)S(1)} %get-tuple-element.42), channel_id=1, source_target_pairs={{0,4},{4,0},{8,12},{12,8},{1,5},{5,1},{9,13},{13,9},{2,6},{6,2},{1... | collective-permute-start | bytes 393224 | tf_op jit(solution)/shard_map/ppermute | solution.py:275
  51.9 17.5 %collective-permute-start.8 = (bf16[512,128]{1,0:T(8,128)(2,1)S(1)}, bf16[512,128]{1,0:T(8,128)(2,1)S(1)}, u32[]{:S(2)}, u32[]{:S(2)}) collective-permute-start(bf16[512,128]{1,0:T(8,128)(2,1)S(1)} %get-tuple-element.37), channel_id=1, source_target_pairs={{0,8},{4,12},{8,0},{12,4},{1,9},{5,13},{9,1},{13,5},{2,10},{6,14},... | collective-permute-start | bytes 393224 | tf_op jit(solution)/shard_map/ppermute | solution.py:275
  55.7 13.7 %collective-permute-start.9 = (bf16[512,128]{1,0:T(8,128)(2,1)S(1)}, bf16[512,128]{1,0:T(8,128)(2,1)S(1)}, u32[]{:S(2)}, u32[]{:S(2)}) collective-permute-start(bf16[512,128]{1,0:T(8,128)(2,1)S(1)} %get-tuple-element.38), channel_id=1, source_target_pairs={{0,12},{4,8},{8,4},{12,0},{1,13},{5,9},{9,5},{13,1},{2,14},{6,10},... | collective-permute-start | bytes 393224 | tf_op jit(solution)/shard_map/ppermute | solution.py:275
  59.7 9.7 %collective-permute-start.10 = (bf16[512,128]{1,0:T(8,128)(2,1)S(1)}, bf16[512,128]{1,0:T(8,128)(2,1)S(1)}, u32[]{:S(2)}, u32[]{:S(2)}) collective-permute-start(bf16[512,128]{1,0:T(8,128)(2,1)S(1)} %get-tuple-element.39), channel_id=1, source_target_pairs={{0,4},{4,0},{8,12},{12,8},{1,5},{5,1},{9,13},{13,9},{2,6},{6,2},{1... | collective-permute-start | bytes 393224 | tf_op jit(solution)/shard_map/ppermute | solution.py:275
  66.9 2.7 %collective-permute-start.14 = (bf16[2,512,128]{2,1,0:T(8,128)(2,1)S(1)}, bf16[2,512,128]{2,1,0:T(8,128)(2,1)S(1)}, u32[]{:S(2)}, u32[]{:S(2)}) collective-permute-start(bf16[2,512,128]{2,1,0:T(8,128)(2,1)S(1)} %stack.21), channel_id=1, source_target_pairs={{0,1},{1,0},{2,3},{3,2},{4,5},{5,4},{6,7},{7,6},{8,9},{9,8},{10,11... | collective-permute-start | bytes 786440 | tf_op jit(solution)/shard_map/ppermute | solution.py:320
  69.6 1.6 %copy-start = (bf16[512,1536]{1,0:T(8,128)(2,1)S(1)}, bf16[512,1536]{1,0:T(8,128)(2,1)}, u32[]{:S(2)}) copy-start(bf16[512,1536]{1,0:T(8,128)(2,1)} %grid_ref.1) | copy-start | bytes 4718596
  69.6 1.6 %collective-permute-start.15 = (bf16[2,512,128]{2,1,0:T(8,128)(2,1)S(1)}, bf16[2,512,128]{2,1,0:T(8,128)(2,1)S(1)}, u32[]{:S(2)}, u32[]{:S(2)}) collective-permute-start(bf16[2,512,128]{2,1,0:T(8,128)(2,1)S(1)} %stack.20.ready_ref), channel_id=1, source_target_pairs={{0,1},{1,0},{2,3},{3,2},{4,5},{5,4},{6,7},{7,6},{8,9},{9,8},{10,11... | collective-permute-start | bytes 786440 | tf_op jit(solution)/shard_map/ppermute | solution.py:320
